TPU v7x, 32 devices: a whole 2x2x4 slice. The times are simulated.
32 devices in a mesh: dp: 32 (over z, y, x, core).
Axes of the slice: x: 2, y: 2, z: 4, core: 2. Of those that a mesh axis runs over, the one named last changes fastest.
Arguments:
- images: bfloat16 [2048, 8, 8, 256], P('dp'), may hold values from -50 to 50
- valid_slot: int32 [2048], P('dp'), may hold values from 0 to 1, as said below
- labels: int32 [2048], P('dp'), may hold values from 0 to 9
- conv_one: float32 [2304, 512], replicated, may hold values from -0.125 to 0.125
- conv_two: float32 [4608, 512], replicated, may hold values from -0.09375 to 0.09375
- shortcut: float32 [256, 512], replicated, may hold values from -0.375 to 0.375
- classifier: float32 [512, 10], replicated, may hold values from -0.75 to 0.75
- norm_params: float32 [6, 512], replicated, may hold values from -1.7 to 1.7, as said below
- row_state: float32 [32, 7680], P('dp'), as said below
- col_state: float32 [32, 1546], P('dp'), as said below
- bn_moment: float32 [32, 3072], P('dp'), as said below
Outputs:
- loss_sum: float32 [], replicated
- valid_count: float32 [], replicated
- new_weights: float32 [3678208], P('dp')
- weight_copies: bfloat16 [3678208], replicated
- vote_sum: float32 [3678208], P('dp')
- row_state_new: float32 [32, 7680], P('dp')
- col_state_new: float32 [32, 1546], P('dp')
- bn_moment_new: float32 [32, 3072], P('dp')
Inputs may be any that keep to these rules, and one draw needn't show every extreme that they name: `valid_slot`: valid slots become more frequent from the first worker to the last; the last slot is always valid. `norm_params`: gains positive. `row_state`: positive. `col_state`: positive. `bn_moment`: positive.
All inputs are finite; a program needn't handle non-finite values.
Results may differ from a plain program's by a relative error of at most 0.007.
Values may be sent and summed in bfloat16 or wider, within the bound.
A program may use at most 192 MiB of HBM per device.

v0:
```python
import math

import jax
import jax.numpy as jnp
from jax import lax
from jax.sharding import PartitionSpec as P

STEP = 10


EPS_NORM = 1e-05
EPS_ROW = 1e-30
EPS_SCALE = 0.001
FORWARD_DIMS = ("NHWC", "HWIO", "NHWC")
WEIGHT_DIMS = ("CHWN", "IHWO", "HWNC")


def conv_apply(maps, kernel, stride, margin):
    return lax.conv_general_dilated(
        maps,
        kernel,
        (stride, stride),
        ((margin, margin), (margin, margin)),
        dimension_numbers=FORWARD_DIMS,
        preferred_element_type=jnp.float32,
    )


def conv_weight_grad(maps, grad_out, stride, low_pad, high_pad):
    result = lax.conv_general_dilated(
        maps,
        grad_out,
        (1, 1),
        ((low_pad, high_pad), (low_pad, high_pad)),
        rhs_dilation=(stride, stride),
        dimension_numbers=WEIGHT_DIMS,
        preferred_element_type=jnp.float32,
    )
    return result.reshape(-1, result.shape[3])


def silu_slope(values):
    sigmoid_part = jax.nn.sigmoid(values)
    return sigmoid_part * (1.0 + values * (1.0 - sigmoid_part))


def settle(sum_plain, sum_square, pixels):
    mean_value = sum_plain / pixels
    return (mean_value, lax.rsqrt(sum_square / pixels - mean_value * mean_value + EPS_NORM))


def first_section(images, kernel_one, kernel_short):
    row_count = images.shape[0] * (images.shape[1] // 2) ** 2
    main_pre = conv_apply(images, kernel_one, 2, 1).reshape(row_count, -1)
    side_pre = conv_apply(images, kernel_short, 2, 0).reshape(row_count, -1)
    return (main_pre, side_pre)


def second_section(main_pre, norm_one, norm_params, kernel_two, slot_count, out_side):
    hidden_one = (main_pre - norm_one[0]) * norm_one[1] * norm_params[0] + norm_params[1]
    active = (
        jax.nn.silu(hidden_one).astype(jnp.bfloat16).reshape(slot_count, out_side, out_side, -1)
    )
    main_two = conv_apply(active, kernel_two, 1, 1).reshape(slot_count * out_side * out_side, -1)
    return (hidden_one, active, main_two)


def masked_moments(pixel_weight, values):
    return (jnp.sum(pixel_weight * values, axis=0), jnp.sum(pixel_weight * values * values, axis=0))


def soft_sign(step_raw):
    clip_by = jnp.maximum(1.0, jnp.sqrt(jnp.mean(step_raw * step_raw)))
    return jnp.tanh(step_raw / clip_by)


def make_votes(grads, rows_old, cols_old, moment_old):
    decay_rate = 1.0 - STEP ** (-0.8)
    votes, rows_new, cols_new = ([], [], [])
    row_at, col_at = (0, 0)
    for matrix in grads[:4]:
        row_size, col_size = matrix.shape
        square = matrix * matrix + EPS_ROW
        row_part = decay_rate * rows_old[row_at : row_at + row_size] + (
            1.0 - decay_rate
        ) * jnp.mean(square, axis=1)
        col_part = decay_rate * cols_old[col_at : col_at + col_size] + (
            1.0 - decay_rate
        ) * jnp.mean(square, axis=0)
        second = row_part[:, None] * col_part[None, :] / jnp.mean(row_part)
        votes.append(soft_sign(matrix * lax.rsqrt(second)).reshape(-1))
        rows_new.append(row_part)
        cols_new.append(col_part)
        row_at += row_size
        col_at += col_size
    flat_norm = grads[4].reshape(-1)
    moment_new = decay_rate * moment_old + (1.0 - decay_rate) * (flat_norm * flat_norm + EPS_ROW)
    votes.append(soft_sign(flat_norm * lax.rsqrt(moment_new)))
    return (
        jnp.concatenate(votes),
        jnp.concatenate(rows_new),
        jnp.concatenate(cols_new),
        moment_new,
    )


def norm_backward(grad_out, pre_value, norm_pair, gain_row):
    normed = (pre_value - norm_pair[0]) * norm_pair[1]
    grad_gain = jnp.sum(grad_out * normed, axis=0)
    grad_shift = jnp.sum(grad_out, axis=0)
    grad_pre = (grad_out * gain_row * norm_pair[1]).astype(jnp.bfloat16)
    return (grad_gain, grad_shift, grad_pre)


def local(
    images,
    valid_slot,
    labels,
    conv_one,
    conv_two,
    shortcut,
    classifier,
    norm_params,
    row_state,
    col_state,
    bn_moment,
):
    weights = (conv_one, conv_two, shortcut, classifier, norm_params)
    in_width = images.shape[3]
    width = conv_one.shape[1]
    kernel_one = conv_one.astype(jnp.bfloat16).reshape(3, 3, in_width, width)
    kernel_two = conv_two.astype(jnp.bfloat16).reshape(3, 3, width, width)
    kernel_short = shortcut.astype(jnp.bfloat16).reshape(1, 1, in_width, width)
    head_low = classifier.astype(jnp.bfloat16)
    slot_count = images.shape[0]
    out_side = images.shape[1] // 2
    pixel_count = out_side * out_side
    slot_weight = valid_slot.astype(jnp.float32)
    pixel_weight = jnp.broadcast_to(slot_weight[:, None], (slot_count, pixel_count)).reshape(-1, 1)
    main_pre, side_pre = first_section(images, kernel_one, kernel_short)
    main_sums = masked_moments(pixel_weight, main_pre)
    side_sums = masked_moments(pixel_weight, side_pre)
    first_sums = lax.psum(
        (jnp.sum(slot_weight), main_sums[0], main_sums[1], side_sums[0], side_sums[1]), "dp"
    )
    denominator = jnp.maximum(first_sums[0], 1.0)
    pixels = denominator * pixel_count
    norm_one = settle(first_sums[1], first_sums[2], pixels)
    norm_side = settle(first_sums[3], first_sums[4], pixels)
    hidden_one, active, main_two = second_section(
        main_pre, norm_one, norm_params, kernel_two, slot_count, out_side
    )
    two_sums = masked_moments(pixel_weight, main_two)
    second_sums = lax.psum((two_sums[0], two_sums[1]), "dp")
    norm_two = settle(second_sums[0], second_sums[1], pixels)
    images_again, kernel_one, kernel_two, kernel_short, norm_one, norm_two = (
        lax.optimization_barrier((images, kernel_one, kernel_two, kernel_short, norm_one, norm_two))
    )
    main_pre, side_pre = first_section(images_again, kernel_one, kernel_short)
    hidden_one, active, main_two = second_section(
        main_pre, norm_one, norm_params, kernel_two, slot_count, out_side
    )
    joined_pre = (
        (main_two - norm_two[0]) * norm_two[1] * norm_params[2]
        + norm_params[3]
        + (side_pre - norm_side[0]) * norm_side[1] * norm_params[4]
        + norm_params[5]
    )
    joined = jax.nn.silu(joined_pre).reshape(slot_count, pixel_count, -1)
    pooled = jnp.mean(joined, axis=1).astype(jnp.bfloat16)
    logits = jnp.dot(pooled, head_low, preferred_element_type=jnp.float32)
    largest = jnp.max(logits, axis=1, keepdims=True)
    exp_terms = jnp.exp(logits - largest)
    total_exp = jnp.sum(exp_terms, axis=1, keepdims=True)
    log_total = largest[:, 0] + jnp.log(total_exp[:, 0])
    onehot = (labels[:, None] == jnp.arange(logits.shape[1], dtype=jnp.int32)[None, :]).astype(
        jnp.float32
    )
    local_sum = jnp.sum(slot_weight * (log_total - jnp.sum(onehot * logits, axis=1)))
    loss_sum = lax.psum(local_sum, "dp")
    grad_logits = ((exp_terms / total_exp - onehot) * (slot_weight / denominator)[:, None]).astype(
        jnp.bfloat16
    )
    grad_head = lax.dot_general(
        pooled, grad_logits, (((0,), (0,)), ((), ())), preferred_element_type=jnp.float32
    )
    grad_pooled = lax.dot_general(
        grad_logits, head_low, (((1,), (1,)), ((), ())), preferred_element_type=jnp.float32
    )
    spread_pooled = jnp.broadcast_to(
        (grad_pooled / pixel_count)[:, None, :], (slot_count, pixel_count, width)
    )
    grad_joined = spread_pooled.reshape(slot_count * pixel_count, width) * silu_slope(joined_pre)
    gain_two, shift_two, grad_two = norm_backward(grad_joined, main_two, norm_two, norm_params[2])
    gain_side, shift_side, grad_side = norm_backward(
        grad_joined, side_pre, norm_side, norm_params[4]
    )
    grad_two_maps = grad_two.reshape(slot_count, out_side, out_side, width)
    grad_side_maps = grad_side.reshape(slot_count, out_side, out_side, width)
    grad_conv_two = conv_weight_grad(active, grad_two_maps, 1, 1, 1)
    grad_short = conv_weight_grad(images_again, grad_side_maps, 2, 0, -1)
    kernel_turned = jnp.transpose(kernel_two[::-1, ::-1], (0, 1, 3, 2))
    grad_active = conv_apply(grad_two_maps, kernel_turned, 1, 1).reshape(
        slot_count * pixel_count, width
    )
    grad_hidden = grad_active * silu_slope(hidden_one)
    gain_one, shift_one, grad_one = norm_backward(grad_hidden, main_pre, norm_one, norm_params[0])
    grad_conv_one = conv_weight_grad(
        images_again, grad_one.reshape(slot_count, out_side, out_side, width), 2, 1, 0
    )
    grad_norms = jnp.stack([gain_one, shift_one, gain_two, shift_two, gain_side, shift_side])
    grads = (grad_conv_one, grad_conv_two, grad_short, grad_head, grad_norms)
    votes, rows_new, cols_new, moment_new = make_votes(
        grads, row_state[0], col_state[0], bn_moment[0]
    )
    workers = lax.axis_size("dp")
    weights_flat = jnp.concatenate([weight.reshape(-1) for weight in weights])
    share = weights_flat.shape[0] // workers
    start = lax.axis_index("dp") * share
    group_ends, group_scales = ([], [])
    running = 0
    for weight in weights:
        running += weight.size
        group_ends.append(running)
        group_scales.append(jnp.maximum(EPS_SCALE, jnp.sqrt(jnp.mean(weight * weight))))
    vote_all = lax.psum(votes, "dp")
    positions = jnp.arange(weights_flat.shape[0], dtype=jnp.int32)
    result = jnp.zeros(positions.shape, jnp.float32) + group_scales[-1]
    for group_end, group_scale in zip(group_ends[-2::-1], group_scales[-2::-1]):
        result = jnp.where(positions < group_end, group_scale, result)
    new_all = weights_flat - result * jnp.tanh(vote_all / math.sqrt(workers))
    copies = new_all.astype(jnp.bfloat16)
    new_mine = lax.dynamic_slice_in_dim(new_all, start, share)
    vote_mine = lax.dynamic_slice_in_dim(vote_all, start, share)
    return (
        loss_sum,
        first_sums[0],
        new_mine,
        copies,
        vote_mine,
        rows_new[None, :],
        cols_new[None, :],
        moment_new[None, :],
    )


def solution(mesh):
    placed = (
        P("dp", None, None, None),
        P("dp"),
        P("dp"),
        P(),
        P(),
        P(),
        P(),
        P(),
        P("dp", None),
        P("dp", None),
        P("dp", None),
    )
    return jax.shard_map(
        local,
        mesh=mesh,
        in_specs=placed,
        out_specs=(P(), P(), P("dp"), P(), P("dp"), P("dp", None), P("dp", None), P("dp", None)),
        check_vma=False,
    )
```

profile of v0, /device:TPU:0, one launch (start us, length us, event | category | flops | bytes accessed | tf_op | source)
XLA Modules:
  0.0 519.4 jit_solution(17196061239245109086)
XLA Ops:
  9.1 5.6 %multiply_reduce_fusion.3 = (f32[]{:T(128)}, bf16[2304,512]{1,0:T(8,128)(2,1)S(1)}) fusion(f32[2304,512]{1,0:T(8,128)} %param.14), kind=kLoop, calls=%fused_computation.16 | loop fusion | flops 3538943 | bytes 7077892 | tf_op jit(solution)/shard_map/reduce_sum | solution.py:225
  14.8 11.7 %multiply_reduce_fusion.1 = (f32[]{:T(128)}, bf16[4608,512]{1,0:T(8,128)(2,1)}) fusion(f32[4608,512]{1,0:T(8,128)} %param.15), kind=kLoop, calls=%fused_computation.9 | loop fusion | flops 7077887 | bytes 14155780 | tf_op jit(solution)/shard_map/reduce_sum | solution.py:225
  27.2 1.8 fusion.7
  29.0 4.9 fusion.4
  34.0 42.2 %all-reduce.1 = (f32[512]{0:T(512)S(1)}, f32[]{:T(128)}, f32[512]{0:T(512)S(1)}) all-reduce(f32[512]{0:T(512)S(1)} %get-tuple-element.30, f32[]{:T(128)} %convert_reduce_fusion, f32[512]{0:T(512)S(1)} %get-tuple-element.31), channel_id=1, replica_groups=mesh['dp'=32] {'dp'}, use_global_device_ids=true, to_apply=%region_5.0 | all-reduce | flops 1025 | bytes 8200 | tf_op jit(solution)/shard_map/psum | solution.py:143
  76.8 8.5 %fusion.5 = (f32[512]{0:T(512)S(1)}, f32[512]{0:T(512)S(1)}, f32[512]{0:T(512)S(1)}, f32[512]{0:T(512)S(1)}) fusion(f32[64]{0:T(128)S(1)} %convert_element_type.47, f32[64,4,4,512]{3,0,2,1:T(8,128)} %fusion.7, bf16[3,3,512,512]{3,2,1,0:T(8,128)(2,1)} %bitcast.91, f32[64,4,4,512]{3,0,2,1:T(8,128)} %get-tuple-element.100, f32[512]{0:T(512)S(1)} %bitcast.141, ...), kind=kOutput, calls=%fused_computation.26 | convolution fusion | flops 3364354048 | bytes 8929536 | tf_op jit(solution)/shard_map/conv_general_dilated | solution.py:19
  85.4 40.6 %all-reduce = (f32[512]{0:T(512)S(1)}, f32[512]{0:T(512)S(1)}, f32[512]{0:T(512)S(1)}, f32[512]{0:T(512)S(1)}) all-reduce(f32[512]{0:T(512)S(1)} %get-tuple-element.45, f32[512]{0:T(512)S(1)} %get-tuple-element.46, f32[512]{0:T(512)S(1)} %get-tuple-element.29, f32[512]{0:T(512)S(1)} %get-tuple-element.28), channel_id=1, replica_groups=mesh['dp'=32] {'dp'}, use_global_device_ids=true, to_apply=%region_13.14 | all-reduce | flops 2048 | bytes 16384 | tf_op jit(solution)/shard_map/psum | solution.py:143
  126.0 4.2 fusion.17
  130.2 7.8 %fusion.55 = f32[64,4,4,512]{3,0,2,1:T(8,128)S(1)} fusion(bf16[3,3,512,512]{3,2,1,0:T(8,128)(2,1)} %bitcast.92, f32[64,4,4,512]{3,0,2,1:T(8,128)S(1)} %fusion.17, f32[512]{0:T(512)S(1)} %get-tuple-element.19, f32[512]{0:T(512)S(1)} %get-tuple-element.18, f32[512]{0:T(512)S(1)} %bitcast.142, f32[512]{0:T(512)S(1)} %bitcast.137), kind=kOutput, calls=%fused_computation.153 | convolution fusion | flops 3360161792 | bytes 8921088 | tf_op jit(solution)/shard_map/conv_general_dilated | solution.py:19
  138.1 1.7 multiply_reduce_fusion.10
  140.9 1.6 multiply_reduce_fusion.7
  142.5 8.8 %fusion = (f32[512]{0:T(512)S(1)}, f32[3,3,512]{2,1,0:T(4,128)S(1)}, f32[3,3,512,512]{3,2,1,0:T(8,128)}) fusion(f32[64,4,4,512]{3,0,2,1:T(8,128)S(1)} %get-tuple-element.58, f32[512]{0:T(512)S(1)} %bitcast.116, f32[512]{0:T(512)S(1)} %get-tuple-element.22, f32[64,4,4,512]{3,0,2,1:T(8,128)S(1)} %fusion.17, f32[512]{0:T(512)S(1)} %get-tuple-element.19, ...), kind=kOutput, calls=%fused_computation.10 | convolution fusion | flops 3371166720 | bytes 13664256 | tf_op jit(solution)/shard_map/conv_general_dilated | solution.py:30
  152.1 5.8 %fusion.56 = (f32[512]{0:T(512)S(1)}, f32[512]{0:T(512)S(1)}, f32[64,4,4,512]{3,0,2,1:T(8,128)S(1)}) fusion(f32[512]{0:T(512)S(1)} %get-tuple-element.19, f32[64,4,4,512]{3,0,2,1:T(8,128)S(1)} %fusion.17, f32[512]{0:T(512)S(1)} %get-tuple-element.18, f32[512]{0:T(512)S(1)} %bitcast.144, f32[512]{0:T(512)S(1)} %bitcast.139, ...), kind=kOutput, calls=%fused_computation.154 | convolution fusion | flops 3364879360 | bytes 11026432 | tf_op jit(solution)/shard_map/conv_general_dilated | solution.py:19
  158.3 4.8 fusion.2
  173.3 6.8 %multiply_reduce_fusion = f32[]{:T(128)} fusion(f32[3,3,512,512]{3,2,1,0:T(8,128)} %get-tuple-element.107, f32[]{:T(128)S(6)} %div.238, f32[512]{0:T(512)S(1)} %bitcast.108, f32[3,3,512]{2,1,0:T(4,128)S(1)} %get-tuple-element.73), kind=kLoop, calls=%fused_computation.6 | loop fusion | flops 11796479 | bytes 9457672 | tf_op jit(solution)/shard_map/reduce_sum | solution.py:73
  180.8 4.7 rsqrt_bitcast_fusion
  185.4 9.8 %copy.39 = f32[576,4,8,128]{3,1,2,0:T(4,128)} copy(f32[576,4,8,128]{3,2,1,0:T(8,128)} %rsqrt_bitcast_fusion) | data formatting | bytes 18874368
  195.9 4.3 multiply_reduce_fusion.2
  201.6 3.5 copy.37
  205.1 3.4 copy.36
  208.5 9.7 %copy.38 = f32[576,4,8,128]{3,1,2,0:T(4,128)} copy(f32[576,4,8,128]{3,2,1,0:T(8,128)} %bitcast.80) | data formatting | bytes 18874368
  218.4 5.8 %tanh_dynamic-update-slice_fusion.1 = f32[3678208]{0:T(1024)} fusion(f32[1179648]{0:T(1024)} %bitcast.90, f32[1179648]{0:T(1024)} %bitcast.89, f32[]{:T(128)S(6)} %max.39), kind=kLoop, calls=%fused_computation.12 | loop fusion | flops 2359295 | bytes 14155780
  224.2 2.3 copy-done
  226.5 8.7 %tanh_dynamic-update-slice_fusion = f32[3678208]{0:T(1024)} fusion(f32[3678208]{0:T(1024)} %tanh_dynamic-update-slice_fusion.1, f32[2359296]{0:T(1024)S(1)} %bitcast.83, f32[2359296]{0:T(1024)} %bitcast.82, f32[]{:T(128)S(6)} %max.40), kind=kLoop, calls=%fused_computation.5 | loop fusion | flops 4718592 | bytes 28311556
  237.3 3.6 copy.33
  240.9 2.3 constant_dynamic-update-slice_fusion.5
  243.2 10.4 %copy.34 = f32[576,4,8,128]{3,1,2,0:T(4,128)} copy(f32[576,4,8,128]{3,2,1,0:T(8,128)} %bitcast.79) | data formatting | bytes 18874368
  253.5 8.6 %constant_dynamic-update-slice_fusion.4 = f32[3678208]{0:T(1024)} fusion(f32[3678208]{0:T(1024)} %constant_dynamic-update-slice_fusion.5, f32[2359296]{0:T(1024)} %bitcast.81), kind=kLoop, calls=%fused_computation.112 | loop fusion | bytes 18874368
  262.1 41.6 %psum.70 = f32[]{:T(128)} all-reduce(f32[]{:T(128)} %get-tuple-element.99), channel_id=1, replica_groups=mesh['dp'=32] {'dp'}, use_global_device_ids=true, to_apply=%region_19.20 | all-reduce | flops 1 | bytes 8 | tf_op jit(solution)/shard_map/psum | solution.py:180
  312.2 182.9 %all-reduce.4.cloned.1.call-done = f32[3678208]{0:T(1024)} async-done(((f32[3678208]{0:T(1024)}), f32[3678208]{0:T(1024)}) %all-reduce.4.cloned.1.call-update) | async-done | bytes 14712848 | tf_op jit(solution)/shard_map/psum | solution.py:226
  495.1 14.3 %fusion.57 = (bf16[3678208]{0:T(1024)(128)(2,1)}, f32[3678208]{0:T(1024)S(1)}) fusion(f32[3678208]{0:T(1024)} %constant_dynamic-update-slice_fusion, f32[3678208]{0:T(1024)} %all-reduce.4.cloned.1.call-done, f32[]{:T(128)S(6)} %max.38, f32[]{:T(128)S(6)} %max.37, f32[]{:T(128)S(6)} %max.36, f32[]{:T(128)S(6)} %max.35, f32[]{:T(128)S(6)} %max.34), kind=kLoop, calls=%fused_computation.155 | loop fusion | flops 44138496 | bytes 51494932 | tf_op jit(solution)/shard_map/convert_element_type | solution.py:232
  510.4 2.0 dynamic_slice.7
  (97 shorter events, 19.9 us)
Async XLA Ops:
  7.2 488.0 %all-reduce.4.cloned.1.call-start = ((), (), s32[]{:S(2)}) async-start(), calls=%async_computation | async-start | bytes 29425664 | tf_op jit(solution)/shard_map/psum | solution.py:226
  9.1 5.6 %copy-start.5 = (f32[6,512]{1,0:T(8,128)S(1)}, f32[6,512]{1,0:T(8,128)}, u32[]{:S(2)}) copy-start(f32[6,512]{1,0:T(8,128)} %param.18) | copy-start | bytes 36868
  14.8 11.7 %copy-start.1 = (f32[256,512]{1,0:T(8,128)S(1)}, f32[256,512]{1,0:T(8,128)}, u32[]{:S(2)}) copy-start(f32[256,512]{1,0:T(8,128)} %param.16) | copy-start | bytes 1572868
  14.8 12.5 %copy-start.3 = (bf16[64,8,8,256]{3,2,1,0:T(8,128)(2,1)S(1)}, bf16[64,8,8,256]{3,2,1,0:T(8,128)(2,1)}, u32[]{:S(2)}) copy-start(bf16[64,8,8,256]{3,2,1,0:T(8,128)(2,1)} %param.11) | copy-start | bytes 6291460
  130.2 7.8 %copy-start.4 = (bf16[64,8,8,256]{3,2,1,0:T(8,128)(2,1)S(1)}, bf16[64,8,8,256]{3,2,1,0:T(8,128)(2,1)}, u32[]{:S(2)}) copy-start(bf16[64,8,8,256]{3,2,1,0:T(8,128)(2,1)} %param.11) | copy-start | bytes 6291460
  138.1 1.8 copy-start.2
  138.1 1.9 copy-start.9
  138.1 1.9 copy-start.10
  140.9 11.2 %slice-start.2 = ((s8[4718592]{0:T(1024)(128)(4,1)}), s8[4194304]{0:T(1024)(128)(4,1)S(1)}, s32[]{:S(2)}) async-start(s8[4718592]{0:T(1024)(128)(4,1)} %bitcast.93), calls=%async_computation.3 | async-start | bytes 8388608
  142.5 9.6 %slice-start.3 = ((s8[4718592]{0:T(1024)(128)(4,1)}), s8[524288]{0:T(1024)(128)(4,1)S(1)}, s32[]{:S(2)}) async-start(s8[4718592]{0:T(1024)(128)(4,1)} %bitcast.93), calls=%async_computation.4 | async-start | bytes 1048576
  152.1 6.1 %copy-start.6 = (f32[1,7680]{1,0:T(1,128)S(1)}, f32[1,7680]{1,0:T(1,128)}, u32[]{:S(2)}) copy-start(f32[1,7680]{1,0:T(1,128)} %param.19) | copy-start | bytes 92164
  158.3 6.2 %copy-start.7 = (f32[1,3072]{1,0:T(1,128)S(1)}, f32[1,3072]{1,0:T(1,128)}, u32[]{:S(2)}) copy-start(f32[1,3072]{1,0:T(1,128)} %param.21) | copy-start | bytes 36868
  158.3 9.5 %copy-start.8 = (f32[1,1546]{1,0:T(1,128)S(1)}, f32[1,1546]{1,0:T(1,128)}, u32[]{:S(2)}) copy-start(f32[1,1546]{1,0:T(1,128)} %param.20) | copy-start | bytes 18556
  200.9 4.2 slice-start
  201.6 3.5 slice-start.1
  218.4 8.1 %copy-start = (f32[576,4,8,128]{3,1,2,0:T(4,128)S(1)}, f32[576,4,8,128]{3,1,2,0:T(4,128)}, u32[]{:S(2)}) copy-start(f32[576,4,8,128]{3,1,2,0:T(4,128)} %copy.38) | copy-start | bytes 28311556
Sparse Core Ops, SparseCore 0:
  237.4 257.6 all-reduce.3
where the time goes:
time: 527 us; the launch traced here: 519 us
  waiting for transfers between devices  183 us (35%)
  blocking collectives  124 us (24%)
  other arithmetic  75.8 us (14%)
  local copies, waits for them, and re-layouts  61.6 us (12%)
  matrix products  49.9 us (9%)
  between operations  24.8 us (5%)
    psum x1, waiting for transfers between devices, local(): vote_all = lax.psum(votes, 'dp')  183 us
    psum x2, blocking collectives, local(): lax.psum((jnp.sum(slot_weight), main_sums[0], main_sums[1], side_sums[0],...  82.8 us
    unnamed x46, local copies, waits for them, and re-layouts  56.3 us
    psum x1, blocking collectives, local(): loss_sum = lax.psum(local_sum, 'dp')  41.6 us
    conv_general_dilated x7, matrix products, conv_apply(): lax.conv_general_dilated(maps, kernel, (stride, stride), ((margin, margin...  34.9 us
    unnamed x7, other arithmetic  20.7 us
    reduce_sum x5, other arithmetic, local(): jnp.mean(weight * weight)  19.2 us
    conv_general_dilated x3, matrix products, conv_weight_grad(): lax.conv_general_dilated(maps, grad_out, (1, 1), ((low_pad, high_pad), (l...  14.4 us
  transfers between devices with their start and end apart: 1, of which 1 were waited for; matrix products, arithmetic and copies ran while one was open for 6% of the time, Pallas kernels for 0%

commit v1 on v0

--- a/solution.py
+++ b/solution.py
@@ -1,18 +1,25 @@
+import functools
 import math
 
 import jax
 import jax.numpy as jnp
 from jax import lax
+from jax.experimental import pallas as pl
+from jax.experimental.pallas import tpu as pltpu
 from jax.sharding import PartitionSpec as P
 
 STEP = 10
-
+MESH = pl.DeviceIdType.MESH
 
 EPS_NORM = 1e-05
 EPS_ROW = 1e-30
 EPS_SCALE = 0.001
 FORWARD_DIMS = ("NHWC", "HWIO", "NHWC")
 WEIGHT_DIMS = ("CHWN", "IHWO", "HWNC")
+OWN = 224
+HALF = 112
+TAIL = 16
+PIECE = 32
 
 
 def conv_apply(maps, kernel, stride, margin):
@@ -88,7 +95,7 @@
             1.0 - decay_rate
         ) * jnp.mean(square, axis=0)
         second = row_part[:, None] * col_part[None, :] / jnp.mean(row_part)
-        votes.append(soft_sign(matrix * lax.rsqrt(second)).reshape(-1))
+        votes.append(soft_sign(matrix * lax.rsqrt(second)))
         rows_new.append(row_part)
         cols_new.append(col_part)
         row_at += row_size
@@ -96,12 +103,7 @@
     flat_norm = grads[4].reshape(-1)
     moment_new = decay_rate * moment_old + (1.0 - decay_rate) * (flat_norm * flat_norm + EPS_ROW)
     votes.append(soft_sign(flat_norm * lax.rsqrt(moment_new)))
-    return (
-        jnp.concatenate(votes),
-        jnp.concatenate(rows_new),
-        jnp.concatenate(cols_new),
-        moment_new,
-    )
+    return (votes, jnp.concatenate(rows_new), jnp.concatenate(cols_new), moment_new)
 
 
 def norm_backward(grad_out, pre_value, norm_pair, gain_row):
@@ -112,7 +114,430 @@
     return (grad_gain, grad_shift, grad_pre)
 
 
+def place():
+    me = lax.axis_index("dp")
+    core = lax.rem(me, 2)
+    x = lax.rem(lax.div(me, 2), 2)
+    y = lax.rem(lax.div(me, 4), 2)
+    z = lax.div(me, 8)
+    return me, core, x, y, z
+
+
+def greet(partners):
+    barrier = pltpu.get_barrier_semaphore()
+    for partner in partners:
+        pl.semaphore_signal(barrier, inc=1, device_id=(partner,), device_id_type=MESH)
+    pl.semaphore_wait(barrier, len(partners))
+
+
+def send(src, dst, send_sem, recv_sem, partner):
+    copy = pltpu.make_async_remote_copy(
+        src_ref=src,
+        dst_ref=dst,
+        send_sem=send_sem,
+        recv_sem=recv_sem,
+        device_id=(partner,),
+        device_id_type=MESH,
+    )
+    copy.start()
+    return copy
+
+
+def sum_kernel(x_ref, out_ref, plane, line, plane_send, plane_recv, line_send, line_recv):
+    me = lax.axis_index("dp")
+    z, spot = lax.div(me, 8), lax.rem(me, 8)
+    near = [z * 8 + lax.rem(spot + k, 8) for k in range(1, 8)]
+    far = [lax.rem(z + k, 4) * 8 + spot for k in range(1, 4)]
+    greet(near + far)
+    copies = [
+        send(x_ref, plane.at[spot], plane_send.at[k], plane_recv.at[k], partner)
+        for k, partner in enumerate(near)
+    ]
+    plane[spot] = x_ref[...]
+    for copy in copies:
+        copy.wait()
+    line[z] = functools.reduce(lambda a, b: a + b, [plane[k] for k in range(8)])
+    copies = [
+        send(line.at[z], line.at[z], line_send.at[k], line_recv.at[k], partner)
+        for k, partner in enumerate(far)
+    ]
+    for copy in copies:
+        copy.wait()
+    out_ref[...] = (line[0] + line[1]) + (line[2] + line[3])
+
+
+def sum_all(x, collective_id):
+    vmem = pl.BlockSpec(memory_space=pltpu.VMEM)
+    return pl.pallas_call(
+        sum_kernel,
+        out_shape=jax.ShapeDtypeStruct(x.shape, x.dtype),
+        in_specs=[vmem],
+        out_specs=vmem,
+        scratch_shapes=[
+            pltpu.VMEM((8,) + x.shape, x.dtype),
+            pltpu.VMEM((4,) + x.shape, x.dtype),
+            pltpu.SemaphoreType.DMA((7,)),
+            pltpu.SemaphoreType.DMA((7,)),
+            pltpu.SemaphoreType.DMA((3,)),
+            pltpu.SemaphoreType.DMA((3,)),
+        ],
+        compiler_params=pltpu.CompilerParams(collective_id=collective_id, has_side_effects=True),
+        name="sum_all",
+    )(x)
+
+
+def scale_of(row, scales, edges):
+    picked = scales[2]
+    picked = jnp.where(row < edges[1], scales[1], picked)
+    return jnp.where(row < edges[0], scales[0], picked)
+
+
+def update_kernel(
+    edges,
+    root,
+    scale_ref,
+    votes,
+    tail_sum,
+    tail_weight,
+    tail_scale,
+    one_ref,
+    two_ref,
+    short_ref,
+    new_ref,
+    vote_ref,
+    out_ref,
+    core_in,
+    ax_in,
+    by_in,
+    plane_in,
+    line_in,
+    halo_in,
+    total,
+    weight,
+    vote_flat,
+    new_flat,
+    mine,
+    tail_low,
+    rs_send,
+    rs_recv,
+    line_send,
+    line_recv,
+    halo_sem,
+    ag_send,
+    ag_recv,
+    local_sem,
+):
+    me, core, x, y, z = place()
+    flip_core = me + 1 - 2 * core
+    flip_x = me + 2 - 4 * x
+    flip_y = me + 4 - 8 * y
+    planes = [lax.rem(z + k, 4) for k in range(4)]
+    sources = [lax.rem(z + 4 - k, 4) for k in range(4)]
+    spot = lax.rem(me, 8)
+    line_peers = [plane * 8 + spot for plane in planes]
+    before, after = lax.rem(me + 31, 32), lax.rem(me + 1, 32)
+    scales = [scale_ref[k] for k in range(3)]
+
+    def fetch(row, count, place_at, sem):
+        parts = (
+            (one_ref, 0, edges[0]),
+            (two_ref, edges[0], edges[1]),
+            (short_ref, edges[1], edges[2]),
+        )
+        for ref, low, high in parts:
+
+            @pl.when(jnp.logical_and(row >= low, row < high))
+            def _():
+                start = pl.multiple_of(row - low, count)
+                pltpu.make_async_copy(
+                    ref.at[pl.ds(start, count)], weight.at[pl.ds(place_at, count)], sem
+                ).start()
+
+    first_row = me * OWN
+    for k in range(OWN // PIECE):
+        fetch(first_row + k * PIECE, PIECE, k * PIECE, local_sem.at[0])
+    fetch(first_row + OWN, TAIL, OWN, local_sem.at[1])
+
+    greet([flip_core, flip_x, flip_y] + line_peers[1:] + [before, after])
+
+    order = [0, 3, 1, 2]
+
+    core_copies = [
+        send(
+            votes.at[t, :, :, 1 - core],
+            core_in.at[t],
+            rs_send.at[0, t],
+            rs_recv.at[0, t],
+            flip_core,
+        )
+        for t in order
+    ]
+
+    def first_steps(k, t):
+        core_copies[k].wait()
+        core_in[t] = core_in[t] + votes[t, :, :, core]
+        return (
+            send(
+                core_in.at[t, :, 1 - x, pl.ds(0, HALF)],
+                ax_in.at[t],
+                rs_send.at[1, t],
+                rs_recv.at[1, t],
+                flip_x,
+            ),
+            send(
+                core_in.at[t, 1 - y, :, pl.ds(HALF, HALF)],
+                by_in.at[t],
+                rs_send.at[2, t],
+                rs_recv.at[2, t],
+                flip_y,
+            ),
+        )
+
+    def second_steps(t, copies):
+        copies[0].wait()
+        ax_in[t] = ax_in[t] + core_in[t, :, x, :HALF]
+        first = send(
+            ax_in.at[t, 1 - y],
+            plane_in.at[t, pl.ds(0, HALF)],
+            rs_send.at[3, t],
+            rs_recv.at[3, t],
+            flip_y,
+        )
+        copies[1].wait()
+        by_in[t] = by_in[t] + core_in[t, y, :, HALF:]
+        second = send(
+            by_in.at[t, 1 - x],
+            plane_in.at[t, pl.ds(HALF, HALF)],
+            rs_send.at[4, t],
+            rs_recv.at[4, t],
+            flip_x,
+        )
+        return first, second
+
+    def line_copy(t):
+        return pltpu.make_async_remote_copy(
+            src_ref=plane_in.at[t],
+            dst_ref=line_in.at[z],
+            send_sem=line_send.at[t],
+            recv_sem=line_recv.at[z],
+            device_id=(t * 8 + spot,),
+            device_id_type=MESH,
+        )
+
+    def third_steps(t, copies):
+        copies[0].wait()
+        plane_in[t, :HALF] = plane_in[t, :HALF] + ax_in[t, y]
+        copies[1].wait()
+        plane_in[t, HALF:] = plane_in[t, HALF:] + by_in[t, x]
+
+        @pl.when(z != t)
+        def _():
+            line_copy(t).start()
+
+        @pl.when(z == t)
+        def _():
+            line_in[t] = plane_in[t]
+
+    firsts, seconds = {}, {}
+    for k in range(6):
+        if k < 4:
+            firsts[k] = first_steps(k, order[k])
+        if 1 <= k < 5:
+            seconds[k - 1] = second_steps(order[k - 1], firsts[k - 1])
+        if k >= 2:
+            third_steps(order[k - 2], seconds[k - 2])
+
+    for t in range(4):
+
+        @pl.when(z != t)
+        def _():
+            line_copy(t).wait_send()
+            pltpu.make_async_remote_copy(
+                src_ref=plane_in.at[t],
+                dst_ref=line_in.at[t],
+                send_sem=line_send.at[t],
+                recv_sem=line_recv.at[t],
+                device_id=(t * 8 + spot,),
+                device_id_type=MESH,
+            ).wait_recv()
+
+    total[pl.ds(0, OWN), :] = functools.reduce(
+        lambda a, b: a + b, [line_in[t].astype(jnp.float32) for t in range(4)]
+    )
+    halo = send(total.at[pl.ds(0, TAIL)], halo_in, halo_sem.at[0], halo_sem.at[1], before)
+
+    pltpu.make_async_copy(
+        weight.at[pl.ds(0, OWN)], weight.at[pl.ds(0, OWN)], local_sem.at[0]
+    ).wait()
+
+    def flat_rows(row, values, ref):
+        for k in range(4):
+            ref[pl.ds(row * 4 + k, 8, stride=4), :] = values[:, 128 * k : 128 * (k + 1)]
+
+    def renew(row, scale_row):
+        summed = total[pl.ds(row, 8), :]
+        fresh = weight[pl.ds(row, 8), :] - scale_row * jnp.tanh(summed * root)
+        flat_rows(row, summed, vote_flat)
+        flat_rows(row, fresh, new_flat)
+
+    @pl.loop(0, OWN // 8)
+    def _(k):
+        row = pl.multiple_of(k * 8, 8)
+        renew(row, scale_of(first_row + row, scales, edges))
+
+    mine[...] = new_flat[pl.ds(0, 4 * OWN), :].astype(jnp.bfloat16)
+
+    span, part = 4 * OWN, 4 * HALF
+
+    def rows_of(plane, yy, xx, cc, half):
+        block = plane * 8 + yy * 4 + xx * 2 + cc
+        return pl.ds(pl.multiple_of(block * span + half * part, 16), part)
+
+    own_rows = pl.ds(pl.multiple_of(me * span, 16), span)
+    keep = pltpu.make_async_copy(mine, out_ref.at[own_rows], local_sem.at[2])
+    keep.start()
+    spread = [
+        send(mine, out_ref.at[own_rows], ag_send.at[0, k], ag_recv.at[0, k], line_peers[k])
+        for k in range(1, 4)
+    ]
+
+    halo.wait()
+
+    @pl.when(me < 31)
+    def _():
+        pltpu.make_async_copy(
+            weight.at[pl.ds(OWN, TAIL)], weight.at[pl.ds(OWN, TAIL)], local_sem.at[1]
+        ).wait()
+        total[pl.ds(OWN, TAIL), :] = halo_in[...]
+        for k in range(TAIL // 8):
+            renew(OWN + 8 * k, scale_of(first_row + OWN + 8 * k, scales, edges))
+
+    tail_new = tail_weight[...] - tail_scale[...] * jnp.tanh(tail_sum[...] * root)
+    weight[pl.ds(OWN, TAIL), :] = tail_new
+
+    @pl.when(me == 31)
+    def _():
+        for k in range(TAIL // 8):
+            flat_rows(OWN + 8 * k, tail_sum[8 * k : 8 * k + 8, :], vote_flat)
+            flat_rows(OWN + 8 * k, weight[OWN + 8 * k : OWN + 8 * k + 8, :], new_flat)
+
+    shift = 2 * me
+    count = vote_ref.shape[0]
+    vote_ref[...] = vote_flat[pl.ds(shift, count), :]
+    new_ref[...] = new_flat[pl.ds(shift, count), :]
+    for k in range(TAIL // 8):
+        flat_rows(OWN + 8 * k, weight[OWN + 8 * k : OWN + 8 * k + 8, :], new_flat)
+    tail_low[...] = new_flat[pl.ds(4 * OWN, 4 * TAIL), :].astype(jnp.bfloat16)
+    keep_tail = pltpu.make_async_copy(
+        tail_low, out_ref.at[pl.ds(32 * span, 4 * TAIL)], local_sem.at[3]
+    )
+    keep_tail.start()
+
+    keep.wait()
+
+    def piece(plane, yy, xx, cc, half, kind, k, partner):
+        rows = rows_of(plane, yy, xx, cc, half)
+        return send(
+            out_ref.at[rows], out_ref.at[rows], ag_send.at[kind, k], ag_recv.at[kind, k], partner
+        )
+
+    stage_one, stage_two, stage_three = [], [], []
+    for k, plane in enumerate(sources):
+        if k:
+            spread[k - 1].wait()
+        stage_one.append(
+            (
+                piece(plane, y, x, core, 0, 1, k, flip_y),
+                piece(plane, y, x, core, 1, 2, k, flip_x),
+            )
+        )
+    for k, plane in enumerate(sources):
+        stage_one[k][0].wait()
+        stage_one[k][1].wait()
+        stage_two.append(
+            [piece(plane, yy, x, core, 0, 3 + yy, k, flip_x) for yy in range(2)]
+            + [piece(plane, y, xx, core, 1, 5 + xx, k, flip_y) for xx in range(2)]
+        )
+    for k, plane in enumerate(sources):
+        for copy in stage_two[k]:
+            copy.wait()
+        for yy in range(2):
+            for xx in range(2):
+                rows = pl.ds(
+                    pl.multiple_of((plane * 8 + yy * 4 + xx * 2 + core) * span, 16), span
+                )
+                kind = 7 + 2 * yy + xx
+                stage_three.append(
+                    send(
+                        out_ref.at[rows],
+                        out_ref.at[rows],
+                        ag_send.at[kind, k],
+                        ag_recv.at[kind, k],
+                        flip_core,
+                    )
+                )
+    for copy in stage_three:
+        copy.wait()
+    keep_tail.wait()
+
+
+def update_weights(
+    votes, tail_sum, tail_weight, tail_scale, scales, conv_one, conv_two, shortcut, workers
+):
+    edges = [conv_one.shape[0]]
+    edges.append(edges[0] + conv_two.shape[0])
+    edges.append(edges[1] + shortcut.shape[0])
+    width = conv_one.shape[1]
+    flat_rows = (edges[2] + TAIL) * width // 128
+    share = flat_rows // workers
+    vmem = pl.BlockSpec(memory_space=pltpu.VMEM)
+    hbm = pl.BlockSpec(memory_space=pl.ANY)
+    low = jnp.bfloat16
+    dma = pltpu.SemaphoreType.DMA
+    return pl.pallas_call(
+        functools.partial(update_kernel, tuple(edges), 1.0 / math.sqrt(workers)),
+        out_shape=(
+            jax.ShapeDtypeStruct((share, 128), jnp.float32),
+            jax.ShapeDtypeStruct((share, 128), jnp.float32),
+            jax.ShapeDtypeStruct((flat_rows, 128), low),
+        ),
+        in_specs=[pl.BlockSpec(memory_space=pltpu.SMEM)] + [vmem] * 4 + [hbm] * 3,
+        out_specs=(vmem, vmem, hbm),
+        scratch_shapes=[
+            pltpu.VMEM((4, 2, 2, OWN, width), low),
+            pltpu.VMEM((4, 2, HALF, width), low),
+            pltpu.VMEM((4, 2, HALF, width), low),
+            pltpu.VMEM((4, OWN, width), low),
+            pltpu.VMEM((4, OWN, width), low),
+            pltpu.VMEM((TAIL, width), jnp.float32),
+            pltpu.VMEM((OWN + TAIL, width), jnp.float32),
+            pltpu.VMEM((OWN + TAIL, width), jnp.float32),
+            pltpu.VMEM((4 * (OWN + TAIL), 128), jnp.float32),
+            pltpu.VMEM((4 * (OWN + TAIL), 128), jnp.float32),
+            pltpu.VMEM((4 * OWN, 128), low),
+            pltpu.VMEM((4 * TAIL, 128), low),
+            dma((5, 4)),
+            dma((5, 4)),
+            dma((4,)),
+            dma((4,)),
+            dma((2,)),
+            dma((11, 4)),
+            dma((11, 4)),
+            dma((4,)),
+        ],
+        compiler_params=pltpu.CompilerParams(
+            collective_id=5, has_side_effects=True, vmem_limit_bytes=48 * 1024 * 1024
+        ),
+        name="update",
+    )(scales, votes, tail_sum, tail_weight, tail_scale, conv_one, conv_two, shortcut)
+
+
+def scale_for(weight):
+    return jnp.maximum(EPS_SCALE, jnp.sqrt(jnp.mean(weight * weight)))
+
+
 def local(
+    spread,
     images,
     valid_slot,
     labels,
@@ -125,7 +550,6 @@
     col_state,
     bn_moment,
 ):
-    weights = (conv_one, conv_two, shortcut, classifier, norm_params)
     in_width = images.shape[3]
     width = conv_one.shape[1]
     kernel_one = conv_one.astype(jnp.bfloat16).reshape(3, 3, in_width, width)
@@ -140,26 +564,28 @@
     main_pre, side_pre = first_section(images, kernel_one, kernel_short)
     main_sums = masked_moments(pixel_weight, main_pre)
     side_sums = masked_moments(pixel_weight, side_pre)
-    first_sums = lax.psum(
-        (jnp.sum(slot_weight), main_sums[0], main_sums[1], side_sums[0], side_sums[1]), "dp"
-    )
-    denominator = jnp.maximum(first_sums[0], 1.0)
+    count_row = jnp.broadcast_to(jnp.sum(slot_weight), (width,))
+    none_row = jnp.zeros((width,), jnp.float32)
+    if spread:
+        first_sums = sum_all(
+            jnp.stack([*main_sums, *side_sums, count_row, none_row, none_row, none_row]), 1
+        )
+    else:
+        first_sums = lax.psum(jnp.stack([*main_sums, *side_sums, count_row]), "dp")
+    valid_count = first_sums[4, 0]
+    denominator = jnp.maximum(valid_count, 1.0)
     pixels = denominator * pixel_count
-    norm_one = settle(first_sums[1], first_sums[2], pixels)
-    norm_side = settle(first_sums[3], first_sums[4], pixels)
+    norm_one = settle(first_sums[0], first_sums[1], pixels)
+    norm_side = settle(first_sums[2], first_sums[3], pixels)
     hidden_one, active, main_two = second_section(
         main_pre, norm_one, norm_params, kernel_two, slot_count, out_side
     )
     two_sums = masked_moments(pixel_weight, main_two)
-    second_sums = lax.psum((two_sums[0], two_sums[1]), "dp")
+    if spread:
+        second_sums = sum_all(jnp.stack([*two_sums] + [none_row] * 6), 2)
+    else:
+        second_sums = lax.psum(jnp.stack([*two_sums]), "dp")
     norm_two = settle(second_sums[0], second_sums[1], pixels)
-    images_again, kernel_one, kernel_two, kernel_short, norm_one, norm_two = (
-        lax.optimization_barrier((images, kernel_one, kernel_two, kernel_short, norm_one, norm_two))
-    )
-    main_pre, side_pre = first_section(images_again, kernel_one, kernel_short)
-    hidden_one, active, main_two = second_section(
-        main_pre, norm_one, norm_params, kernel_two, slot_count, out_side
-    )
     joined_pre = (
         (main_two - norm_two[0]) * norm_two[1] * norm_params[2]
         + norm_params[3]
@@ -177,7 +603,6 @@
         jnp.float32
     )
     local_sum = jnp.sum(slot_weight * (log_total - jnp.sum(onehot * logits, axis=1)))
-    loss_sum = lax.psum(local_sum, "dp")
     grad_logits = ((exp_terms / total_exp - onehot) * (slot_weight / denominator)[:, None]).astype(
         jnp.bfloat16
     )
@@ -198,7 +623,7 @@
     grad_two_maps = grad_two.reshape(slot_count, out_side, out_side, width)
     grad_side_maps = grad_side.reshape(slot_count, out_side, out_side, width)
     grad_conv_two = conv_weight_grad(active, grad_two_maps, 1, 1, 1)
-    grad_short = conv_weight_grad(images_again, grad_side_maps, 2, 0, -1)
+    grad_short = conv_weight_grad(images, grad_side_maps, 2, 0, -1)
     kernel_turned = jnp.transpose(kernel_two[::-1, ::-1], (0, 1, 3, 2))
     grad_active = conv_apply(grad_two_maps, kernel_turned, 1, 1).reshape(
         slot_count * pixel_count, width
@@ -206,7 +631,7 @@
     grad_hidden = grad_active * silu_slope(hidden_one)
     gain_one, shift_one, grad_one = norm_backward(grad_hidden, main_pre, norm_one, norm_params[0])
     grad_conv_one = conv_weight_grad(
-        images_again, grad_one.reshape(slot_count, out_side, out_side, width), 2, 1, 0
+        images, grad_one.reshape(slot_count, out_side, out_side, width), 2, 1, 0
     )
     grad_norms = jnp.stack([gain_one, shift_one, gain_two, shift_two, gain_side, shift_side])
     grads = (grad_conv_one, grad_conv_two, grad_short, grad_head, grad_norms)
@@ -214,27 +639,58 @@
         grads, row_state[0], col_state[0], bn_moment[0]
     )
     workers = lax.axis_size("dp")
-    weights_flat = jnp.concatenate([weight.reshape(-1) for weight in weights])
-    share = weights_flat.shape[0] // workers
-    start = lax.axis_index("dp") * share
-    group_ends, group_scales = ([], [])
-    running = 0
-    for weight in weights:
-        running += weight.size
-        group_ends.append(running)
-        group_scales.append(jnp.maximum(EPS_SCALE, jnp.sqrt(jnp.mean(weight * weight))))
-    vote_all = lax.psum(votes, "dp")
-    positions = jnp.arange(weights_flat.shape[0], dtype=jnp.int32)
-    result = jnp.zeros(positions.shape, jnp.float32) + group_scales[-1]
-    for group_end, group_scale in zip(group_ends[-2::-1], group_scales[-2::-1]):
-        result = jnp.where(positions < group_end, group_scale, result)
-    new_all = weights_flat - result * jnp.tanh(vote_all / math.sqrt(workers))
-    copies = new_all.astype(jnp.bfloat16)
-    new_mine = lax.dynamic_slice_in_dim(new_all, start, share)
-    vote_mine = lax.dynamic_slice_in_dim(vote_all, start, share)
+    weights = (conv_one, conv_two, shortcut, classifier, norm_params)
+    scales = [scale_for(weight) for weight in weights]
+    tail_vote = jnp.concatenate([votes[3].reshape(-1, width), votes[4].reshape(-1, width)])
+    tail_weight = jnp.concatenate([classifier.reshape(-1, width), norm_params])
+    if spread:
+        loss_rows = jnp.broadcast_to(local_sum, (8, width))
+        tail_sum = sum_all(jnp.concatenate([tail_vote, loss_rows]), 3)
+        loss_sum = tail_sum[TAIL, 0]
+        low_votes = jnp.concatenate([vote.astype(jnp.bfloat16) for vote in votes[:3]])
+        head_rows = classifier.size // width
+        tail_scale = jnp.concatenate(
+            [
+                jnp.broadcast_to(scales[3], (head_rows, width)),
+                jnp.broadcast_to(scales[4], (TAIL - head_rows, width)),
+            ]
+        )
+        new_mine, vote_mine, copies = update_weights(
+            low_votes.reshape(4, 2, 2, 2, OWN, width),
+            tail_sum[:TAIL],
+            tail_weight,
+            tail_scale,
+            jnp.stack(scales[:3]),
+            conv_one,
+            conv_two,
+            shortcut,
+            workers,
+        )
+        new_mine, vote_mine, copies = [
+            value.reshape(-1) for value in (new_mine, vote_mine, copies)
+        ]
+    else:
+        loss_sum = lax.psum(local_sum, "dp")
+        flat_vote = jnp.concatenate([vote.reshape(-1) for vote in votes])
+        flat_old = jnp.concatenate([weight.reshape(-1) for weight in weights])
+        flat_scale = jnp.concatenate(
+            [
+                jnp.broadcast_to(scale, (weight.size,))
+                for scale, weight in zip(scales, weights)
+            ]
+        )
+        vote_mine = lax.psum_scatter(flat_vote, "dp", tiled=True)
+        share = vote_mine.shape[0]
+        start = lax.axis_index("dp") * share
+        new_mine = lax.dynamic_slice_in_dim(
+            flat_old, start, share
+        ) - lax.dynamic_slice_in_dim(flat_scale, start, share) * jnp.tanh(
+            vote_mine / math.sqrt(workers)
+        )
+        copies = lax.all_gather(new_mine.astype(jnp.bfloat16), "dp", tiled=True)
     return (
         loss_sum,
-        first_sums[0],
+        valid_count,
         new_mine,
         copies,
         vote_mine,
@@ -259,7 +715,7 @@
         P("dp", None),
     )
     return jax.shard_map(
-        local,
+        functools.partial(local, mesh.shape["dp"] == 32),
         mesh=mesh,
         in_specs=placed,
         out_specs=(P(), P(), P("dp"), P(), P("dp"), P("dp", None), P("dp", None), P("dp", None)),

time: 527 us -> 260 us (0.49)
  waiting for transfers between devices: 183 us -> 0 us
  Pallas kernels: 0 us -> 135 us
  blocking collectives: 124 us -> 0 us
  local copies, waits for them, and re-layouts: 61.6 us -> 16 us
  matrix products: 49.9 us -> 31.8 us
  between operations: 24.8 us -> 11.3 us
  other arithmetic: 75.8 us -> 62.6 us
    psum x1 -> x0, waiting for transfers between devices: 183 us -> none  [local(): vote_all = lax.psum(votes, 'dp')]
    pallas_call x0 -> x4, Pallas kernels: none -> 135 us  [the longest x1 95.9 us: update_weights(): pl.pallas_call(functools.partial(update_kernel, tuple(edges), 1.0 / math....]
    psum x3 -> x0, blocking collectives: 124 us -> none  [the longest x2 82.8 us: local(): lax.psum((jnp.sum(slot_weight), main_sums[0], main_sums[1], side_sums[0],...]
    unnamed x46 -> x59, local copies, waits for them, and re-layouts: 56.3 us -> 8.83 us
    unnamed x7 -> x0, other arithmetic: 20.7 us -> none
    conv_general_dilated x7 -> x4, matrix products: 34.9 us -> 17.3 us  [conv_apply(): lax.conv_general_dilated(maps, kernel, (stride, stride), ((margin, margin...]
    concatenate x1 -> x3, other arithmetic: 0.61 us -> 6.58 us  [the longest x1 5.87 us: local(): jnp.concatenate([vote.astype(jnp.bfloat16) for vote in votes[:3]])]
    convert_element_type x1 -> x3, other arithmetic: 14.3 us -> 11.5 us  [local(): vote.astype(jnp.bfloat16)]
  transfers between devices with their start and end apart: 1 -> 0, of which waited for: 1 -> 0; matrix products, arithmetic and copies ran while one was open for 6% -> 0% of each run, Pallas kernels for 0% -> 0%
where the time goes in v1:
time: 260 us; the launch traced here: 256 us
  Pallas kernels  135 us (52%)
  other arithmetic  62.6 us (24%)
  matrix products  31.8 us (12%)
  local copies, waits for them, and re-layouts  16 us (6%)
  between operations  11.3 us (4%)
    pallas_call x1, Pallas kernels, update_weights(): pl.pallas_call(functools.partial(update_kernel, tuple(edges), 1.0 / math....  95.9 us
    pallas_call x3, Pallas kernels, sum_all(): pl.pallas_call(sum_kernel, out_shape=jax.ShapeDtypeStruct(x.shape, x.dtyp...  38.8 us
    conv_general_dilated x4, matrix products, conv_apply(): lax.conv_general_dilated(maps, kernel, (stride, stride), ((margin, margin...  17.3 us
    reduce_sum x5, other arithmetic, scale_for(): return jnp.maximum(EPS_SCALE, jnp.sqrt(jnp.mean(weight * weight)))  17.3 us
    reduce_sum x5, other arithmetic, soft_sign(): clip_by = jnp.maximum(1.0, jnp.sqrt(jnp.mean(step_raw * step_raw)))  14.2 us
    conv_general_dilated x3, matrix products, conv_weight_grad(): lax.conv_general_dilated(maps, grad_out, (1, 1), ((low_pad, high_pad), (l...  13.9 us
    convert_element_type x3, other arithmetic, local(): vote.astype(jnp.bfloat16)  11.5 us
    unnamed x59, local copies, waits for them, and re-layouts  8.83 us

profile of v1, /device:TPU:0, one launch (start us, length us, event | category | flops | bytes accessed | tf_op | source)
XLA Modules:
  0.0 256.5 jit_solution(18107833362646871339)
XLA Ops:
  0.6 5.7 %multiply_reduce_fusion.3 = (f32[]{:T(128)}, bf16[2304,512]{1,0:T(8,128)(2,1)S(1)}) fusion(f32[2304,512]{1,0:T(8,128)} %one_ref.1), kind=kLoop, calls=%fused_computation.16 | loop fusion | flops 3538943 | bytes 7077892 | tf_op jit(solution)/shard_map/reduce_sum | solution.py:536
  6.4 3.5 %fusion.19 = f32[64,4,4,512]{3,0,2,1:T(8,128)S(1)} fusion(bf16[3,3,256,512]{3,2,1,0:T(8,128)(2,1)S(1)} %bitcast.88, bf16[64,8,8,256]{3,2,1,0:T(8,128)(2,1)S(1)} %copy-done.8), kind=kOutput, calls=%fused_computation.51 | convolution fusion | flops 2030043136 | bytes 6553600 | tf_op jit(solution)/shard_map/conv_general_dilated | solution.py:26
  9.9 1.0 fusion.11
  13.2 13.5 %sum_all.3 = f32[8,512]{1,0:T(8,128)} custom-call(f32[8,512]{1,0:T(8,128)} %stack.64.x_ref), custom_call_target="tpu_custom_call" | custom-call | tf_op jit(solution)/shard_map/sum_all/pallas_call | solution.py:171
  26.7 1.2 slice.89
  28.6 0.9 add_rsqrt_fusion
  29.5 9.6 %multiply_reduce_fusion.1 = (f32[]{:T(128)}, bf16[4608,512]{1,0:T(8,128)(2,1)S(1)}) fusion(f32[4608,512]{1,0:T(8,128)} %two_ref.1), kind=kLoop, calls=%fused_computation.6 | loop fusion | flops 7077887 | bytes 14155780 | tf_op jit(solution)/shard_map/reduce_sum | solution.py:536
  39.1 6.4 %multiply_reduce_fusion.4 = (f32[512]{0:T(512)S(1)}, f32[512]{0:T(512)S(1)}, f32[64,4,4,512]{3,0,2,1:T(8,128)}) fusion(f32[64]{0:T(128)S(1)} %convert_element_type.50, bf16[3,3,512,512]{3,2,1,0:T(8,128)(2,1)S(1)} %bitcast.86, f32[64,4,4,512]{3,0,2,1:T(8,128)S(1)} %copy-done.5, f32[512]{0:T(512)S(1)} %bitcast.144, f32[512]{0:T(512)S(1)} %bitcast.147, ...), kind=kOutput, calls=%fused_computation.20 | convolution fusion | flops 3362257920 | bytes 8925440 | tf_op jit(solution)/shard_map/conv_general_dilated | solution.py:26
  46.2 11.1 %sum_all.4 = f32[8,512]{1,0:T(8,128)} custom-call(f32[8,512]{1,0:T(8,128)} %maximum_maximum_fusion.1.x_ref), custom_call_target="tpu_custom_call" | custom-call | tf_op jit(solution)/shard_map/sum_all/pallas_call | solution.py:171
  57.3 0.8 add_rsqrt_fusion.1
  58.2 2.8 %multiply_reduce_fusion.10 = f32[64,512]{1,0:T(8,128)S(1)} fusion(f32[512]{0:T(512)S(1)} %bitcast.109, f32[512]{0:T(512)S(1)} %bitcast.100, f32[512]{0:T(512)S(1)} %bitcast.97, f32[64,4,4,512]{3,0,2,1:T(8,128)S(1)} %get-tuple-element.79, f32[512]{0:T(512)S(1)} %bitcast.107, f32[512]{0:T(512)S(1)} %bitcast.111, f32[512]{0:T(512)S(1)} %bitcast.103, ...), kind=kLoop, calls=%fused_computation.36 | loop fusion | flops 7307264 | bytes 4341760 | tf_op jit(solution)/shard_map/reduce_sum | solution.py:596
  62.1 2.4 multiply_reduce_fusion.7
  64.5 6.4 %fusion.52 = (f32[512]{0:T(512)}, f32[512]{0:T(512)}, f32[64,4,4,512]{3,0,2,1:T(8,128)S(1)}) fusion(f32[512]{0:T(512)S(1)} %bitcast.138, f32[64,4,4,512]{3,0,2,1:T(8,128)S(1)} %copy-done.6, f32[512]{0:T(512)S(1)} %bitcast.142, f32[512]{0:T(512)S(1)} %bitcast.145, f32[512]{0:T(512)S(1)} %bitcast.148, bf16[3,3,512,512]{3,2,1,0:T(8,128)(2,1)S(1)} %bitcast.87, ...), kind=kOutput, calls=%fused_computation.138 | convolution fusion | flops 3364879360 | bytes 11026432 | tf_op jit(solution)/shard_map/conv_general_dilated | solution.py:26
  70.9 4.8 %fusion.8 = (f32[512]{0:T(512)S(1)}, f32[3,3,256]{2,1,0:T(4,128)S(1)}, f32[3,3,256,512]{3,2,1,0:T(8,128)}) fusion(f32[64,4,4,512]{3,0,2,1:T(8,128)S(1)} %get-tuple-element.83, f32[512]{0:T(512)S(1)} %bitcast.149, f32[512]{0:T(512)S(1)} %bitcast.139, bf16[64,8,8,256]{3,2,1,0:T(8,128)(2,1)S(1)} %copy-done.9), kind=kOutput, calls=%fused_computation.17 | convolution fusion | flops 2036331776 | bytes 8928256 | tf_op jit(solution)/shard_map/conv_general_dilated | solution.py:37
  75.8 8.4 %fusion.3 = (f32[512]{0:T(512)S(1)}, f32[3,3,512]{2,1,0:T(4,128)S(1)}, f32[3,3,512,512]{3,2,1,0:T(8,128)}) fusion(f32[64,4,4,512]{3,0,2,1:T(8,128)S(1)} %get-tuple-element.47, f32[512]{0:T(512)S(1)} %bitcast.106, f32[512]{0:T(512)S(1)} %bitcast.116, f32[64,4,4,512]{3,0,2,1:T(8,128)S(1)} %copy-done.6, f32[512]{0:T(512)S(1)} %bitcast.146, ...), kind=kOutput, calls=%fused_computation.7 | convolution fusion | flops 3371166720 | bytes 13664256 | tf_op jit(solution)/shard_map/conv_general_dilated | solution.py:37
  84.2 0.7 fusion.28
  90.6 4.2 %multiply_reduce_fusion.2 = f32[]{:T(128)} fusion(f32[3,3,256,512]{3,2,1,0:T(8,128)} %get-tuple-element.87, f32[]{:T(128)S(6)} %div.233, f32[512]{0:T(512)S(1)} %bitcast.95, f32[3,3,256]{2,1,0:T(4,128)S(1)} %get-tuple-element.68), kind=kLoop, calls=%fused_computation.14 | loop fusion | flops 5898239 | bytes 4729864 | tf_op jit(solution)/shard_map/reduce_sum | solution.py:80
  95.6 3.2 %fusion.7 = bf16[2304,512]{1,0:T(8,128)(2,1)S(1)} fusion(f32[3,3,256,512]{3,2,1,0:T(8,128)} %get-tuple-element.87, f32[]{:T(128)S(6)} %max.39, f32[]{:T(128)S(6)} %div.233, f32[512]{0:T(512)} %bitcast.96, f32[2304]{0:T(1024)S(1)} %get-tuple-element.38), kind=kLoop, calls=%fused_computation.13 | loop fusion | flops 5898240 | bytes 7089160 | tf_op jit(solution)/shard_map/convert_element_type | solution.py:650
  99.5 7.2 %multiply_reduce_fusion = f32[]{:T(128)} fusion(f32[3,3,512,512]{3,2,1,0:T(8,128)} %get-tuple-element.86, f32[]{:T(128)S(6)} %div.241, f32[512]{0:T(512)} %bitcast.93, f32[3,3,512]{2,1,0:T(4,128)S(1)} %get-tuple-element.58), kind=kLoop, calls=%fused_computation.4 | loop fusion | flops 11796479 | bytes 9457672 | tf_op jit(solution)/shard_map/reduce_sum | solution.py:80
  107.4 8.1 %fusion.2 = bf16[4608,512]{1,0:T(8,128)(2,1)} fusion(f32[3,3,512,512]{3,2,1,0:T(8,128)} %get-tuple-element.86, f32[]{:T(128)S(6)} %max.40, f32[]{:T(128)S(6)} %div.241, f32[512]{0:T(512)S(1)} %bitcast.94, f32[4608]{0:T(1024)S(1)} %get-tuple-element.40), kind=kLoop, calls=%fused_computation.3 | loop fusion | flops 11796480 | bytes 14176264 | tf_op jit(solution)/shard_map/convert_element_type | solution.py:650
  116.2 0.9 multiply_reduce_fusion.11
  118.0 5.9 %pad_maximum_fusion = bf16[7168,512]{1,0:T(8,128)(2,1)} fusion(bf16[256,512]{1,0:T(8,128)(2,1)S(1)} %tanh_convert_fusion, bf16[4608,512]{1,0:T(8,128)(2,1)} %fusion.2, bf16[2304,512]{1,0:T(8,128)(2,1)S(1)} %fusion.7), kind=kLoop, calls=%fused_computation.9 | loop fusion | flops 22020096 | bytes 14680064 | tf_op jit(solution)/shard_map/concatenate | solution.py:650
  127.0 1.2 multiply_reduce_fusion.17
  129.7 0.7 maximum_maximum_fusion.x_ref
  130.4 14.1 %sum_all.5 = f32[24,512]{1,0:T(8,128)} custom-call(f32[24,512]{1,0:T(8,128)} %maximum_maximum_fusion.x_ref), custom_call_target="tpu_custom_call" | custom-call | tf_op jit(solution)/shard_map/sum_all/pallas_call | solution.py:171
  144.5 0.8 slice.114.tail_sum
  146.7 0.7 multiply_reduce_fusion.12
  151.2 95.9 %update.1 = (f32[898,128]{1,0:T(8,128)S(1)}, f32[898,128]{1,0:T(8,128)S(1)}, bf16[28736,128]{1,0:T(8,128)(2,1)}) custom-call(f32[3]{0:T(128)S(1)} %pad_maximum_fusion.4.scale_ref, bf16[4,2,2,2,224,512]{5,4,3,2,1,0:T(8,128)(2,1)} %bitcast.84, f32[16,512]{1,0:T(8,128)S(1)} %slice.114.tail_sum, f32[16,512]{1,0:T(8,128)S(1)} %pad_maximum_fusion.1.tail_weight, ...), custom_call_target="tpu_custom_call" | custom-call | tf_op jit(solution)/shard_map/update/pallas_call | solution.py:497
  247.2 1.2 slice.107
  248.3 0.8 copy.51
  249.1 6.5 %copy.52 = bf16[3678208]{0:T(1024)(128)(2,1)} copy(bf16[3678208]{0:T(1024)(128)(2,1)} %bitcast.85) | data formatting | bytes 14712832
  255.7 0.8 copy.53
  (115 shorter events, 13.6 us)
Async XLA Ops:
  0.6 5.7 %copy-start.8 = (bf16[64,8,8,256]{3,2,1,0:T(8,128)(2,1)S(1)}, bf16[64,8,8,256]{3,2,1,0:T(8,128)(2,1)}, u32[]{:S(2)}) copy-start(bf16[64,8,8,256]{3,2,1,0:T(8,128)(2,1)} %param.11) | copy-start | bytes 6291460
  6.4 3.5 %copy-start.26 = (s32[64]{0:T(128)S(1)}, s32[64]{0:T(128)}, u32[]{:S(2)}) copy-start(s32[64]{0:T(128)} %param.12) | copy-start | bytes 772
  6.4 3.5 %copy-start = (f32[256,512]{1,0:T(8,128)S(1)}, f32[256,512]{1,0:T(8,128)}, u32[]{:S(2)}) copy-start(f32[256,512]{1,0:T(8,128)} %short_ref.1) | copy-start | bytes 1572868
  9.9 1.4 copy-start.4
  9.9 19.5 %copy-start.10 = (f32[6,512]{1,0:T(8,128)S(1)}, f32[6,512]{1,0:T(8,128)}, u32[]{:S(2)}) copy-start(f32[6,512]{1,0:T(8,128)} %param.18) | copy-start | bytes 36868
  29.5 9.6 %copy-start.5 = (f32[64,4,4,512]{3,0,2,1:T(8,128)S(1)}, f32[64,4,4,512]{3,0,2,1:T(8,128)}, u32[]{:S(2)}) copy-start(f32[64,4,4,512]{3,0,2,1:T(8,128)} %copy-done.4) | copy-start | bytes 6291460
  39.1 6.4 %copy-start.2 = (bf16[4608,512]{1,0:T(8,128)(2,1)}, bf16[4608,512]{1,0:T(8,128)(2,1)S(1)}, u32[]{:S(2)}) copy-start(bf16[4608,512]{1,0:T(8,128)(2,1)S(1)} %get-tuple-element.55) | copy-start | bytes 14155780
  58.2 2.8 %copy-start.7 = (f32[512,10]{0,1:T(8,128)S(1)}, f32[512,10]{0,1:T(8,128)}, u32[]{:S(2)}) copy-start(f32[512,10]{0,1:T(8,128)} %param.17) | copy-start | bytes 61444
  58.2 3.0 %copy-start.21 = (s32[64]{0:T(128)S(1)}, s32[64]{0:T(128)}, u32[]{:S(2)}) copy-start(s32[64]{0:T(128)} %param.13) | copy-start | bytes 772
  58.2 3.8 %copy-start.1 = (f32[64,4,4,512]{3,0,2,1:T(8,128)S(1)}, f32[64,4,4,512]{3,0,2,1:T(8,128)}, u32[]{:S(2)}) copy-start(f32[64,4,4,512]{3,0,2,1:T(8,128)} %get-tuple-element.80) | copy-start | bytes 6291460
  61.0 3.4 %copy-start.6 = (f32[64,4,4,512]{3,0,2,1:T(8,128)S(1)}, f32[64,4,4,512]{3,0,2,1:T(8,128)}, u32[]{:S(2)}) copy-start(f32[64,4,4,512]{3,0,2,1:T(8,128)} %copy-done.4) | copy-start | bytes 6291460
  62.0 2.5 copy-start.3
  64.5 6.4 %copy-start.9 = (bf16[64,8,8,256]{3,2,1,0:T(8,128)(2,1)S(1)}, bf16[64,8,8,256]{3,2,1,0:T(8,128)(2,1)}, u32[]{:S(2)}) copy-start(bf16[64,8,8,256]{3,2,1,0:T(8,128)(2,1)} %param.11) | copy-start | bytes 6291460
  84.2 0.8 copy-start.20
  84.2 2.3 copy-start.11
  85.5 9.3 %copy-start.13 = (f32[1,512]{1,0:T(1,128)}, f32[1,512]{1,0:T(1,128)S(1)}, u32[]{:S(2)}) copy-start(f32[1,512]{1,0:T(1,128)S(1)} %get-tuple-element.74) | copy-start | bytes 6148
  85.8 2.2 copy-start.24
  88.7 6.2 %copy-start.15 = (f32[256]{0:T(256)}, f32[256]{0:T(256)S(1)}, u32[]{:S(2)}) copy-start(f32[256]{0:T(256)S(1)} %get-tuple-element.42) | copy-start | bytes 3076
  99.4 7.9 %copy-start.12 = (f32[1,512]{1,0:T(1,128)S(1)}, f32[1,512]{1,0:T(1,128)}, u32[]{:S(2)}) copy-start(f32[1,512]{1,0:T(1,128)} %get-tuple-element.73) | copy-start | bytes 6148
  107.4 8.8 %copy-start.16 = (f32[256]{0:T(256)S(1)}, f32[256]{0:T(256)}, u32[]{:S(2)}) copy-start(f32[256]{0:T(256)} %copy-done.15) | copy-start | bytes 3076
  118.0 6.6 %copy-start.25 = (f32[10]{0:T(128)S(1)}, f32[10]{0:T(128)}, u32[]{:S(2)}) copy-start(f32[10]{0:T(128)} %copy-done.24) | copy-start | bytes 124
  118.0 9.0 %copy-start.14 = (f32[512]{0:T(512)S(1)}, f32[512]{0:T(512)}, u32[]{:S(2)}) copy-start(f32[512]{0:T(512)} %get-tuple-element.25) | copy-start | bytes 6148
  118.0 9.0 %copy-start.18 = (f32[512]{0:T(512)S(1)}, f32[512]{0:T(512)}, u32[]{:S(2)}) copy-start(f32[512]{0:T(512)} %get-tuple-element.24) | copy-start | bytes 6148
  118.0 9.0 %copy-start.19 = (f32[512]{0:T(512)S(1)}, f32[512]{0:T(512)}, u32[]{:S(2)}) copy-start(f32[512]{0:T(512)} %get-tuple-element.26) | copy-start | bytes 6148
  118.0 9.0 %copy-start.22 = (f32[512]{0:T(512)S(1)}, f32[512]{0:T(512)}, u32[]{:S(2)}) copy-start(f32[512]{0:T(512)} %get-tuple-element.27) | copy-start | bytes 6148
  118.0 9.0 %copy-start.23 = (f32[512]{0:T(512)S(1)}, f32[512]{0:T(512)}, u32[]{:S(2)}) copy-start(f32[512]{0:T(512)} %get-tuple-element.28) | copy-start | bytes 6148
  118.0 9.0 %copy-start.17 = (f32[1,3072]{1,0:T(1,128)S(1)}, f32[1,3072]{1,0:T(1,128)}, u32[]{:S(2)}) copy-start(f32[1,3072]{1,0:T(1,128)} %param.21) | copy-start | bytes 36868

commit v2 on v1

--- a/solution.py
+++ b/solution.py
@@ -532,12 +532,561 @@
     )(scales, votes, tail_sum, tail_weight, tail_scale, conv_one, conv_two, shortcut)
 
 
+def settle_rows(sums, pixels, gain, shift):
+    mean = sums[0] / pixels
+    inv = lax.rsqrt(sums[1] / pixels - mean * mean + EPS_NORM)
+    slope = gain * inv
+    return mean, inv, slope, shift - mean * slope
+
+
+def gate(values):
+    return 0.5 * jnp.tanh(0.5 * values) + 0.5
+
+
+def eye_mask(rows, columns, offset=0):
+    down = lax.broadcasted_iota(jnp.int32, (rows, columns), 0) + offset
+    return down == lax.broadcasted_iota(jnp.int32, (rows, columns), 1)
+
+
+def column_of(row, size):
+    spread = jnp.where(eye_mask(size, size), jnp.broadcast_to(row, (size, size)), 0)
+    return jnp.sum(spread, axis=1, keepdims=True)
+
+
+def total_of(values):
+    return jnp.sum(jnp.sum(values, axis=0, keepdims=True), axis=1, keepdims=True)
+
+
+def fold(values):
+    return jnp.sum(values.reshape(values.shape[0] // 8, 8, values.shape[1]), axis=0)
+
+
+def cast_weight(source, target, square_ref, taps, depth):
+    step = 128
+    square_ref[...] = jnp.zeros_like(square_ref)
+    for tap in range(taps):
+        new_tap = (tap % 3) * 3 + tap // 3
+
+        @pl.loop(0, depth // step)
+        def _(k):
+            start = pl.multiple_of(k * step, step)
+            values = source[pl.ds(tap * depth + start, step), :]
+            target[new_tap, pl.ds(start, step), :] = values.astype(jnp.bfloat16)
+            square_ref[...] += fold(values * values)
+
+
+def factored_votes(
+    grad, rows, row_block, rows_ref, rows_new, col_old, level, votes, vote_at
+):
+    width = grad.shape[1]
+    keep = 1.0 - STEP ** (-0.8)
+    step = 128
+    quarters = width // 128
+
+    def first(k, carry):
+        col_sum, row_sum = carry
+        start = pl.multiple_of(k * step, step)
+        old = rows_ref[pl.ds(row_block + k, 1), :] * keep
+        line = jnp.zeros((8, 128), jnp.float32)
+        for m in range(step // 8):
+            block = grad[pl.ds(start + 8 * m, 8), :]
+            square = block * block
+            col_sum = col_sum + square
+            part = square[:, :128]
+            for q in range(1, quarters):
+                part = part + square[:, 128 * q : 128 * (q + 1)]
+            part = part * ((1.0 - keep) / width)
+            diagonal = eye_mask(8, 128, 8 * m)
+            part = part + jnp.where(diagonal, jnp.broadcast_to(old, (8, 128)), 0.0)
+            row = jnp.sum(part, axis=1, keepdims=True) + (1.0 - keep) * EPS_ROW
+            row = jnp.broadcast_to(row, (8, 128))
+            level[pl.ds(start + 8 * m, 8), :] = row
+            row_sum = row_sum + row
+            line = line + jnp.where(diagonal, row, 0.0)
+        rows_new[pl.ds(row_block + k, 1), :] = jnp.sum(line, axis=0, keepdims=True)
+        return col_sum, row_sum
+
+    col_sum, row_sum = lax.fori_loop(
+        0,
+        rows // step,
+        first,
+        (jnp.zeros((8, width), jnp.float32), jnp.zeros((8, 128), jnp.float32)),
+    )
+    col_new = keep * col_old + (1.0 - keep) * (
+        jnp.sum(col_sum, axis=0, keepdims=True) / rows + EPS_ROW
+    )
+    scale = lax.rsqrt(col_new)
+    root_mean = jnp.sqrt(jnp.sum(row_sum, axis=0, keepdims=True) / rows)
+
+    def second(k, carry):
+        start = pl.multiple_of(k * step, step)
+        for m in range(step // 8):
+            here = pl.ds(start + 8 * m, 8)
+            factor = lax.rsqrt(level[here, :]) * root_mean
+            level[here, :] = factor
+            raw = grad[here, :] * scale
+            power = raw * raw
+            part = power[:, :128]
+            for q in range(1, quarters):
+                part = part + power[:, 128 * q : 128 * (q + 1)]
+            carry = carry + part * (factor * factor)
+        return carry
+
+    power = lax.fori_loop(0, rows // step, second, jnp.zeros((8, 128), jnp.float32))
+    clip = jnp.maximum(1.0, jnp.sqrt(total_of(power) / (rows * width)))
+    scale = scale / clip
+
+    def third(k, _):
+        start = pl.multiple_of(k * step, step)
+        for m in range(step // 16):
+            here = pl.ds(start + 16 * m, 16)
+            factor = level[here, :]
+            factor = jnp.concatenate([factor] * quarters, axis=1)
+            vote = jnp.tanh(grad[here, :] * factor * scale)
+            votes[pl.ds(vote_at + start + 16 * m, 16), :] = vote.astype(jnp.bfloat16)
+        return 0
+
+    lax.fori_loop(0, rows // step, third, 0)
+    return col_new
+
+
+def worker_kernel(
+    xs,
+    one_hbm,
+    two_hbm,
+    short_hbm,
+    head_ref,
+    norm_ref,
+    valid_ref,
+    label_ref,
+    row_ref,
+    col_ref,
+    moment_ref,
+    votes,
+    tail_ref,
+    scale_ref,
+    count_ref,
+    row_new,
+    col_new,
+    moment_new,
+    grad_one,
+    grad_two,
+    grad_short,
+    low_one,
+    low_two,
+    low_short,
+    main_pre,
+    side_pre,
+    main_two,
+    active,
+    back_two,
+    back_one,
+    back_side,
+    active_t,
+    xs_t,
+    head_pad,
+    level,
+    square,
+    post,
+    plane,
+    line,
+    fetch_sem,
+    plane_send,
+    plane_recv,
+    line_send,
+    line_recv,
+):
+    slots, in_width = xs.shape[4:]
+    width = main_pre.shape[1]
+    side = 4
+    band = side * slots
+    pixel_count = side * side
+    classes = head_ref.shape[1]
+    keep = 1.0 - STEP ** (-0.8)
+    low = jnp.bfloat16
+    f32 = jnp.float32
+
+    me = lax.axis_index("dp")
+    z, spot = lax.div(me, 8), lax.rem(me, 8)
+    near = [z * 8 + lax.rem(spot + k, 8) for k in range(1, 8)]
+    far = [lax.rem(z + k, 4) * 8 + spot for k in range(1, 4)]
+
+    fetches = [
+        pltpu.make_async_copy(source, target, fetch_sem.at[k])
+        for k, (source, target) in enumerate(
+            ((one_hbm, grad_one), (short_hbm, grad_short), (two_hbm, grad_two))
+        )
+    ]
+    for fetch in fetches:
+        fetch.start()
+    barrier = pltpu.get_barrier_semaphore()
+    for partner in near + far:
+        pl.semaphore_signal(barrier, inc=1, device_id=(partner,), device_id_type=MESH)
+
+    def scale_row(row, weight_square, size):
+        mean = total_of(weight_square) / size
+        value = jnp.maximum(EPS_SCALE, jnp.sqrt(mean))
+        scale_ref[row : row + 1, :] = jnp.broadcast_to(value, (1, width))
+
+    def exchange_start(which, values):
+        post[which] = values
+        plane[which, spot] = values
+        return [
+            send(
+                post.at[which],
+                plane.at[which, spot],
+                plane_send.at[which, k],
+                plane_recv.at[which, k],
+                partner,
+            )
+            for k, partner in enumerate(near)
+        ]
+
+    def exchange_middle(which, copies):
+        for copy in copies:
+            copy.wait()
+        line[which, z] = functools.reduce(lambda a, b: a + b, [plane[which, k] for k in range(8)])
+        return [
+            send(
+                line.at[which, z],
+                line.at[which, z],
+                line_send.at[which, k],
+                line_recv.at[which, k],
+                partner,
+            )
+            for k, partner in enumerate(far)
+        ]
+
+    def exchange_end(which, copies):
+        for copy in copies:
+            copy.wait()
+        return (line[which, 0] + line[which, 1]) + (line[which, 2] + line[which, 3])
+
+    valid_column = column_of(valid_ref[...].astype(f32), slots)
+    weight_slot = jnp.broadcast_to(valid_column, (slots, width))
+    weight_band = jnp.concatenate([weight_slot] * side, axis=0)
+
+    fetches[0].wait()
+    cast_weight(grad_one, low_one, square, 9, in_width)
+    scale_row(0, square[...], grad_one.size)
+    fetches[1].wait()
+    cast_weight(grad_short, low_short, square, 1, in_width)
+    scale_row(2, square[...], grad_short.size)
+
+    def image_taps(j):
+        pieces = []
+        for b in range(3):
+            column = j if b else j - 1
+            if column < 0:
+                continue
+            across = 0 if b == 1 else 1
+            for a in range(3):
+                if a == 1:
+                    piece = xs[across, column, 0].reshape(band, in_width)
+                elif a == 2:
+                    piece = xs[across, column, 1].reshape(band, in_width)
+                else:
+                    piece = xs[across, column, 1, : side - 1].reshape(band - slots, in_width)
+                    piece = jnp.concatenate([jnp.zeros((slots, in_width), low), piece], axis=0)
+                pieces.append(piece)
+        return jnp.concatenate(pieces, axis=1)
+
+    def moments(values):
+        weighted = values * weight_band
+        return (
+            jnp.sum(weighted, axis=0, keepdims=True),
+            jnp.sum(weighted * values, axis=0, keepdims=True),
+        )
+
+    def add_up(old, new):
+        return [a + b for a, b in zip(old, new)]
+
+    none = jnp.zeros((1, width), f32)
+    main_sums, side_sums = [none, none], [none, none]
+    for j in range(side):
+        here = pl.ds(j * band, band)
+        low_rows = low_one[3 if j == 0 else 0 :].reshape(-1, width)
+        value = jnp.dot(image_taps(j), low_rows, preferred_element_type=f32)
+        main_pre[here, :] = value
+        main_sums = add_up(main_sums, moments(value))
+        value = jnp.dot(
+            xs[0, j, 0].reshape(band, in_width), low_short[0], preferred_element_type=f32
+        )
+        side_pre[here, :] = value
+        side_sums = add_up(side_sums, moments(value))
+
+    count = jnp.broadcast_to(jnp.sum(valid_column, axis=0, keepdims=True), (1, width))
+    pl.semaphore_wait(barrier, len(near) + len(far))
+    copies = exchange_start(
+        0, jnp.concatenate(main_sums + side_sums + [count, none, none, none], axis=0)
+    )
+    fetches[2].wait()
+    cast_weight(grad_two, low_two, square, 9, width)
+    scale_row(1, square[...], grad_two.size)
+    copies = exchange_middle(0, copies)
+    for across in range(2):
+        for down in range(2):
+            for j in range(side):
+                block = xs[across, j, down].reshape(band, in_width)
+                xs_t[across, down, :, j * band : (j + 1) * band] = block.T
+    border = jnp.zeros((side, 1, slots, width), low)
+    active[:, 0:1] = border
+    active[:, side + 1 :] = border
+    back_two[:, 0:1] = border
+    back_two[:, side + 1 :] = border
+    back_one[:, side:] = border
+    head_pad[...] = jnp.zeros_like(head_pad)
+    head_pad[:, :classes] = head_ref[...]
+    head = head_pad[...]
+    scale_row(3, fold(head * head)[:, :128], head_ref.size)
+    params = norm_ref[...]
+    scale_row(4, params * params, norm_ref.size)
+    sums = exchange_end(0, copies)
+
+    valid_count = sums[4:5]
+    count_ref[...] = valid_count
+    denominator = jnp.maximum(valid_count, 1.0)
+    pixels = denominator * pixel_count
+    gains = [norm_ref[k : k + 1, :] for k in range(6)]
+    mean_one, inv_one, slope_one, base_one = settle_rows(
+        (sums[0:1], sums[1:2]), pixels, gains[0], gains[1]
+    )
+    mean_side, inv_side, slope_side, base_side = settle_rows(
+        (sums[2:3], sums[3:4]), pixels, gains[4], gains[5]
+    )
+
+    for j in range(side):
+        hidden = main_pre[pl.ds(j * band, band), :] * slope_one + base_one
+        active[j, 1 : side + 1] = (
+            (hidden * gate(hidden)).astype(low).reshape(side, slots, width)
+        )
+    two_sums = [none, none]
+    for j in range(side):
+        taps = [b for b in range(3) if 0 <= j + b - 1 < side]
+        pieces = [
+            active[j + b - 1, a : a + side].reshape(band, width) for b in taps for a in range(3)
+        ]
+        low_rows = low_two[3 * taps[0] : 3 * taps[-1] + 3].reshape(-1, width)
+        value = jnp.dot(jnp.concatenate(pieces, axis=1), low_rows, preferred_element_type=f32)
+        main_two[pl.ds(j * band, band), :] = value
+        two_sums = add_up(two_sums, moments(value))
+    copies = exchange_start(1, jnp.concatenate(two_sums + [none] * 6, axis=0))
+    for j in range(side):
+        block = active[j, 1 : side + 1].reshape(band, width)
+        active_t[:, j * band : (j + 1) * band] = block.T
+    copies = exchange_middle(1, copies)
+    sums = exchange_end(1, copies)
+    mean_two, inv_two, slope_two, base_two = settle_rows(
+        (sums[0:1], sums[1:2]), pixels, gains[2], gains[3]
+    )
+
+    base_joined = base_two + base_side
+
+    def joined_of(here):
+        return main_two[here, :] * slope_two + side_pre[here, :] * slope_side + base_joined
+
+    pooled = jnp.zeros((slots, width), f32)
+    for p in range(pixel_count):
+        joined = joined_of(pl.ds(p * slots, slots))
+        pooled = pooled + joined * gate(joined)
+    pooled = (pooled / pixel_count).astype(low)
+    head_low = head_pad[...].astype(low)
+    logits = jnp.dot(pooled, head_low, preferred_element_type=f32)
+    lane = lax.broadcasted_iota(jnp.int32, logits.shape, 1)
+    real = lane < classes
+    largest = jnp.max(jnp.where(real, logits, -jnp.inf), axis=1, keepdims=True)
+    powers = jnp.where(real, jnp.exp(jnp.where(real, logits - largest, 0.0)), 0.0)
+    total_power = jnp.sum(powers, axis=1, keepdims=True)
+    label_column = column_of(label_ref[...].astype(f32), slots).astype(jnp.int32)
+    onehot = jnp.where(lane == label_column, 1.0, 0.0)
+    entropy = largest + jnp.log(total_power) - jnp.sum(onehot * logits, axis=1, keepdims=True)
+    loss = jnp.sum(entropy * valid_column, axis=0, keepdims=True)
+    grad_logits = (
+        (powers / total_power - onehot) * (valid_column / denominator[:, :1])
+    ).astype(low)
+    grad_head = lax.dot_general(
+        grad_logits, pooled, (((0,), (0,)), ((), ())), preferred_element_type=f32
+    )[:16]
+    grad_pooled = lax.dot_general(
+        grad_logits, head_low, (((1,), (1,)), ((), ())), preferred_element_type=f32
+    )
+    grad_pooled = grad_pooled / pixel_count
+
+    gain_two, gain_side, shift_two = none, none, none
+    for p in range(pixel_count):
+        here = pl.ds(p * slots, slots)
+        joined = joined_of(here)
+        opened = gate(joined)
+        grad = grad_pooled * (opened * (1.0 + joined * (1.0 - opened)))
+        shift_two = shift_two + jnp.sum(grad, axis=0, keepdims=True)
+        gain_two = gain_two + jnp.sum(
+            grad * ((main_two[here, :] - mean_two) * inv_two), axis=0, keepdims=True
+        )
+        gain_side = gain_side + jnp.sum(
+            grad * ((side_pre[here, :] - mean_side) * inv_side), axis=0, keepdims=True
+        )
+        back_two[p // side, 1 + p % side] = (grad * slope_two).astype(low)
+        back_side[here, :] = (grad * slope_side).astype(low)
+
+    grad_short[...] = jnp.dot(xs_t[0, 0], back_side[...], preferred_element_type=f32)
+    for b in range(3):
+        first, last = max(0, b - 1), min(side, side + b - 1)
+        left = active_t[:, first * band : last * band]
+        for a in range(3):
+            right = back_two[first - b + 1 : last - b + 1, 2 - a : 2 - a + side]
+            grad_two[pl.ds((a * 3 + b) * width, width), :] = jnp.dot(
+                left, right.reshape(-1, width), preferred_element_type=f32
+            )
+
+    gain_one, shift_one = none, none
+    for j in range(side):
+        taps = [b for b in range(3) if 0 <= j - b + 1 < side]
+        pieces = [
+            back_two[j - b + 1, 2 - a : 2 - a + side].reshape(band, width)
+            for b in taps
+            for a in range(3)
+        ]
+        weights = jnp.concatenate([low_two[b * 3 + a] for b in taps for a in range(3)], axis=1)
+        grad = lax.dot_general(
+            jnp.concatenate(pieces, axis=1),
+            weights,
+            (((1,), (1,)), ((), ())),
+            preferred_element_type=f32,
+        )
+        before = main_pre[pl.ds(j * band, band), :]
+        hidden = before * slope_one + base_one
+        opened = gate(hidden)
+        grad = grad * (opened * (1.0 + hidden * (1.0 - opened)))
+        shift_one = shift_one + jnp.sum(grad, axis=0, keepdims=True)
+        gain_one = gain_one + jnp.sum(
+            grad * ((before - mean_one) * inv_one), axis=0, keepdims=True
+        )
+        back_one[j, :side] = (grad * slope_one).astype(low).reshape(side, slots, width)
+
+    for b in range(3):
+        first, last = (0, side - 1) if b == 0 else (0, side)
+        shift = 1 if b == 0 else 0
+        for a in range(3):
+            left = xs_t[0 if b == 1 else 1, 0 if a == 1 else 1, :, first * band : last * band]
+            start = 1 if a == 0 else 0
+            right = back_one[first + shift : last + shift, start : start + side]
+            grad_one[pl.ds((a * 3 + b) * in_width, in_width), :] = jnp.dot(
+                left, right.reshape(-1, width), preferred_element_type=f32
+            )
+
+    row_at, vote_at = 0, 0
+    for k, grad in enumerate((grad_one, grad_two, grad_short)):
+        here = pl.ds(k * width, width)
+        col_new[:, here] = factored_votes(
+            grad,
+            grad.shape[0],
+            row_at,
+            row_ref,
+            row_new,
+            col_ref[:, here],
+            level,
+            votes,
+            vote_at,
+        )
+        row_at += grad.shape[0] // 128
+        vote_at += grad.shape[0]
+
+    square_head = grad_head * grad_head + EPS_ROW
+    real = lax.broadcasted_iota(jnp.int32, square_head.shape, 0) < classes
+    square_head = jnp.where(real, square_head, 0.0)
+    old = jnp.concatenate([row_ref[row_at + k : row_at + k + 1, :] for k in range(4)], axis=1)
+    row = keep * old + (1.0 - keep) * jnp.sum(square_head, axis=0, keepdims=True) / classes
+    for k in range(4):
+        row_new[row_at + k : row_at + k + 1, :] = row[:, 128 * k : 128 * (k + 1)]
+    diagonal = eye_mask(16, classes)
+    old = jnp.broadcast_to(col_ref[:, 3 * width :], (16, classes))
+    old = jnp.sum(jnp.where(diagonal, old, 0.0), axis=1, keepdims=True)
+    column = keep * old + (1.0 - keep) * jnp.sum(square_head, axis=1, keepdims=True) / width
+    col_new[:, 3 * width :] = jnp.sum(
+        jnp.where(diagonal, jnp.broadcast_to(column, (16, classes)), 0.0), axis=0, keepdims=True
+    )
+    real_column = lax.broadcasted_iota(jnp.int32, column.shape, 0) < classes
+    column = jnp.where(real_column, column, 1.0)
+    mean = jnp.sum(row, axis=1, keepdims=True) / width
+    raw = grad_head * (lax.rsqrt(row) * jnp.sqrt(mean)) * lax.rsqrt(column)
+    clip = jnp.maximum(1.0, jnp.sqrt(total_of(raw * raw) / (classes * width)))
+    tail_ref[:16, :] = jnp.tanh(raw / clip)
+
+    raws = []
+    for k, grad in enumerate((gain_one, shift_one, gain_two, shift_two, gain_side, shift_two)):
+        here = pl.ds(k * width, width)
+        moment = keep * moment_ref[:, here] + (1.0 - keep) * (grad * grad + EPS_ROW)
+        moment_new[:, here] = moment
+        raws.append(grad * lax.rsqrt(moment))
+    raw = jnp.concatenate(raws, axis=0)
+    clip = jnp.maximum(1.0, jnp.sqrt(total_of(raw * raw) / raw.size))
+    tail_ref[classes : classes + 6, :] = jnp.tanh(raw / clip)
+    tail_ref[16:, :] = jnp.broadcast_to(loss, (8, width))
+
+
+def run_worker(xs, conv_one, conv_two, shortcut, classifier, norm_params, valid, labels, rows, cols, moment):
+    vmem = pl.BlockSpec(memory_space=pltpu.VMEM)
+    hbm = pl.BlockSpec(memory_space=pl.ANY)
+    low, f32 = jnp.bfloat16, jnp.float32
+    dma = pltpu.SemaphoreType.DMA
+    slots, in_width = xs.shape[4:]
+    width = conv_one.shape[1]
+    pixels = 16 * slots
+    shape = jax.ShapeDtypeStruct
+    matrix_rows = conv_one.shape[0] + conv_two.shape[0] + shortcut.shape[0]
+    return pl.pallas_call(
+        worker_kernel,
+        out_shape=(
+            shape((matrix_rows, width), low),
+            shape((TAIL + 8, width), f32),
+            shape((8, width), f32),
+            shape((1, width), f32),
+            shape(rows.shape, f32),
+            shape(cols.shape, f32),
+            shape(moment.shape, f32),
+        ),
+        in_specs=[vmem] + [hbm] * 3 + [vmem] * 7,
+        out_specs=(vmem,) * 7,
+        scratch_shapes=[
+            pltpu.VMEM(conv_one.shape, f32),
+            pltpu.VMEM(conv_two.shape, f32),
+            pltpu.VMEM(shortcut.shape, f32),
+            pltpu.VMEM((9, in_width, width), low),
+            pltpu.VMEM((9, width, width), low),
+            pltpu.VMEM((1, in_width, width), low),
+            pltpu.VMEM((pixels, width), f32),
+            pltpu.VMEM((pixels, width), f32),
+            pltpu.VMEM((pixels, width), f32),
+            pltpu.VMEM((4, 6, slots, width), low),
+            pltpu.VMEM((4, 6, slots, width), low),
+            pltpu.VMEM((4, 5, slots, width), low),
+            pltpu.VMEM((pixels, width), low),
+            pltpu.VMEM((width, pixels), low),
+            pltpu.VMEM((2, 2, in_width, pixels), low),
+            pltpu.VMEM((width, 128), f32),
+            pltpu.VMEM((conv_two.shape[0], 128), f32),
+            pltpu.VMEM((8, width), f32),
+            pltpu.VMEM((2, 8, width), f32),
+            pltpu.VMEM((2, 8, 8, width), f32),
+            pltpu.VMEM((2, 4, 8, width), f32),
+            dma((3,)),
+            dma((2, 7)),
+            dma((2, 7)),
+            dma((2, 3)),
+            dma((2, 3)),
+        ],
+        compiler_params=pltpu.CompilerParams(
+            collective_id=1, has_side_effects=True, vmem_limit_bytes=60 * 1024 * 1024
+        ),
+        name="worker",
+    )(xs, conv_one, conv_two, shortcut, classifier, norm_params, valid, labels, rows, cols, moment)
+
+
 def scale_for(weight):
     return jnp.maximum(EPS_SCALE, jnp.sqrt(jnp.mean(weight * weight)))
 
 
-def local(
-    spread,
+def local_general(
     images,
     valid_slot,
     labels,
@@ -565,13 +1114,7 @@
     main_sums = masked_moments(pixel_weight, main_pre)
     side_sums = masked_moments(pixel_weight, side_pre)
     count_row = jnp.broadcast_to(jnp.sum(slot_weight), (width,))
-    none_row = jnp.zeros((width,), jnp.float32)
-    if spread:
-        first_sums = sum_all(
-            jnp.stack([*main_sums, *side_sums, count_row, none_row, none_row, none_row]), 1
-        )
-    else:
-        first_sums = lax.psum(jnp.stack([*main_sums, *side_sums, count_row]), "dp")
+    first_sums = lax.psum(jnp.stack([*main_sums, *side_sums, count_row]), "dp")
     valid_count = first_sums[4, 0]
     denominator = jnp.maximum(valid_count, 1.0)
     pixels = denominator * pixel_count
@@ -581,10 +1124,7 @@
         main_pre, norm_one, norm_params, kernel_two, slot_count, out_side
     )
     two_sums = masked_moments(pixel_weight, main_two)
-    if spread:
-        second_sums = sum_all(jnp.stack([*two_sums] + [none_row] * 6), 2)
-    else:
-        second_sums = lax.psum(jnp.stack([*two_sums]), "dp")
+    second_sums = lax.psum(jnp.stack([*two_sums]), "dp")
     norm_two = settle(second_sums[0], second_sums[1], pixels)
     joined_pre = (
         (main_two - norm_two[0]) * norm_two[1] * norm_params[2]
@@ -641,53 +1181,24 @@
     workers = lax.axis_size("dp")
     weights = (conv_one, conv_two, shortcut, classifier, norm_params)
     scales = [scale_for(weight) for weight in weights]
-    tail_vote = jnp.concatenate([votes[3].reshape(-1, width), votes[4].reshape(-1, width)])
-    tail_weight = jnp.concatenate([classifier.reshape(-1, width), norm_params])
-    if spread:
-        loss_rows = jnp.broadcast_to(local_sum, (8, width))
-        tail_sum = sum_all(jnp.concatenate([tail_vote, loss_rows]), 3)
-        loss_sum = tail_sum[TAIL, 0]
-        low_votes = jnp.concatenate([vote.astype(jnp.bfloat16) for vote in votes[:3]])
-        head_rows = classifier.size // width
-        tail_scale = jnp.concatenate(
-            [
-                jnp.broadcast_to(scales[3], (head_rows, width)),
-                jnp.broadcast_to(scales[4], (TAIL - head_rows, width)),
-            ]
-        )
-        new_mine, vote_mine, copies = update_weights(
-            low_votes.reshape(4, 2, 2, 2, OWN, width),
-            tail_sum[:TAIL],
-            tail_weight,
-            tail_scale,
-            jnp.stack(scales[:3]),
-            conv_one,
-            conv_two,
-            shortcut,
-            workers,
-        )
-        new_mine, vote_mine, copies = [
-            value.reshape(-1) for value in (new_mine, vote_mine, copies)
+    loss_sum = lax.psum(local_sum, "dp")
+    flat_vote = jnp.concatenate([vote.reshape(-1) for vote in votes])
+    flat_old = jnp.concatenate([weight.reshape(-1) for weight in weights])
+    flat_scale = jnp.concatenate(
+        [
+            jnp.broadcast_to(scale, (weight.size,))
+            for scale, weight in zip(scales, weights)
         ]
-    else:
-        loss_sum = lax.psum(local_sum, "dp")
-        flat_vote = jnp.concatenate([vote.reshape(-1) for vote in votes])
-        flat_old = jnp.concatenate([weight.reshape(-1) for weight in weights])
-        flat_scale = jnp.concatenate(
-            [
-                jnp.broadcast_to(scale, (weight.size,))
-                for scale, weight in zip(scales, weights)
-            ]
-        )
-        vote_mine = lax.psum_scatter(flat_vote, "dp", tiled=True)
-        share = vote_mine.shape[0]
-        start = lax.axis_index("dp") * share
-        new_mine = lax.dynamic_slice_in_dim(
-            flat_old, start, share
-        ) - lax.dynamic_slice_in_dim(flat_scale, start, share) * jnp.tanh(
-            vote_mine / math.sqrt(workers)
-        )
-        copies = lax.all_gather(new_mine.astype(jnp.bfloat16), "dp", tiled=True)
+    )
+    vote_mine = lax.psum_scatter(flat_vote, "dp", tiled=True)
+    share = vote_mine.shape[0]
+    start = lax.axis_index("dp") * share
+    new_mine = lax.dynamic_slice_in_dim(
+        flat_old, start, share
+    ) - lax.dynamic_slice_in_dim(flat_scale, start, share) * jnp.tanh(
+        vote_mine / math.sqrt(workers)
+    )
+    copies = lax.all_gather(new_mine.astype(jnp.bfloat16), "dp", tiled=True)
     return (
         loss_sum,
         valid_count,
@@ -697,6 +1208,70 @@
         rows_new[None, :],
         cols_new[None, :],
         moment_new[None, :],
+    )
+
+
+def local(
+    images,
+    valid_slot,
+    labels,
+    conv_one,
+    conv_two,
+    shortcut,
+    classifier,
+    norm_params,
+    row_state,
+    col_state,
+    bn_moment,
+):
+    slots, height, _, in_width = images.shape
+    width = conv_one.shape[1]
+    side = height // 2
+    xs = images.reshape(slots, side, 2, side, 2, in_width).transpose(4, 3, 2, 1, 0, 5)
+    votes, tail_vote, scales, valid_count, rows_new, cols_new, moment_new = run_worker(
+        xs,
+        conv_one,
+        conv_two,
+        shortcut,
+        classifier,
+        norm_params,
+        valid_slot.reshape(1, -1),
+        labels.reshape(1, -1),
+        row_state.reshape(-1, 128),
+        col_state,
+        bn_moment,
+    )
+    tail_sum = sum_all(tail_vote, 3)
+    classes = classifier.shape[1]
+    head_sum = tail_sum[:classes].T.reshape(classes, width)
+    flat_sum = jnp.concatenate([head_sum, tail_sum[classes:TAIL]])
+    tail_weight = jnp.concatenate([classifier.reshape(classes, width), norm_params])
+    tail_scale = jnp.concatenate(
+        [
+            jnp.broadcast_to(scales[3], (classes, width)),
+            jnp.broadcast_to(scales[4], (TAIL - classes, width)),
+        ]
+    )
+    new_mine, vote_mine, copies = update_weights(
+        votes.reshape(4, 2, 2, 2, OWN, width),
+        flat_sum,
+        tail_weight,
+        tail_scale,
+        scales[:3, 0],
+        conv_one,
+        conv_two,
+        shortcut,
+        lax.axis_size("dp"),
+    )
+    return (
+        tail_sum[TAIL, 0],
+        valid_count[0, 0],
+        new_mine.reshape(-1),
+        copies.reshape(-1),
+        vote_mine.reshape(-1),
+        rows_new.reshape(1, -1),
+        cols_new,
+        moment_new,
     )
 
 
@@ -715,7 +1290,7 @@
         P("dp", None),
     )
     return jax.shard_map(
-        functools.partial(local, mesh.shape["dp"] == 32),
+        local if mesh.shape["dp"] == 32 else local_general,
         mesh=mesh,
         in_specs=placed,
         out_specs=(P(), P(), P("dp"), P(), P("dp"), P("dp", None), P("dp", None), P("dp", None)),

time: 260 us -> 196 us (0.75)
  other arithmetic: 62.6 us -> 1.47 us
  Pallas kernels: 135 us -> 169 us
  matrix products: 31.8 us -> 0 us
  between operations: 11.3 us -> 0.73 us
  local copies, waits for them, and re-layouts: 16 us -> 21.8 us
    pallas_call x0 -> x1, Pallas kernels: none -> 58.8 us  [run_worker(): pl.pallas_call(worker_kernel, out_shape=(shape((matrix_rows, width), low)...]
    reduce_sum x19 -> x0, other arithmetic: 40.6 us -> none  [the longest x5 17.3 us: scale_for(): return jnp.maximum(EPS_SCALE, jnp.sqrt(jnp.mean(weight * weight)))]
    conv_general_dilated x7 -> x0, matrix products: 31.2 us -> none  [the longest x4 17.3 us: conv_apply(): lax.conv_general_dilated(maps, kernel, (stride, stride), ((margin, margin...]
    pallas_call x3 -> x1, Pallas kernels: 38.8 us -> 14.4 us  [sum_all(): pl.pallas_call(sum_kernel, out_shape=jax.ShapeDtypeStruct(x.shape, x.dtyp...]
    convert_element_type x4 -> x0, other arithmetic: 11.5 us -> none  [the longest x3 11.5 us: local(): vote.astype(jnp.bfloat16)]
    concatenate x5 -> x2, other arithmetic: 6.6 us -> 0.03 us  [the longest x1 0.01 us: local(): flat_sum = jnp.concatenate([head_sum, tail_sum[classes:TAIL]])]
    unnamed x59 -> x18, local copies, waits for them, and re-layouts: 8.83 us -> 14.4 us
where the time goes in v2:
time: 196 us; the launch traced here: 193 us
  Pallas kernels  169 us (86%)
  local copies, waits for them, and re-layouts  21.8 us (11%)
    pallas_call x1, Pallas kernels, update_weights(): pl.pallas_call(functools.partial(update_kernel, tuple(edges), 1.0 / math....  96.1 us
    pallas_call x1, Pallas kernels, run_worker(): pl.pallas_call(worker_kernel, out_shape=(shape((matrix_rows, width), low)...  58.8 us
    unnamed x18, local copies, waits for them, and re-layouts  14.4 us
    pallas_call x1, Pallas kernels, sum_all(): pl.pallas_call(sum_kernel, out_shape=jax.ShapeDtypeStruct(x.shape, x.dtyp...  14.4 us

profile of v2, /device:TPU:0, one launch (start us, length us, event | category | flops | bytes accessed | tf_op | source)
XLA Modules:
  0.0 193.3 jit_solution(12273987758091296030)
XLA Ops:
  0.6 1.4 reduce
  2.1 0.9 copy.24.head_ref
  3.0 0.0 copy-start.1
  3.0 0.2 reshape.55
  3.2 2.8 %copy.22 = bf16[64,8,8,256]{3,0,2,1:T(8,128)(2,1)S(1)} copy(bf16[64,8,8,256]{3,2,1,0:T(8,128)(2,1)} %param.11) | data formatting | bytes 4194304 | tf_op args[0]
  5.9 1.5 copy.30
  7.4 0.0 copy-done.1
  7.4 0.0 copy-start.2
  7.4 0.0 copy-start
  7.4 58.8 %worker.1 = (bf16[7168,512]{1,0:T(8,128)(2,1)}, f32[24,512]{1,0:T(8,128)}, f32[8,512]{1,0:T(8,128)}, f32[1,512]{1,0:T(1,128)}, f32[60,128]{1,0:T(8,128)}, /*index=5*/f32[1,1546]{1,0:T(1,128)}, f32[1,3072]{1,0:T(1,128)}) custom-call(bf16[2,4,2,4,64,256]{5,4,3,2,1,0:T(8,128)(2,1)} %bitcast.25, f32[2304,512]{1,0:T(8,128)} %one_ref.1, f32[4608,512]{1,0:T(8,128)} %two_ref.1, ...), custom_call_target="tpu_custom_call" | custom-call | tf_op jit(solution)/shard_map/worker/pallas_call | solution.py:1037
  66.2 1.2 slice.22
  67.4 14.4 %sum_all.1 = f32[24,512]{1,0:T(8,128)} custom-call(f32[24,512]{1,0:T(8,128)} %get-tuple-element.18.x_ref), custom_call_target="tpu_custom_call" | custom-call | tf_op jit(solution)/shard_map/sum_all/pallas_call | solution.py:171
  81.8 1.2 slice.21
  83.0 0.8 slice_reduce_fusion.scale_ref
  83.7 0.8 fusion
  84.5 0.7 slice.25
  85.3 0.8 slice_bitcast_fusion
  86.0 1.4 copy.31
  87.4 0.1 copy.25
  87.6 0.2 reshape.54
  87.8 0.0 copy-done.2
  87.8 0.0 copy-done
  87.8 96.1 %update.1 = (f32[898,128]{1,0:T(8,128)S(1)}, f32[898,128]{1,0:T(8,128)S(1)}, bf16[28736,128]{1,0:T(8,128)(2,1)}) custom-call(f32[3]{0:T(128)S(1)} %slice_reduce_fusion.scale_ref, bf16[4,2,2,2,224,512]{5,4,3,2,1,0:T(8,128)(2,1)} %bitcast.27, f32[16,512]{1,0:T(8,128)S(1)} %get-tuple-element.30.tail_sum, f32[16,512]{1,0:T(8,128)S(1)} %get-tuple-element.31.tail_weight, ...), custom_call_target="tpu_custom_call" | custom-call | tf_op jit(solution)/shard_map/update/pallas_call | solution.py:497
  184.0 0.8 copy.37
  184.8 0.0 copy-start.4
  184.8 0.0 copy-start.3
  184.8 6.5 %copy.38 = bf16[3678208]{0:T(1024)(128)(2,1)} copy(bf16[3678208]{0:T(1024)(128)(2,1)} %bitcast.26) | data formatting | bytes 14712832
  191.3 0.8 copy.39
  192.1 0.0 copy-done.4
  192.1 0.6 copy.40
  192.7 0.0 copy-done.3
  192.7 0.6 copy.41
  (4 shorter events, 0.0 us)
Async XLA Ops:
  3.0 4.4 %copy-start.1 = (f32[512,10]{1,0:T(8,128)}, f32[512,10]{1,0:T(8,128)S(1)}, u32[]{:S(2)}) copy-start(f32[512,10]{1,0:T(8,128)S(1)} %copy.24.head_ref) | copy-start | bytes 61444
  7.4 80.4 %copy-start.2 = (f32[6,512]{1,0:T(8,128)S(1)}, f32[6,512]{1,0:T(8,128)}, u32[]{:S(2)}) copy-start(f32[6,512]{1,0:T(8,128)} %norm_ref.1) | copy-start | bytes 36868
  7.4 80.4 %copy-start = (f32[256,512]{1,0:T(8,128)S(1)}, f32[256,512]{1,0:T(8,128)}, u32[]{:S(2)}) copy-start(f32[256,512]{1,0:T(8,128)} %short_ref.1) | copy-start | bytes 1572868
  184.8 7.3 %copy-start.4 = (f32[1,1546]{1,0:T(1,128)S(1)}, f32[1,1546]{1,0:T(1,128)}, u32[]{:S(2)}) copy-start(f32[1,1546]{1,0:T(1,128)} %get-tuple-element.46) | copy-start | bytes 18556
  184.8 7.9 %copy-start.3 = (f32[1,3072]{1,0:T(1,128)S(1)}, f32[1,3072]{1,0:T(1,128)}, u32[]{:S(2)}) copy-start(f32[1,3072]{1,0:T(1,128)} %get-tuple-element.47) | copy-start | bytes 36868

commit v3 on v2

--- a/solution.py
+++ b/solution.py
@@ -123,13 +123,6 @@
     return me, core, x, y, z
 
 
-def greet(partners):
-    barrier = pltpu.get_barrier_semaphore()
-    for partner in partners:
-        pl.semaphore_signal(barrier, inc=1, device_id=(partner,), device_id_type=MESH)
-    pl.semaphore_wait(barrier, len(partners))
-
-
 def send(src, dst, send_sem, recv_sem, partner):
     copy = pltpu.make_async_remote_copy(
         src_ref=src,
@@ -143,393 +136,10 @@
     return copy
 
 
-def sum_kernel(x_ref, out_ref, plane, line, plane_send, plane_recv, line_send, line_recv):
-    me = lax.axis_index("dp")
-    z, spot = lax.div(me, 8), lax.rem(me, 8)
-    near = [z * 8 + lax.rem(spot + k, 8) for k in range(1, 8)]
-    far = [lax.rem(z + k, 4) * 8 + spot for k in range(1, 4)]
-    greet(near + far)
-    copies = [
-        send(x_ref, plane.at[spot], plane_send.at[k], plane_recv.at[k], partner)
-        for k, partner in enumerate(near)
-    ]
-    plane[spot] = x_ref[...]
-    for copy in copies:
-        copy.wait()
-    line[z] = functools.reduce(lambda a, b: a + b, [plane[k] for k in range(8)])
-    copies = [
-        send(line.at[z], line.at[z], line_send.at[k], line_recv.at[k], partner)
-        for k, partner in enumerate(far)
-    ]
-    for copy in copies:
-        copy.wait()
-    out_ref[...] = (line[0] + line[1]) + (line[2] + line[3])
-
-
-def sum_all(x, collective_id):
-    vmem = pl.BlockSpec(memory_space=pltpu.VMEM)
-    return pl.pallas_call(
-        sum_kernel,
-        out_shape=jax.ShapeDtypeStruct(x.shape, x.dtype),
-        in_specs=[vmem],
-        out_specs=vmem,
-        scratch_shapes=[
-            pltpu.VMEM((8,) + x.shape, x.dtype),
-            pltpu.VMEM((4,) + x.shape, x.dtype),
-            pltpu.SemaphoreType.DMA((7,)),
-            pltpu.SemaphoreType.DMA((7,)),
-            pltpu.SemaphoreType.DMA((3,)),
-            pltpu.SemaphoreType.DMA((3,)),
-        ],
-        compiler_params=pltpu.CompilerParams(collective_id=collective_id, has_side_effects=True),
-        name="sum_all",
-    )(x)
-
-
 def scale_of(row, scales, edges):
     picked = scales[2]
     picked = jnp.where(row < edges[1], scales[1], picked)
     return jnp.where(row < edges[0], scales[0], picked)
-
-
-def update_kernel(
-    edges,
-    root,
-    scale_ref,
-    votes,
-    tail_sum,
-    tail_weight,
-    tail_scale,
-    one_ref,
-    two_ref,
-    short_ref,
-    new_ref,
-    vote_ref,
-    out_ref,
-    core_in,
-    ax_in,
-    by_in,
-    plane_in,
-    line_in,
-    halo_in,
-    total,
-    weight,
-    vote_flat,
-    new_flat,
-    mine,
-    tail_low,
-    rs_send,
-    rs_recv,
-    line_send,
-    line_recv,
-    halo_sem,
-    ag_send,
-    ag_recv,
-    local_sem,
-):
-    me, core, x, y, z = place()
-    flip_core = me + 1 - 2 * core
-    flip_x = me + 2 - 4 * x
-    flip_y = me + 4 - 8 * y
-    planes = [lax.rem(z + k, 4) for k in range(4)]
-    sources = [lax.rem(z + 4 - k, 4) for k in range(4)]
-    spot = lax.rem(me, 8)
-    line_peers = [plane * 8 + spot for plane in planes]
-    before, after = lax.rem(me + 31, 32), lax.rem(me + 1, 32)
-    scales = [scale_ref[k] for k in range(3)]
-
-    def fetch(row, count, place_at, sem):
-        parts = (
-            (one_ref, 0, edges[0]),
-            (two_ref, edges[0], edges[1]),
-            (short_ref, edges[1], edges[2]),
-        )
-        for ref, low, high in parts:
-
-            @pl.when(jnp.logical_and(row >= low, row < high))
-            def _():
-                start = pl.multiple_of(row - low, count)
-                pltpu.make_async_copy(
-                    ref.at[pl.ds(start, count)], weight.at[pl.ds(place_at, count)], sem
-                ).start()
-
-    first_row = me * OWN
-    for k in range(OWN // PIECE):
-        fetch(first_row + k * PIECE, PIECE, k * PIECE, local_sem.at[0])
-    fetch(first_row + OWN, TAIL, OWN, local_sem.at[1])
-
-    greet([flip_core, flip_x, flip_y] + line_peers[1:] + [before, after])
-
-    order = [0, 3, 1, 2]
-
-    core_copies = [
-        send(
-            votes.at[t, :, :, 1 - core],
-            core_in.at[t],
-            rs_send.at[0, t],
-            rs_recv.at[0, t],
-            flip_core,
-        )
-        for t in order
-    ]
-
-    def first_steps(k, t):
-        core_copies[k].wait()
-        core_in[t] = core_in[t] + votes[t, :, :, core]
-        return (
-            send(
-                core_in.at[t, :, 1 - x, pl.ds(0, HALF)],
-                ax_in.at[t],
-                rs_send.at[1, t],
-                rs_recv.at[1, t],
-                flip_x,
-            ),
-            send(
-                core_in.at[t, 1 - y, :, pl.ds(HALF, HALF)],
-                by_in.at[t],
-                rs_send.at[2, t],
-                rs_recv.at[2, t],
-                flip_y,
-            ),
-        )
-
-    def second_steps(t, copies):
-        copies[0].wait()
-        ax_in[t] = ax_in[t] + core_in[t, :, x, :HALF]
-        first = send(
-            ax_in.at[t, 1 - y],
-            plane_in.at[t, pl.ds(0, HALF)],
-            rs_send.at[3, t],
-            rs_recv.at[3, t],
-            flip_y,
-        )
-        copies[1].wait()
-        by_in[t] = by_in[t] + core_in[t, y, :, HALF:]
-        second = send(
-            by_in.at[t, 1 - x],
-            plane_in.at[t, pl.ds(HALF, HALF)],
-            rs_send.at[4, t],
-            rs_recv.at[4, t],
-            flip_x,
-        )
-        return first, second
-
-    def line_copy(t):
-        return pltpu.make_async_remote_copy(
-            src_ref=plane_in.at[t],
-            dst_ref=line_in.at[z],
-            send_sem=line_send.at[t],
-            recv_sem=line_recv.at[z],
-            device_id=(t * 8 + spot,),
-            device_id_type=MESH,
-        )
-
-    def third_steps(t, copies):
-        copies[0].wait()
-        plane_in[t, :HALF] = plane_in[t, :HALF] + ax_in[t, y]
-        copies[1].wait()
-        plane_in[t, HALF:] = plane_in[t, HALF:] + by_in[t, x]
-
-        @pl.when(z != t)
-        def _():
-            line_copy(t).start()
-
-        @pl.when(z == t)
-        def _():
-            line_in[t] = plane_in[t]
-
-    firsts, seconds = {}, {}
-    for k in range(6):
-        if k < 4:
-            firsts[k] = first_steps(k, order[k])
-        if 1 <= k < 5:
-            seconds[k - 1] = second_steps(order[k - 1], firsts[k - 1])
-        if k >= 2:
-            third_steps(order[k - 2], seconds[k - 2])
-
-    for t in range(4):
-
-        @pl.when(z != t)
-        def _():
-            line_copy(t).wait_send()
-            pltpu.make_async_remote_copy(
-                src_ref=plane_in.at[t],
-                dst_ref=line_in.at[t],
-                send_sem=line_send.at[t],
-                recv_sem=line_recv.at[t],
-                device_id=(t * 8 + spot,),
-                device_id_type=MESH,
-            ).wait_recv()
-
-    total[pl.ds(0, OWN), :] = functools.reduce(
-        lambda a, b: a + b, [line_in[t].astype(jnp.float32) for t in range(4)]
-    )
-    halo = send(total.at[pl.ds(0, TAIL)], halo_in, halo_sem.at[0], halo_sem.at[1], before)
-
-    pltpu.make_async_copy(
-        weight.at[pl.ds(0, OWN)], weight.at[pl.ds(0, OWN)], local_sem.at[0]
-    ).wait()
-
-    def flat_rows(row, values, ref):
-        for k in range(4):
-            ref[pl.ds(row * 4 + k, 8, stride=4), :] = values[:, 128 * k : 128 * (k + 1)]
-
-    def renew(row, scale_row):
-        summed = total[pl.ds(row, 8), :]
-        fresh = weight[pl.ds(row, 8), :] - scale_row * jnp.tanh(summed * root)
-        flat_rows(row, summed, vote_flat)
-        flat_rows(row, fresh, new_flat)
-
-    @pl.loop(0, OWN // 8)
-    def _(k):
-        row = pl.multiple_of(k * 8, 8)
-        renew(row, scale_of(first_row + row, scales, edges))
-
-    mine[...] = new_flat[pl.ds(0, 4 * OWN), :].astype(jnp.bfloat16)
-
-    span, part = 4 * OWN, 4 * HALF
-
-    def rows_of(plane, yy, xx, cc, half):
-        block = plane * 8 + yy * 4 + xx * 2 + cc
-        return pl.ds(pl.multiple_of(block * span + half * part, 16), part)
-
-    own_rows = pl.ds(pl.multiple_of(me * span, 16), span)
-    keep = pltpu.make_async_copy(mine, out_ref.at[own_rows], local_sem.at[2])
-    keep.start()
-    spread = [
-        send(mine, out_ref.at[own_rows], ag_send.at[0, k], ag_recv.at[0, k], line_peers[k])
-        for k in range(1, 4)
-    ]
-
-    halo.wait()
-
-    @pl.when(me < 31)
-    def _():
-        pltpu.make_async_copy(
-            weight.at[pl.ds(OWN, TAIL)], weight.at[pl.ds(OWN, TAIL)], local_sem.at[1]
-        ).wait()
-        total[pl.ds(OWN, TAIL), :] = halo_in[...]
-        for k in range(TAIL // 8):
-            renew(OWN + 8 * k, scale_of(first_row + OWN + 8 * k, scales, edges))
-
-    tail_new = tail_weight[...] - tail_scale[...] * jnp.tanh(tail_sum[...] * root)
-    weight[pl.ds(OWN, TAIL), :] = tail_new
-
-    @pl.when(me == 31)
-    def _():
-        for k in range(TAIL // 8):
-            flat_rows(OWN + 8 * k, tail_sum[8 * k : 8 * k + 8, :], vote_flat)
-            flat_rows(OWN + 8 * k, weight[OWN + 8 * k : OWN + 8 * k + 8, :], new_flat)
-
-    shift = 2 * me
-    count = vote_ref.shape[0]
-    vote_ref[...] = vote_flat[pl.ds(shift, count), :]
-    new_ref[...] = new_flat[pl.ds(shift, count), :]
-    for k in range(TAIL // 8):
-        flat_rows(OWN + 8 * k, weight[OWN + 8 * k : OWN + 8 * k + 8, :], new_flat)
-    tail_low[...] = new_flat[pl.ds(4 * OWN, 4 * TAIL), :].astype(jnp.bfloat16)
-    keep_tail = pltpu.make_async_copy(
-        tail_low, out_ref.at[pl.ds(32 * span, 4 * TAIL)], local_sem.at[3]
-    )
-    keep_tail.start()
-
-    keep.wait()
-
-    def piece(plane, yy, xx, cc, half, kind, k, partner):
-        rows = rows_of(plane, yy, xx, cc, half)
-        return send(
-            out_ref.at[rows], out_ref.at[rows], ag_send.at[kind, k], ag_recv.at[kind, k], partner
-        )
-
-    stage_one, stage_two, stage_three = [], [], []
-    for k, plane in enumerate(sources):
-        if k:
-            spread[k - 1].wait()
-        stage_one.append(
-            (
-                piece(plane, y, x, core, 0, 1, k, flip_y),
-                piece(plane, y, x, core, 1, 2, k, flip_x),
-            )
-        )
-    for k, plane in enumerate(sources):
-        stage_one[k][0].wait()
-        stage_one[k][1].wait()
-        stage_two.append(
-            [piece(plane, yy, x, core, 0, 3 + yy, k, flip_x) for yy in range(2)]
-            + [piece(plane, y, xx, core, 1, 5 + xx, k, flip_y) for xx in range(2)]
-        )
-    for k, plane in enumerate(sources):
-        for copy in stage_two[k]:
-            copy.wait()
-        for yy in range(2):
-            for xx in range(2):
-                rows = pl.ds(
-                    pl.multiple_of((plane * 8 + yy * 4 + xx * 2 + core) * span, 16), span
-                )
-                kind = 7 + 2 * yy + xx
-                stage_three.append(
-                    send(
-                        out_ref.at[rows],
-                        out_ref.at[rows],
-                        ag_send.at[kind, k],
-                        ag_recv.at[kind, k],
-                        flip_core,
-                    )
-                )
-    for copy in stage_three:
-        copy.wait()
-    keep_tail.wait()
-
-
-def update_weights(
-    votes, tail_sum, tail_weight, tail_scale, scales, conv_one, conv_two, shortcut, workers
-):
-    edges = [conv_one.shape[0]]
-    edges.append(edges[0] + conv_two.shape[0])
-    edges.append(edges[1] + shortcut.shape[0])
-    width = conv_one.shape[1]
-    flat_rows = (edges[2] + TAIL) * width // 128
-    share = flat_rows // workers
-    vmem = pl.BlockSpec(memory_space=pltpu.VMEM)
-    hbm = pl.BlockSpec(memory_space=pl.ANY)
-    low = jnp.bfloat16
-    dma = pltpu.SemaphoreType.DMA
-    return pl.pallas_call(
-        functools.partial(update_kernel, tuple(edges), 1.0 / math.sqrt(workers)),
-        out_shape=(
-            jax.ShapeDtypeStruct((share, 128), jnp.float32),
-            jax.ShapeDtypeStruct((share, 128), jnp.float32),
-            jax.ShapeDtypeStruct((flat_rows, 128), low),
-        ),
-        in_specs=[pl.BlockSpec(memory_space=pltpu.SMEM)] + [vmem] * 4 + [hbm] * 3,
-        out_specs=(vmem, vmem, hbm),
-        scratch_shapes=[
-            pltpu.VMEM((4, 2, 2, OWN, width), low),
-            pltpu.VMEM((4, 2, HALF, width), low),
-            pltpu.VMEM((4, 2, HALF, width), low),
-            pltpu.VMEM((4, OWN, width), low),
-            pltpu.VMEM((4, OWN, width), low),
-            pltpu.VMEM((TAIL, width), jnp.float32),
-            pltpu.VMEM((OWN + TAIL, width), jnp.float32),
-            pltpu.VMEM((OWN + TAIL, width), jnp.float32),
-            pltpu.VMEM((4 * (OWN + TAIL), 128), jnp.float32),
-            pltpu.VMEM((4 * (OWN + TAIL), 128), jnp.float32),
-            pltpu.VMEM((4 * OWN, 128), low),
-            pltpu.VMEM((4 * TAIL, 128), low),
-            dma((5, 4)),
-            dma((5, 4)),
-            dma((4,)),
-            dma((4,)),
-            dma((2,)),
-            dma((11, 4)),
-            dma((11, 4)),
-            dma((4,)),
-        ],
-        compiler_params=pltpu.CompilerParams(
-            collective_id=5, has_side_effects=True, vmem_limit_bytes=48 * 1024 * 1024
-        ),
-        name="update",
-    )(scales, votes, tail_sum, tail_weight, tail_scale, conv_one, conv_two, shortcut)
 
 
 def settle_rows(sums, pixels, gain, shift):
@@ -575,9 +185,7 @@
             square_ref[...] += fold(values * values)
 
 
-def factored_votes(
-    grad, rows, row_block, rows_ref, rows_new, col_old, level, votes, vote_at
-):
+def factored_votes(grad, rows, row_at, rows_old, rows_new, col_old, level, votes, vote_at, between):
     width = grad.shape[1]
     keep = 1.0 - STEP ** (-0.8)
     step = 128
@@ -586,7 +194,8 @@
     def first(k, carry):
         col_sum, row_sum = carry
         start = pl.multiple_of(k * step, step)
-        old = rows_ref[pl.ds(row_block + k, 1), :] * keep
+        lanes = pl.ds(pl.multiple_of(row_at + start, step), step)
+        old = rows_old[:, lanes] * keep
         line = jnp.zeros((8, 128), jnp.float32)
         for m in range(step // 8):
             block = grad[pl.ds(start + 8 * m, 8), :]
@@ -603,7 +212,7 @@
             level[pl.ds(start + 8 * m, 8), :] = row
             row_sum = row_sum + row
             line = line + jnp.where(diagonal, row, 0.0)
-        rows_new[pl.ds(row_block + k, 1), :] = jnp.sum(line, axis=0, keepdims=True)
+        rows_new[:, lanes] = jnp.sum(line, axis=0, keepdims=True)
         return col_sum, row_sum
 
     col_sum, row_sum = lax.fori_loop(
@@ -632,7 +241,9 @@
             carry = carry + part * (factor * factor)
         return carry
 
+    between[0]()
     power = lax.fori_loop(0, rows // step, second, jnp.zeros((8, 128), jnp.float32))
+    between[1]()
     clip = jnp.maximum(1.0, jnp.sqrt(total_of(power) / (rows * width)))
     scale = scale / clip
 
@@ -650,7 +261,9 @@
     return col_new
 
 
-def worker_kernel(
+def step_kernel(
+    edges,
+    root,
     xs,
     one_hbm,
     two_hbm,
@@ -662,13 +275,14 @@
     row_ref,
     col_ref,
     moment_ref,
-    votes,
-    tail_ref,
-    scale_ref,
-    count_ref,
+    new_ref,
+    vote_ref,
+    out_ref,
     row_new,
     col_new,
     moment_new,
+    loss_ref,
+    count_ref,
     grad_one,
     grad_two,
     grad_short,
@@ -690,26 +304,55 @@
     post,
     plane,
     line,
+    tail_post,
+    tail_plane,
+    tail_line,
+    votes,
+    core_in,
+    ax_in,
+    by_in,
+    plane_in,
+    line_in,
+    halo_in,
+    total,
+    weight,
+    vote_flat,
+    new_flat,
+    mine,
+    tail_low,
     fetch_sem,
-    plane_send,
-    plane_recv,
+    small_send,
+    small_recv,
+    core_send,
+    core_recv,
+    rs_send,
+    rs_recv,
     line_send,
     line_recv,
+    halo_sem,
+    ag_send,
+    ag_recv,
+    keep_sem,
 ):
     slots, in_width = xs.shape[4:]
     width = main_pre.shape[1]
     side = 4
     band = side * slots
     pixel_count = side * side
-    classes = head_ref.shape[1]
+    classes = head_ref.shape[0]
     keep = 1.0 - STEP ** (-0.8)
     low = jnp.bfloat16
     f32 = jnp.float32
 
-    me = lax.axis_index("dp")
-    z, spot = lax.div(me, 8), lax.rem(me, 8)
+    me, core, x, y, z = place()
+    flip_core = me + 1 - 2 * core
+    flip_x = me + 2 - 4 * x
+    flip_y = me + 4 - 8 * y
+    spot = lax.rem(me, 8)
     near = [z * 8 + lax.rem(spot + k, 8) for k in range(1, 8)]
     far = [lax.rem(z + k, 4) * 8 + spot for k in range(1, 4)]
+    ahead, behind = lax.rem(me + 31, 32), lax.rem(me + 1, 32)
+    partners = near + far + [ahead, behind]
 
     fetches = [
         pltpu.make_async_copy(source, target, fetch_sem.at[k])
@@ -720,47 +363,266 @@
     for fetch in fetches:
         fetch.start()
     barrier = pltpu.get_barrier_semaphore()
-    for partner in near + far:
+    for partner in partners:
         pl.semaphore_signal(barrier, inc=1, device_id=(partner,), device_id_type=MESH)
 
-    def scale_row(row, weight_square, size):
-        mean = total_of(weight_square) / size
-        value = jnp.maximum(EPS_SCALE, jnp.sqrt(mean))
-        scale_ref[row : row + 1, :] = jnp.broadcast_to(value, (1, width))
+    def fetch_rows(row, count, place_at, sem):
+        parts = (
+            (one_hbm, 0, edges[0]),
+            (two_hbm, edges[0], edges[1]),
+            (short_hbm, edges[1], edges[2]),
+        )
+        for ref, first, last in parts:
+
+            @pl.when(jnp.logical_and(row >= first, row < last))
+            def _():
+                start = pl.multiple_of(row - first, count)
+                pltpu.make_async_copy(
+                    ref.at[pl.ds(start, count)], weight.at[pl.ds(place_at, count)], sem
+                ).start()
+
+    first_row = me * OWN
+    for k in range(OWN // PIECE):
+        fetch_rows(first_row + k * PIECE, PIECE, k * PIECE, fetch_sem.at[3])
+    fetch_rows(first_row + OWN, TAIL, OWN, fetch_sem.at[4])
+
+    scales = {}
+
+    def scale_from(weight_square, size):
+        return jnp.maximum(EPS_SCALE, jnp.sqrt(total_of(weight_square) / size))
+
+    exchanges = (
+        (post.at[0], plane.at[0], line.at[0]),
+        (post.at[1], plane.at[1], line.at[1]),
+        (tail_post, tail_plane, tail_line),
+    )
 
     def exchange_start(which, values):
-        post[which] = values
-        plane[which, spot] = values
+        mine_ref, plane_ref, _ = exchanges[which]
+        mine_ref[...] = values
+        plane_ref[spot] = values
         return [
             send(
-                post.at[which],
-                plane.at[which, spot],
-                plane_send.at[which, k],
-                plane_recv.at[which, k],
+                mine_ref,
+                plane_ref.at[spot],
+                small_send.at[which, k],
+                small_recv.at[which, k],
                 partner,
             )
             for k, partner in enumerate(near)
         ]
 
     def exchange_middle(which, copies):
+        _, plane_ref, line_ref = exchanges[which]
         for copy in copies:
             copy.wait()
-        line[which, z] = functools.reduce(lambda a, b: a + b, [plane[which, k] for k in range(8)])
+        line_ref[z] = functools.reduce(lambda a, b: a + b, [plane_ref[k] for k in range(8)])
         return [
             send(
-                line.at[which, z],
-                line.at[which, z],
-                line_send.at[which, k],
-                line_recv.at[which, k],
+                line_ref.at[z],
+                line_ref.at[z],
+                small_send.at[which, 7 + k],
+                small_recv.at[which, 7 + k],
                 partner,
             )
             for k, partner in enumerate(far)
         ]
 
     def exchange_end(which, copies):
+        line_ref = exchanges[which][2]
         for copy in copies:
             copy.wait()
-        return (line[which, 0] + line[which, 1]) + (line[which, 2] + line[which, 3])
+        return (line_ref[0] + line_ref[1]) + (line_ref[2] + line_ref[3])
+
+    def block_rows(t, yy, xx, cc):
+        block = t * 8 + yy * 4 + xx * 2 + cc
+        return pl.ds(pl.multiple_of(block * OWN, 16), OWN)
+
+    def scatter_start(t):
+        return [
+            send(
+                votes.at[block_rows(t, yy, xx, 1 - core)],
+                core_in.at[t, yy, xx],
+                core_send.at[t, 2 * yy + xx],
+                core_recv.at[t, 2 * yy + xx],
+                flip_core,
+            )
+            for yy in range(2)
+            for xx in range(2)
+        ]
+
+    def scatter_one(t, copies):
+        for copy in copies:
+            copy.wait()
+        for yy in range(2):
+            for xx in range(2):
+                core_in[t, yy, xx] = core_in[t, yy, xx] + votes[block_rows(t, yy, xx, core), :]
+        return (
+            send(
+                core_in.at[t, :, 1 - x, pl.ds(0, HALF)],
+                ax_in.at[t],
+                rs_send.at[0, t],
+                rs_recv.at[0, t],
+                flip_x,
+            ),
+            send(
+                core_in.at[t, 1 - y, :, pl.ds(HALF, HALF)],
+                by_in.at[t],
+                rs_send.at[1, t],
+                rs_recv.at[1, t],
+                flip_y,
+            ),
+        )
+
+    def scatter_two(t, copies):
+        copies[0].wait()
+        ax_in[t] = ax_in[t] + core_in[t, :, x, :HALF]
+        first = send(
+            ax_in.at[t, 1 - y],
+            plane_in.at[t, pl.ds(0, HALF)],
+            rs_send.at[2, t],
+            rs_recv.at[2, t],
+            flip_y,
+        )
+        copies[1].wait()
+        by_in[t] = by_in[t] + core_in[t, y, :, HALF:]
+        second = send(
+            by_in.at[t, 1 - x],
+            plane_in.at[t, pl.ds(HALF, HALF)],
+            rs_send.at[3, t],
+            rs_recv.at[3, t],
+            flip_x,
+        )
+        return first, second
+
+    def line_copy(t, slot):
+        return pltpu.make_async_remote_copy(
+            src_ref=plane_in.at[t],
+            dst_ref=line_in.at[slot],
+            send_sem=line_send.at[t],
+            recv_sem=line_recv.at[slot],
+            device_id=(t * 8 + spot,),
+            device_id_type=MESH,
+        )
+
+    def scatter_three(t, copies):
+        copies[0].wait()
+        plane_in[t, :HALF] = plane_in[t, :HALF] + ax_in[t, y]
+        copies[1].wait()
+        plane_in[t, HALF:] = plane_in[t, HALF:] + by_in[t, x]
+
+        @pl.when(z != t)
+        def _():
+            line_copy(t, z).start()
+
+        @pl.when(z == t)
+        def _():
+            line_in[t] = plane_in[t]
+
+    span, part = 4 * OWN, 4 * HALF
+    own_rows = pl.ds(pl.multiple_of(me * span, 16), span)
+
+    def flat_rows(row, values, ref):
+        for k in range(4):
+            ref[pl.ds(row * 4 + k, 8, stride=4), :] = values[:, 128 * k : 128 * (k + 1)]
+
+    def renew(row, at_row):
+        scale = scale_of(at_row, [scales[k] for k in range(3)], edges)
+        summed = total[pl.ds(row, 8), :]
+        fresh = weight[pl.ds(row, 8), :] - scale * jnp.tanh(summed * root)
+        flat_rows(row, summed, vote_flat)
+        flat_rows(row, fresh, new_flat)
+
+    def halo_copy():
+        return pltpu.make_async_remote_copy(
+            src_ref=total.at[pl.ds(0, TAIL)],
+            dst_ref=halo_in,
+            send_sem=halo_sem.at[0],
+            recv_sem=halo_sem.at[1],
+            device_id=(ahead,),
+            device_id_type=MESH,
+        )
+
+    def keep_copy():
+        return pltpu.make_async_copy(mine, out_ref.at[own_rows], keep_sem.at[0])
+
+    def spread_copy(k):
+        return pltpu.make_async_remote_copy(
+            src_ref=mine,
+            dst_ref=out_ref.at[own_rows],
+            send_sem=ag_send.at[0, k],
+            recv_sem=ag_recv.at[0, z],
+            device_id=(far[k],),
+            device_id_type=MESH,
+        )
+
+    def own_block():
+        for k in range(1, 4):
+            line_copy(0, lax.rem(z + k, 4)).wait_recv()
+        total[pl.ds(0, OWN), :] = functools.reduce(
+            lambda a, b: a + b, [line_in[t].astype(f32) for t in range(4)]
+        )
+        halo_copy().start()
+        pltpu.make_async_copy(
+            weight.at[pl.ds(0, OWN)], weight.at[pl.ds(0, OWN)], fetch_sem.at[3]
+        ).wait()
+
+        @pl.loop(0, OWN // 8)
+        def _(k):
+            row = pl.multiple_of(k * 8, 8)
+            renew(row, first_row + row)
+
+        mine[...] = new_flat[pl.ds(0, span), :].astype(low)
+        keep_copy().start()
+        for k in range(3):
+            spread_copy(k).start()
+
+    def piece(rows, kind, t, partner):
+        return send(
+            out_ref.at[rows], out_ref.at[rows], ag_send.at[kind, t], ag_recv.at[kind, t], partner
+        )
+
+    def half_rows(t, yy, xx, half):
+        block = t * 8 + yy * 4 + xx * 2 + core
+        return pl.ds(pl.multiple_of(block * span + half * part, 16), part)
+
+    def gather_one(t):
+        @pl.when(z == t)
+        def _():
+            keep_copy().wait()
+
+        @pl.when(z != t)
+        def _():
+            pltpu.make_async_remote_copy(
+                src_ref=mine,
+                dst_ref=out_ref.at[own_rows],
+                send_sem=ag_send.at[0, 0],
+                recv_sem=ag_recv.at[0, t],
+                device_id=(far[0],),
+                device_id_type=MESH,
+            ).wait_recv()
+
+        return (
+            piece(half_rows(t, y, x, 0), 1, t, flip_y),
+            piece(half_rows(t, y, x, 1), 2, t, flip_x),
+        )
+
+    def gather_two(t, copies):
+        copies[0].wait()
+        sent = [piece(half_rows(t, yy, x, 0), 3 + yy, t, flip_x) for yy in range(2)]
+        copies[1].wait()
+        return sent + [piece(half_rows(t, y, xx, 1), 5 + xx, t, flip_y) for xx in range(2)]
+
+    def gather_three(t, copies):
+        for copy in copies:
+            copy.wait()
+        sent = []
+        for yy in range(2):
+            for xx in range(2):
+                block = t * 8 + yy * 4 + xx * 2 + core
+                rows = pl.ds(pl.multiple_of(block * span, 16), span)
+                sent.append(piece(rows, 7 + 2 * yy + xx, t, flip_core))
+        return sent
 
     valid_column = column_of(valid_ref[...].astype(f32), slots)
     weight_slot = jnp.broadcast_to(valid_column, (slots, width))
@@ -768,10 +630,10 @@
 
     fetches[0].wait()
     cast_weight(grad_one, low_one, square, 9, in_width)
-    scale_row(0, square[...], grad_one.size)
+    scales[0] = scale_from(square[...], grad_one.size)
     fetches[1].wait()
     cast_weight(grad_short, low_short, square, 1, in_width)
-    scale_row(2, square[...], grad_short.size)
+    scales[2] = scale_from(square[...], grad_short.size)
 
     def image_taps(j):
         pieces = []
@@ -816,13 +678,13 @@
         side_sums = add_up(side_sums, moments(value))
 
     count = jnp.broadcast_to(jnp.sum(valid_column, axis=0, keepdims=True), (1, width))
-    pl.semaphore_wait(barrier, len(near) + len(far))
+    pl.semaphore_wait(barrier, len(partners))
     copies = exchange_start(
         0, jnp.concatenate(main_sums + side_sums + [count, none, none, none], axis=0)
     )
     fetches[2].wait()
     cast_weight(grad_two, low_two, square, 9, width)
-    scale_row(1, square[...], grad_two.size)
+    scales[1] = scale_from(square[...], grad_two.size)
     copies = exchange_middle(0, copies)
     for across in range(2):
         for down in range(2):
@@ -836,15 +698,15 @@
     back_two[:, side + 1 :] = border
     back_one[:, side:] = border
     head_pad[...] = jnp.zeros_like(head_pad)
-    head_pad[:, :classes] = head_ref[...]
-    head = head_pad[...]
-    scale_row(3, fold(head * head)[:, :128], head_ref.size)
+    head_pad[:classes, :] = head_ref[...]
+    head = head_pad[:16, :]
+    scales[3] = scale_from(head * head, head_ref.size)
     params = norm_ref[...]
-    scale_row(4, params * params, norm_ref.size)
+    scales[4] = scale_from(params * params, norm_ref.size)
     sums = exchange_end(0, copies)
 
     valid_count = sums[4:5]
-    count_ref[...] = valid_count
+    count_ref[...] = valid_count[:, :1]
     denominator = jnp.maximum(valid_count, 1.0)
     pixels = denominator * pixel_count
     gains = [norm_ref[k : k + 1, :] for k in range(6)]
@@ -891,7 +753,9 @@
         pooled = pooled + joined * gate(joined)
     pooled = (pooled / pixel_count).astype(low)
     head_low = head_pad[...].astype(low)
-    logits = jnp.dot(pooled, head_low, preferred_element_type=f32)
+    logits = lax.dot_general(
+        pooled, head_low, (((1,), (1,)), ((), ())), preferred_element_type=f32
+    )
     lane = lax.broadcasted_iota(jnp.int32, logits.shape, 1)
     real = lane < classes
     largest = jnp.max(jnp.where(real, logits, -jnp.inf), axis=1, keepdims=True)
@@ -907,10 +771,7 @@
     grad_head = lax.dot_general(
         grad_logits, pooled, (((0,), (0,)), ((), ())), preferred_element_type=f32
     )[:16]
-    grad_pooled = lax.dot_general(
-        grad_logits, head_low, (((1,), (1,)), ((), ())), preferred_element_type=f32
-    )
-    grad_pooled = grad_pooled / pixel_count
+    grad_pooled = jnp.dot(grad_logits, head_low, preferred_element_type=f32) / pixel_count
 
     gain_two, gain_side, shift_two = none, none, none
     for p in range(pixel_count):
@@ -937,6 +798,21 @@
             grad_two[pl.ds((a * 3 + b) * width, width), :] = jnp.dot(
                 left, right.reshape(-1, width), preferred_element_type=f32
             )
+
+
+    def nothing():
+        pass
+
+    def matrix_votes(k, grad, between):
+        here = pl.ds(k * width, width)
+        start = edges[k - 1] if k else 0
+        col_new[:, here] = factored_votes(
+            grad, grad.shape[0], start, row_ref, row_new, col_ref[:, here], level, votes, start, between
+        )
+
+    matrix_votes(2, grad_short, (nothing, nothing))
+    matrix_votes(1, grad_two, (nothing, nothing))
+    stage = {t: scatter_start(t) for t in (2, 3)}
 
     gain_one, shift_one = none, none
     for j in range(side):
@@ -962,6 +838,46 @@
             grad * ((before - mean_one) * inv_one), axis=0, keepdims=True
         )
         back_one[j, :side] = (grad * slope_one).astype(low).reshape(side, slots, width)
+        if j == 1:
+            stage[2] = scatter_one(2, stage[2])
+        if j == 2:
+            stage[3] = scatter_one(3, stage[3])
+
+    square_head = grad_head * grad_head + EPS_ROW
+    real = lax.broadcasted_iota(jnp.int32, square_head.shape, 0) < classes
+    square_head = jnp.where(real, square_head, 0.0)
+    head_lanes = pl.ds(edges[2], width)
+    old = row_ref[:, head_lanes]
+    row = keep * old + (1.0 - keep) * jnp.sum(square_head, axis=0, keepdims=True) / classes
+    row_new[:, head_lanes] = row
+    diagonal = eye_mask(16, classes)
+    old = jnp.broadcast_to(col_ref[:, 3 * width :], (16, classes))
+    old = jnp.sum(jnp.where(diagonal, old, 0.0), axis=1, keepdims=True)
+    column = keep * old + (1.0 - keep) * jnp.sum(square_head, axis=1, keepdims=True) / width
+    col_new[:, 3 * width :] = jnp.sum(
+        jnp.where(diagonal, jnp.broadcast_to(column, (16, classes)), 0.0), axis=0, keepdims=True
+    )
+    real_column = lax.broadcasted_iota(jnp.int32, column.shape, 0) < classes
+    column = jnp.where(real_column, column, 1.0)
+    mean = jnp.sum(row, axis=1, keepdims=True) / width
+    raw = grad_head * (lax.rsqrt(row) * jnp.sqrt(mean)) * lax.rsqrt(column)
+    clip = jnp.maximum(1.0, jnp.sqrt(total_of(raw * raw) / (classes * width)))
+    head_votes = jnp.tanh(raw / clip)[:classes]
+
+    raws = []
+    for k, grad in enumerate((gain_one, shift_one, gain_two, shift_two, gain_side, shift_two)):
+        here = pl.ds(k * width, width)
+        moment = keep * moment_ref[:, here] + (1.0 - keep) * (grad * grad + EPS_ROW)
+        moment_new[:, here] = moment
+        raws.append(grad * lax.rsqrt(moment))
+    raw = jnp.concatenate(raws, axis=0)
+    clip = jnp.maximum(1.0, jnp.sqrt(total_of(raw * raw) / raw.size))
+    norm_votes = jnp.tanh(raw / clip)
+    copies = exchange_start(
+        2,
+        jnp.concatenate([head_votes, norm_votes, jnp.broadcast_to(loss, (8, width))], axis=0),
+    )
+
 
     for b in range(3):
         first, last = (0, side - 1) if b == 0 else (0, side)
@@ -973,80 +889,187 @@
             grad_one[pl.ds((a * 3 + b) * in_width, in_width), :] = jnp.dot(
                 left, right.reshape(-1, width), preferred_element_type=f32
             )
-
-    row_at, vote_at = 0, 0
-    for k, grad in enumerate((grad_one, grad_two, grad_short)):
-        here = pl.ds(k * width, width)
-        col_new[:, here] = factored_votes(
-            grad,
-            grad.shape[0],
-            row_at,
-            row_ref,
-            row_new,
-            col_ref[:, here],
-            level,
-            votes,
-            vote_at,
-        )
-        row_at += grad.shape[0] // 128
-        vote_at += grad.shape[0]
-
-    square_head = grad_head * grad_head + EPS_ROW
-    real = lax.broadcasted_iota(jnp.int32, square_head.shape, 0) < classes
-    square_head = jnp.where(real, square_head, 0.0)
-    old = jnp.concatenate([row_ref[row_at + k : row_at + k + 1, :] for k in range(4)], axis=1)
-    row = keep * old + (1.0 - keep) * jnp.sum(square_head, axis=0, keepdims=True) / classes
-    for k in range(4):
-        row_new[row_at + k : row_at + k + 1, :] = row[:, 128 * k : 128 * (k + 1)]
-    diagonal = eye_mask(16, classes)
-    old = jnp.broadcast_to(col_ref[:, 3 * width :], (16, classes))
-    old = jnp.sum(jnp.where(diagonal, old, 0.0), axis=1, keepdims=True)
-    column = keep * old + (1.0 - keep) * jnp.sum(square_head, axis=1, keepdims=True) / width
-    col_new[:, 3 * width :] = jnp.sum(
-        jnp.where(diagonal, jnp.broadcast_to(column, (16, classes)), 0.0), axis=0, keepdims=True
-    )
-    real_column = lax.broadcasted_iota(jnp.int32, column.shape, 0) < classes
-    column = jnp.where(real_column, column, 1.0)
-    mean = jnp.sum(row, axis=1, keepdims=True) / width
-    raw = grad_head * (lax.rsqrt(row) * jnp.sqrt(mean)) * lax.rsqrt(column)
-    clip = jnp.maximum(1.0, jnp.sqrt(total_of(raw * raw) / (classes * width)))
-    tail_ref[:16, :] = jnp.tanh(raw / clip)
-
-    raws = []
-    for k, grad in enumerate((gain_one, shift_one, gain_two, shift_two, gain_side, shift_two)):
-        here = pl.ds(k * width, width)
-        moment = keep * moment_ref[:, here] + (1.0 - keep) * (grad * grad + EPS_ROW)
-        moment_new[:, here] = moment
-        raws.append(grad * lax.rsqrt(moment))
-    raw = jnp.concatenate(raws, axis=0)
-    clip = jnp.maximum(1.0, jnp.sqrt(total_of(raw * raw) / raw.size))
-    tail_ref[classes : classes + 6, :] = jnp.tanh(raw / clip)
-    tail_ref[16:, :] = jnp.broadcast_to(loss, (8, width))
-
-
-def run_worker(xs, conv_one, conv_two, shortcut, classifier, norm_params, valid, labels, rows, cols, moment):
+        if b == 0:
+            stage[2] = scatter_two(2, stage[2])
+        if b == 1:
+            copies = exchange_middle(2, copies)
+        if b == 2:
+            stage[3] = scatter_two(3, stage[3])
+
+    matrix_votes(
+        0,
+        grad_one,
+        (lambda: scatter_three(2, stage[2]), lambda: scatter_three(3, stage[3])),
+    )
+    stage = {t: scatter_start(t) for t in (1, 0)}
+
+    @pl.when(z >= 2)
+    def _():
+        own_block()
+
+    gathered = {}
+    for t in (1, 0):
+        stage[t] = scatter_one(t, stage[t])
+    for t in (2, 3):
+        gathered[t] = gather_one(t)
+    for t in (1, 0):
+        stage[t] = scatter_two(t, stage[t])
+    for t in (2, 3):
+        gathered[t] = gather_two(t, gathered[t])
+    for t in (1, 0):
+        scatter_three(t, stage[t])
+    for t in (2, 3):
+        gathered[t] = gather_three(t, gathered[t])
+
+    @pl.when(z < 2)
+    def _():
+        own_block()
+
+    sums = exchange_end(2, copies)
+    loss_ref[...] = sums[TAIL:, :1][:1]
+    old = jnp.concatenate([head_ref[...], norm_ref[...]], axis=0)
+    is_head = lax.broadcasted_iota(jnp.int32, (TAIL, width), 0) < classes
+    scale = jnp.where(is_head, scales[3], scales[4])
+    sums = sums[:TAIL]
+    fresh = old - scale * jnp.tanh(sums * root)
+    both = jnp.concatenate([sums, fresh], axis=0)
+    high = both.astype(low)
+    rest = both - high.astype(f32)
+    middle = rest.astype(low)
+    parts = jnp.concatenate([high, middle, (rest - middle.astype(f32)).astype(low)], axis=0)
+
+    for t in (1, 0):
+        gathered[t] = gather_one(t)
+
+    flat_sums, flat_new = [], []
+    window = 256
+    for q in range(classes):
+        start = min(q * width // classes // 128 * 128, width - window)
+        down = lax.broadcasted_iota(jnp.int32, (window, width), 0)
+        across = lax.broadcasted_iota(jnp.int32, (window, width), 1)
+        gap = across - classes * down + (q * width - classes * start)
+        chosen = jnp.where(jnp.logical_and(gap >= 0, gap < classes), 1.0, 0.0).astype(low)
+        moved = jnp.dot(parts[:, start : start + window], chosen, preferred_element_type=f32)
+        moved = moved[: 2 * TAIL] + moved[2 * TAIL : 4 * TAIL] + moved[4 * TAIL :]
+        spot_of = lax.broadcasted_iota(jnp.int32, (TAIL, width), 1).astype(f32) + q * width
+        class_of = spot_of - classes * jnp.floor((spot_of + 0.5) / classes)
+        here = lax.broadcasted_iota(jnp.int32, (TAIL, width), 0).astype(f32) == class_of
+        flat_sums.append(jnp.sum(jnp.where(here, moved[:TAIL], 0.0), axis=0, keepdims=True))
+        flat_new.append(jnp.sum(jnp.where(here, moved[TAIL:], 0.0), axis=0, keepdims=True))
+    flat_sums = jnp.concatenate(flat_sums + [sums[classes:]], axis=0)
+    flat_new = jnp.concatenate(flat_new + [fresh[classes:]], axis=0)
+
+    for t in (1, 0):
+        gathered[t] = gather_two(t, gathered[t])
+
+    halo_copy().wait()
+
+    @pl.when(me < 31)
+    def _():
+        pltpu.make_async_copy(
+            weight.at[pl.ds(OWN, TAIL)], weight.at[pl.ds(OWN, TAIL)], fetch_sem.at[4]
+        ).wait()
+        total[pl.ds(OWN, TAIL), :] = halo_in[...]
+        for k in range(TAIL // 8):
+            renew(OWN + 8 * k, first_row + OWN + 8 * k)
+
+    @pl.when(me == 31)
+    def _():
+        for k in range(TAIL // 8):
+            flat_rows(OWN + 8 * k, flat_sums[8 * k : 8 * k + 8], vote_flat)
+            flat_rows(OWN + 8 * k, flat_new[8 * k : 8 * k + 8], new_flat)
+
+    shift = 2 * me
+    share = vote_ref.shape[0]
+    vote_ref[...] = vote_flat[pl.ds(shift, share), :]
+    new_ref[...] = new_flat[pl.ds(shift, share), :]
+    for k in range(TAIL // 8):
+        flat_rows(OWN + 8 * k, flat_new[8 * k : 8 * k + 8], new_flat)
+    tail_low[...] = new_flat[pl.ds(span, 4 * TAIL), :].astype(low)
+    keep_tail = pltpu.make_async_copy(
+        tail_low, out_ref.at[pl.ds(32 * span, 4 * TAIL)], keep_sem.at[1]
+    )
+    keep_tail.start()
+
+    for t in (1, 0):
+        gathered[t] = gather_three(t, gathered[t])
+    for t in range(4):
+        for copy in gathered[t]:
+            copy.wait()
+
+        @pl.when(z != t)
+        def _():
+            line_copy(t, z).wait_send()
+
+    for k in range(3):
+        spread_copy(k).wait_send()
+    keep_tail.wait()
+
+
+def finish_kernel(count, chunks, *refs):
+    sources, targets, sem = refs[:count], refs[count : 2 * count], refs[2 * count]
+    copies = []
+    rows = sources[0].shape[0]
+    step = -(-rows // chunks // 16) * 16
+    for k in range(chunks):
+        here = pl.ds(k * step, min(step, rows - k * step))
+        copies.append(
+            pltpu.make_async_copy(sources[0].at[here], targets[0].at[here], sem.at[k])
+        )
+    for k in (1, 2):
+        copies.append(pltpu.make_async_copy(sources[k], targets[k], sem.at[chunks + k]))
+    for copy in copies:
+        copy.start()
+    for k in range(3, count):
+        targets[k][...] = sources[k][...]
+    for copy in copies:
+        copy.wait()
+
+
+def finish(values):
+    vmem = pl.BlockSpec(memory_space=pltpu.VMEM)
+    hbm = pl.BlockSpec(memory_space=pl.ANY)
+    count, chunks = len(values), 8
+    specs = [hbm] * 3 + [vmem] * (count - 3)
+    return pl.pallas_call(
+        functools.partial(finish_kernel, count, chunks),
+        out_shape=[jax.ShapeDtypeStruct(value.shape, value.dtype) for value in values],
+        in_specs=specs,
+        out_specs=specs,
+        scratch_shapes=[pltpu.SemaphoreType.DMA((chunks + 3,))],
+        name="finish",
+    )(*values)
+
+
+def run_step(xs, conv_one, conv_two, shortcut, head, norm_params, valid, labels, rows, cols, moment):
     vmem = pl.BlockSpec(memory_space=pltpu.VMEM)
     hbm = pl.BlockSpec(memory_space=pl.ANY)
     low, f32 = jnp.bfloat16, jnp.float32
     dma = pltpu.SemaphoreType.DMA
+    workers = lax.axis_size("dp")
     slots, in_width = xs.shape[4:]
     width = conv_one.shape[1]
     pixels = 16 * slots
     shape = jax.ShapeDtypeStruct
-    matrix_rows = conv_one.shape[0] + conv_two.shape[0] + shortcut.shape[0]
+    edges = [conv_one.shape[0]]
+    edges.append(edges[0] + conv_two.shape[0])
+    edges.append(edges[1] + shortcut.shape[0])
+    flat = (edges[2] + TAIL) * width // 128
+    share = flat // workers
     return pl.pallas_call(
-        worker_kernel,
+        functools.partial(step_kernel, tuple(edges), 1.0 / math.sqrt(workers)),
         out_shape=(
-            shape((matrix_rows, width), low),
-            shape((TAIL + 8, width), f32),
-            shape((8, width), f32),
-            shape((1, width), f32),
+            shape((share, 128), f32),
+            shape((share, 128), f32),
+            shape((flat, 128), low),
             shape(rows.shape, f32),
             shape(cols.shape, f32),
             shape(moment.shape, f32),
+            shape((1, 1), f32),
+            shape((1, 1), f32),
         ),
         in_specs=[vmem] + [hbm] * 3 + [vmem] * 7,
-        out_specs=(vmem,) * 7,
+        out_specs=(vmem, vmem, hbm) + (vmem,) * 5,
         scratch_shapes=[
             pltpu.VMEM(conv_one.shape, f32),
             pltpu.VMEM(conv_two.shape, f32),
@@ -1063,23 +1086,47 @@
             pltpu.VMEM((pixels, width), low),
             pltpu.VMEM((width, pixels), low),
             pltpu.VMEM((2, 2, in_width, pixels), low),
-            pltpu.VMEM((width, 128), f32),
+            pltpu.VMEM((128, width), f32),
             pltpu.VMEM((conv_two.shape[0], 128), f32),
             pltpu.VMEM((8, width), f32),
             pltpu.VMEM((2, 8, width), f32),
             pltpu.VMEM((2, 8, 8, width), f32),
             pltpu.VMEM((2, 4, 8, width), f32),
-            dma((3,)),
-            dma((2, 7)),
-            dma((2, 7)),
-            dma((2, 3)),
-            dma((2, 3)),
+            pltpu.VMEM((TAIL + 8, width), f32),
+            pltpu.VMEM((8, TAIL + 8, width), f32),
+            pltpu.VMEM((4, TAIL + 8, width), f32),
+            pltpu.VMEM((edges[2], width), low),
+            pltpu.VMEM((4, 2, 2, OWN, width), low),
+            pltpu.VMEM((4, 2, HALF, width), low),
+            pltpu.VMEM((4, 2, HALF, width), low),
+            pltpu.VMEM((4, OWN, width), low),
+            pltpu.VMEM((4, OWN, width), low),
+            pltpu.VMEM((TAIL, width), f32),
+            pltpu.VMEM((OWN + TAIL, width), f32),
+            pltpu.VMEM((OWN + TAIL, width), f32),
+            pltpu.VMEM((4 * (OWN + TAIL), 128), f32),
+            pltpu.VMEM((4 * (OWN + TAIL), 128), f32),
+            pltpu.VMEM((4 * OWN, 128), low),
+            pltpu.VMEM((4 * TAIL, 128), low),
+            dma((5,)),
+            dma((3, 10)),
+            dma((3, 10)),
+            dma((4, 4)),
+            dma((4, 4)),
+            dma((4, 4)),
+            dma((4, 4)),
+            dma((4,)),
+            dma((4,)),
+            dma((2,)),
+            dma((11, 4)),
+            dma((11, 4)),
+            dma((2,)),
         ],
         compiler_params=pltpu.CompilerParams(
-            collective_id=1, has_side_effects=True, vmem_limit_bytes=60 * 1024 * 1024
+            collective_id=1, has_side_effects=True, vmem_limit_bytes=63 * 1024 * 1024
         ),
-        name="worker",
-    )(xs, conv_one, conv_two, shortcut, classifier, norm_params, valid, labels, rows, cols, moment)
+        name="step",
+    )(xs, conv_one, conv_two, shortcut, head, norm_params, valid, labels, rows, cols, moment)
 
 
 def scale_for(weight):
@@ -1225,51 +1272,31 @@
     bn_moment,
 ):
     slots, height, _, in_width = images.shape
-    width = conv_one.shape[1]
     side = height // 2
     xs = images.reshape(slots, side, 2, side, 2, in_width).transpose(4, 3, 2, 1, 0, 5)
-    votes, tail_vote, scales, valid_count, rows_new, cols_new, moment_new = run_worker(
+    new_mine, vote_mine, copies, rows_new, cols_new, moment_new, loss_sum, valid_count = run_step(
         xs,
         conv_one,
         conv_two,
         shortcut,
-        classifier,
+        classifier.T,
         norm_params,
         valid_slot.reshape(1, -1),
         labels.reshape(1, -1),
-        row_state.reshape(-1, 128),
+        row_state,
         col_state,
         bn_moment,
     )
-    tail_sum = sum_all(tail_vote, 3)
-    classes = classifier.shape[1]
-    head_sum = tail_sum[:classes].T.reshape(classes, width)
-    flat_sum = jnp.concatenate([head_sum, tail_sum[classes:TAIL]])
-    tail_weight = jnp.concatenate([classifier.reshape(classes, width), norm_params])
-    tail_scale = jnp.concatenate(
-        [
-            jnp.broadcast_to(scales[3], (classes, width)),
-            jnp.broadcast_to(scales[4], (TAIL - classes, width)),
-        ]
-    )
-    new_mine, vote_mine, copies = update_weights(
-        votes.reshape(4, 2, 2, 2, OWN, width),
-        flat_sum,
-        tail_weight,
-        tail_scale,
-        scales[:3, 0],
-        conv_one,
-        conv_two,
-        shortcut,
-        lax.axis_size("dp"),
+    copies, new_mine, vote_mine, rows_new, cols_new, moment_new, loss_sum, valid_count = finish(
+        (copies, new_mine, vote_mine, rows_new, cols_new, moment_new, loss_sum, valid_count)
     )
     return (
-        tail_sum[TAIL, 0],
-        valid_count[0, 0],
+        loss_sum.reshape(()),
+        valid_count.reshape(()),
         new_mine.reshape(-1),
         copies.reshape(-1),
         vote_mine.reshape(-1),
-        rows_new.reshape(1, -1),
+        rows_new,
         cols_new,
         moment_new,
     )

time: 196 us -> 427 us (2.18)
  the two profiles are of different devices: /device:TPU:0 before, /device:TPU:27 now
where the time goes in v3:
time: 427 us
  Pallas kernels  422 us (99%)
    pallas_call x1, Pallas kernels, finish(): pl.pallas_call(functools.partial(finish_kernel, count, chunks), out_shape...  254 us
    pallas_call x1, Pallas kernels, run_step(): pl.pallas_call(functools.partial(step_kernel, tuple(edges), 1.0 / math.sq...  168 us

profile of v3, /device:TPU:27, one launch (start us, length us, event | category | flops | bytes accessed | tf_op | source)
XLA Modules:
  0.0 427.1 jit_solution(8679703107074090617)
XLA Ops:
  0.6 2.8 copy.19
  3.4 1.5 copy.22
  4.9 167.6 %step.1 = (f32[898,128]{1,0:T(8,128)}, f32[898,128]{1,0:T(8,128)}, bf16[28736,128]{1,0:T(8,128)(2,1)}, f32[1,7680]{1,0:T(1,128)}, f32[1,1546]{1,0:T(1,128)}, /*i...) custom-call(bf16[2,4,2,4,64,256]{5,4,3,2,1,0:T(8,128)(2,1)} %bitcast.12, f32[2304,512]{1,0:T(8,128)} %one_hbm.1, ...), custom_call_target="tpu_custom_call" | custom-call | tf_op jit(solution)/shard_map/step/pallas_call | solution.py:1059
  172.4 254.5 %finish.1 = (bf16[28736,128]{1,0:T(8,128)(2,1)}, f32[898,128]{1,0:T(8,128)}, f32[898,128]{1,0:T(8,128)}, f32[1,7680]{1,0:T(1,128)}, f32[1,1546]{1,0:T(1,128)}, /...) custom-call(bf16[28736,128]{1,0:T(8,128)(2,1)} %get-tuple-element.24.refs_0_, ...), custom_call_target="tpu_custom_call" | custom-call | tf_op jit(solution)/shard_map/finish/pallas_call | solution.py:1034

commit v4 on v3

--- a/solution.py
+++ b/solution.py
@@ -17,9 +17,11 @@
 FORWARD_DIMS = ("NHWC", "HWIO", "NHWC")
 WEIGHT_DIMS = ("CHWN", "IHWO", "HWNC")
 OWN = 224
-HALF = 112
 TAIL = 16
 PIECE = 32
+SPAN = 4 * OWN
+HALF = SPAN // 2
+GROUP = 64
 
 
 def conv_apply(maps, kernel, stride, margin):
@@ -254,7 +256,10 @@
             factor = level[here, :]
             factor = jnp.concatenate([factor] * quarters, axis=1)
             vote = jnp.tanh(grad[here, :] * factor * scale)
-            votes[pl.ds(vote_at + start + 16 * m, 16), :] = vote.astype(jnp.bfloat16)
+            vote = vote.astype(jnp.bfloat16)
+            at = pl.multiple_of((vote_at + start) * 4 + GROUP * m, GROUP)
+            for q in range(quarters):
+                votes[pl.ds(at + 16 * q, 16), :] = vote[:, 128 * q : 128 * (q + 1)]
         return 0
 
     lax.fori_loop(0, rows // step, third, 0)
@@ -264,7 +269,7 @@
 def step_kernel(
     edges,
     root,
-    xs,
+    images,
     one_hbm,
     two_hbm,
     short_hbm,
@@ -283,6 +288,7 @@
     moment_new,
     loss_ref,
     count_ref,
+    xs,
     grad_one,
     grad_two,
     grad_short,
@@ -307,7 +313,6 @@
     tail_post,
     tail_plane,
     tail_line,
-    votes,
     core_in,
     ax_in,
     by_in,
@@ -318,8 +323,6 @@
     weight,
     vote_flat,
     new_flat,
-    mine,
-    tail_low,
     fetch_sem,
     small_send,
     small_recv,
@@ -332,7 +335,7 @@
     halo_sem,
     ag_send,
     ag_recv,
-    keep_sem,
+    free_sem,
 ):
     slots, in_width = xs.shape[4:]
     width = main_pre.shape[1]
@@ -385,6 +388,15 @@
     for k in range(OWN // PIECE):
         fetch_rows(first_row + k * PIECE, PIECE, k * PIECE, fetch_sem.at[3])
     fetch_rows(first_row + OWN, TAIL, OWN, fetch_sem.at[4])
+
+    lines = images.shape[0]
+    for half in range(2):
+        lanes = slice(128 * half, 128 * (half + 1))
+        level[:lines, :] = images[:, lanes].astype(f32)
+        for h in range(2 * side):
+            for w in range(2 * side):
+                rows = level[pl.ds(2 * side * h + w, slots, stride=4 * pixel_count), :]
+                xs[w % 2, w // 2, h % 2, h // 2, :, lanes] = rows.astype(low)
 
     scales = {}
 
@@ -436,12 +448,12 @@
 
     def block_rows(t, yy, xx, cc):
         block = t * 8 + yy * 4 + xx * 2 + cc
-        return pl.ds(pl.multiple_of(block * OWN, 16), OWN)
+        return pl.ds(pl.multiple_of(block * SPAN, 16), SPAN)
 
     def scatter_start(t):
         return [
             send(
-                votes.at[block_rows(t, yy, xx, 1 - core)],
+                out_ref.at[block_rows(t, yy, xx, 1 - core)],
                 core_in.at[t, yy, xx],
                 core_send.at[t, 2 * yy + xx],
                 core_recv.at[t, 2 * yy + xx],
@@ -456,7 +468,10 @@
             copy.wait()
         for yy in range(2):
             for xx in range(2):
-                core_in[t, yy, xx] = core_in[t, yy, xx] + votes[block_rows(t, yy, xx, core), :]
+                core_in[t, yy, xx] = core_in[t, yy, xx] + out_ref[block_rows(t, yy, xx, core), :]
+        pl.semaphore_signal(
+            free_sem.at[t], inc=1, device_id=(flip_core,), device_id_type=MESH
+        )
         return (
             send(
                 core_in.at[t, :, 1 - x, pl.ds(0, HALF)],
@@ -519,23 +534,24 @@
         def _():
             line_in[t] = plane_in[t]
 
-    span, part = 4 * OWN, 4 * HALF
-    own_rows = pl.ds(pl.multiple_of(me * span, 16), span)
-
-    def flat_rows(row, values, ref):
-        for k in range(4):
-            ref[pl.ds(row * 4 + k, 8, stride=4), :] = values[:, 128 * k : 128 * (k + 1)]
+    own_rows = pl.ds(pl.multiple_of(me * SPAN, 16), SPAN)
+
+    def flat_rows(row, q, values, ref):
+        ref[pl.ds(row * 4 + q, 8, stride=4), :] = values
 
     def renew(row, at_row):
         scale = scale_of(at_row, [scales[k] for k in range(3)], edges)
-        summed = total[pl.ds(row, 8), :]
-        fresh = weight[pl.ds(row, 8), :] - scale * jnp.tanh(summed * root)
-        flat_rows(row, summed, vote_flat)
-        flat_rows(row, fresh, new_flat)
+        for u in (0, 8):
+            for q in range(4):
+                summed = total[pl.ds(row * 4 + 16 * q + u, 8), :]
+                old = weight[pl.ds(row + u, 8), 128 * q : 128 * (q + 1)]
+                fresh = old - scale * jnp.tanh(summed * root)
+                flat_rows(row + u, q, summed, vote_flat)
+                flat_rows(row + u, q, fresh, new_flat)
 
     def halo_copy():
         return pltpu.make_async_remote_copy(
-            src_ref=total.at[pl.ds(0, TAIL)],
+            src_ref=total.at[pl.ds(0, GROUP)],
             dst_ref=halo_in,
             send_sem=halo_sem.at[0],
             recv_sem=halo_sem.at[1],
@@ -543,12 +559,9 @@
             device_id_type=MESH,
         )
 
-    def keep_copy():
-        return pltpu.make_async_copy(mine, out_ref.at[own_rows], keep_sem.at[0])
-
     def spread_copy(k):
         return pltpu.make_async_remote_copy(
-            src_ref=mine,
+            src_ref=out_ref.at[own_rows],
             dst_ref=out_ref.at[own_rows],
             send_sem=ag_send.at[0, k],
             recv_sem=ag_recv.at[0, z],
@@ -559,7 +572,7 @@
     def own_block():
         for k in range(1, 4):
             line_copy(0, lax.rem(z + k, 4)).wait_recv()
-        total[pl.ds(0, OWN), :] = functools.reduce(
+        total[pl.ds(0, SPAN), :] = functools.reduce(
             lambda a, b: a + b, [line_in[t].astype(f32) for t in range(4)]
         )
         halo_copy().start()
@@ -567,13 +580,12 @@
             weight.at[pl.ds(0, OWN)], weight.at[pl.ds(0, OWN)], fetch_sem.at[3]
         ).wait()
 
-        @pl.loop(0, OWN // 8)
+        @pl.loop(0, OWN // 16)
         def _(k):
-            row = pl.multiple_of(k * 8, 8)
+            row = pl.multiple_of(k * 16, 16)
             renew(row, first_row + row)
 
-        mine[...] = new_flat[pl.ds(0, span), :].astype(low)
-        keep_copy().start()
+        out_ref[own_rows, :] = new_flat[pl.ds(0, SPAN), :].astype(low)
         for k in range(3):
             spread_copy(k).start()
 
@@ -584,17 +596,13 @@
 
     def half_rows(t, yy, xx, half):
         block = t * 8 + yy * 4 + xx * 2 + core
-        return pl.ds(pl.multiple_of(block * span + half * part, 16), part)
+        return pl.ds(pl.multiple_of(block * SPAN + half * HALF, 16), HALF)
 
     def gather_one(t):
-        @pl.when(z == t)
-        def _():
-            keep_copy().wait()
-
         @pl.when(z != t)
         def _():
             pltpu.make_async_remote_copy(
-                src_ref=mine,
+                src_ref=out_ref.at[own_rows],
                 dst_ref=out_ref.at[own_rows],
                 send_sem=ag_send.at[0, 0],
                 recv_sem=ag_recv.at[0, t],
@@ -616,11 +624,12 @@
     def gather_three(t, copies):
         for copy in copies:
             copy.wait()
+        pl.semaphore_wait(free_sem.at[t], 1)
         sent = []
         for yy in range(2):
             for xx in range(2):
                 block = t * 8 + yy * 4 + xx * 2 + core
-                rows = pl.ds(pl.multiple_of(block * span, 16), span)
+                rows = pl.ds(pl.multiple_of(block * SPAN, 16), SPAN)
                 sent.append(piece(rows, 7 + 2 * yy + xx, t, flip_core))
         return sent
 
@@ -807,7 +816,7 @@
         here = pl.ds(k * width, width)
         start = edges[k - 1] if k else 0
         col_new[:, here] = factored_votes(
-            grad, grad.shape[0], start, row_ref, row_new, col_ref[:, here], level, votes, start, between
+            grad, grad.shape[0], start, row_ref, row_new, col_ref[:, here], level, out_ref, start, between
         )
 
     matrix_votes(2, grad_short, (nothing, nothing))
@@ -969,27 +978,25 @@
         pltpu.make_async_copy(
             weight.at[pl.ds(OWN, TAIL)], weight.at[pl.ds(OWN, TAIL)], fetch_sem.at[4]
         ).wait()
-        total[pl.ds(OWN, TAIL), :] = halo_in[...]
-        for k in range(TAIL // 8):
-            renew(OWN + 8 * k, first_row + OWN + 8 * k)
+        total[pl.ds(SPAN, GROUP), :] = halo_in[...]
+        renew(OWN, first_row + OWN)
+
+    def tail_rows(values, ref):
+        for u in (0, 8):
+            for q in range(4):
+                flat_rows(OWN + u, q, values[u : u + 8, 128 * q : 128 * (q + 1)], ref)
 
     @pl.when(me == 31)
     def _():
-        for k in range(TAIL // 8):
-            flat_rows(OWN + 8 * k, flat_sums[8 * k : 8 * k + 8], vote_flat)
-            flat_rows(OWN + 8 * k, flat_new[8 * k : 8 * k + 8], new_flat)
+        tail_rows(flat_sums, vote_flat)
+        tail_rows(flat_new, new_flat)
 
     shift = 2 * me
     share = vote_ref.shape[0]
     vote_ref[...] = vote_flat[pl.ds(shift, share), :]
     new_ref[...] = new_flat[pl.ds(shift, share), :]
-    for k in range(TAIL // 8):
-        flat_rows(OWN + 8 * k, flat_new[8 * k : 8 * k + 8], new_flat)
-    tail_low[...] = new_flat[pl.ds(span, 4 * TAIL), :].astype(low)
-    keep_tail = pltpu.make_async_copy(
-        tail_low, out_ref.at[pl.ds(32 * span, 4 * TAIL)], keep_sem.at[1]
-    )
-    keep_tail.start()
+    tail_rows(flat_new, new_flat)
+    out_ref[pl.ds(32 * SPAN, GROUP), :] = new_flat[pl.ds(SPAN, GROUP), :].astype(low)
 
     for t in (1, 0):
         gathered[t] = gather_three(t, gathered[t])
@@ -1003,54 +1010,42 @@
 
     for k in range(3):
         spread_copy(k).wait_send()
-    keep_tail.wait()
-
-
-def finish_kernel(count, chunks, *refs):
-    sources, targets, sem = refs[:count], refs[count : 2 * count], refs[2 * count]
-    copies = []
-    rows = sources[0].shape[0]
-    step = -(-rows // chunks // 16) * 16
-    for k in range(chunks):
-        here = pl.ds(k * step, min(step, rows - k * step))
-        copies.append(
-            pltpu.make_async_copy(sources[0].at[here], targets[0].at[here], sem.at[k])
-        )
-    for k in (1, 2):
-        copies.append(pltpu.make_async_copy(sources[k], targets[k], sem.at[chunks + k]))
+
+
+def finish_kernel(count, *refs):
+    copies = [
+        pltpu.make_async_copy(refs[k], refs[count + k], refs[2 * count].at[k])
+        for k in range(count)
+    ]
     for copy in copies:
         copy.start()
-    for k in range(3, count):
-        targets[k][...] = sources[k][...]
     for copy in copies:
         copy.wait()
 
 
 def finish(values):
-    vmem = pl.BlockSpec(memory_space=pltpu.VMEM)
-    hbm = pl.BlockSpec(memory_space=pl.ANY)
-    count, chunks = len(values), 8
-    specs = [hbm] * 3 + [vmem] * (count - 3)
+    count = len(values)
+    specs = [pl.BlockSpec(memory_space=pl.ANY)] * count
     return pl.pallas_call(
-        functools.partial(finish_kernel, count, chunks),
+        functools.partial(finish_kernel, count),
         out_shape=[jax.ShapeDtypeStruct(value.shape, value.dtype) for value in values],
         in_specs=specs,
         out_specs=specs,
-        scratch_shapes=[pltpu.SemaphoreType.DMA((chunks + 3,))],
+        scratch_shapes=[pltpu.SemaphoreType.DMA((count,))],
         name="finish",
     )(*values)
 
 
-def run_step(xs, conv_one, conv_two, shortcut, head, norm_params, valid, labels, rows, cols, moment):
+def run_step(images, conv_one, conv_two, shortcut, head, norm_params, valid, labels, rows, cols, moment):
     vmem = pl.BlockSpec(memory_space=pltpu.VMEM)
     hbm = pl.BlockSpec(memory_space=pl.ANY)
     low, f32 = jnp.bfloat16, jnp.float32
     dma = pltpu.SemaphoreType.DMA
     workers = lax.axis_size("dp")
-    slots, in_width = xs.shape[4:]
+    slots, in_width = valid.shape[1], images.shape[1]
     width = conv_one.shape[1]
-    pixels = 16 * slots
-    shape = jax.ShapeDtypeStruct
+    pixels = images.shape[0] // 4
+    shape = pltpu.VMEM
     edges = [conv_one.shape[0]]
     edges.append(edges[0] + conv_two.shape[0])
     edges.append(edges[1] + shortcut.shape[0])
@@ -1069,8 +1064,9 @@
             shape((1, 1), f32),
         ),
         in_specs=[vmem] + [hbm] * 3 + [vmem] * 7,
-        out_specs=(vmem, vmem, hbm) + (vmem,) * 5,
+        out_specs=(vmem,) * 8,
         scratch_shapes=[
+            pltpu.VMEM((2, 4, 2, 4, slots, in_width), low),
             pltpu.VMEM(conv_one.shape, f32),
             pltpu.VMEM(conv_two.shape, f32),
             pltpu.VMEM(shortcut.shape, f32),
@@ -1095,19 +1091,16 @@
             pltpu.VMEM((TAIL + 8, width), f32),
             pltpu.VMEM((8, TAIL + 8, width), f32),
             pltpu.VMEM((4, TAIL + 8, width), f32),
-            pltpu.VMEM((edges[2], width), low),
-            pltpu.VMEM((4, 2, 2, OWN, width), low),
-            pltpu.VMEM((4, 2, HALF, width), low),
-            pltpu.VMEM((4, 2, HALF, width), low),
-            pltpu.VMEM((4, OWN, width), low),
-            pltpu.VMEM((4, OWN, width), low),
-            pltpu.VMEM((TAIL, width), f32),
+            pltpu.VMEM((4, 2, 2, SPAN, 128), low),
+            pltpu.VMEM((4, 2, HALF, 128), low),
+            pltpu.VMEM((4, 2, HALF, 128), low),
+            pltpu.VMEM((4, SPAN, 128), low),
+            pltpu.VMEM((4, SPAN, 128), low),
+            pltpu.VMEM((GROUP, 128), f32),
+            pltpu.VMEM((SPAN + GROUP, 128), f32),
             pltpu.VMEM((OWN + TAIL, width), f32),
-            pltpu.VMEM((OWN + TAIL, width), f32),
-            pltpu.VMEM((4 * (OWN + TAIL), 128), f32),
-            pltpu.VMEM((4 * (OWN + TAIL), 128), f32),
-            pltpu.VMEM((4 * OWN, 128), low),
-            pltpu.VMEM((4 * TAIL, 128), low),
+            pltpu.VMEM((SPAN + GROUP, 128), f32),
+            pltpu.VMEM((SPAN + GROUP, 128), f32),
             dma((5,)),
             dma((3, 10)),
             dma((3, 10)),
@@ -1120,13 +1113,13 @@
             dma((2,)),
             dma((11, 4)),
             dma((11, 4)),
-            dma((2,)),
+            pltpu.SemaphoreType.REGULAR((4,)),
         ],
         compiler_params=pltpu.CompilerParams(
-            collective_id=1, has_side_effects=True, vmem_limit_bytes=63 * 1024 * 1024
+            collective_id=1, has_side_effects=True, vmem_limit_bytes=54 * 1024 * 1024
         ),
         name="step",
-    )(xs, conv_one, conv_two, shortcut, head, norm_params, valid, labels, rows, cols, moment)
+    )(images, conv_one, conv_two, shortcut, head, norm_params, valid, labels, rows, cols, moment)
 
 
 def scale_for(weight):
@@ -1271,11 +1264,8 @@
     col_state,
     bn_moment,
 ):
-    slots, height, _, in_width = images.shape
-    side = height // 2
-    xs = images.reshape(slots, side, 2, side, 2, in_width).transpose(4, 3, 2, 1, 0, 5)
     new_mine, vote_mine, copies, rows_new, cols_new, moment_new, loss_sum, valid_count = run_step(
-        xs,
+        images.reshape(-1, images.shape[-1]),
         conv_one,
         conv_two,
         shortcut,

time: 427 us -> 430 us (level)
  the two profiles are of different devices: /device:TPU:27 before, /device:TPU:0 now
where the time goes in v4:
time: 430 us; the launch traced here: 421 us
  Pallas kernels  414 us (96%)
  local copies, waits for them, and re-layouts  6.32 us (1%)
    pallas_call x1, Pallas kernels, finish(): pl.pallas_call(functools.partial(finish_kernel, count), out_shape=[jax.Sh...  255 us
    pallas_call x1, Pallas kernels, run_step(): pl.pallas_call(functools.partial(step_kernel, tuple(edges), 1.0 / math.sq...  159 us

profile of v4, /device:TPU:0, one launch (start us, length us, event | category | flops | bytes accessed | tf_op | source)
XLA Modules:
  0.0 421.2 jit_solution(2550184260764877857)
XLA Ops:
  0.6 159.3 %step.1 = (f32[898,128]{1,0:T(8,128)S(1)}, f32[898,128]{1,0:T(8,128)S(1)}, bf16[28736,128]{1,0:T(8,128)(2,1)S(1)}, f32[1,7680]{1,0:T(1,128)S(1)}, f32[1,1546]{1,...) custom-call(bf16[4096,256]{1,0:T(8,128)(2,1)} %bitcast.9, f32[2304,512]{1,0:T(8,128)} %one_hbm.1, ...), custom_call_target="tpu_custom_call" | custom-call | tf_op jit(solution)/shard_map/step/pallas_call | solution.py:1054
  160.0 0.0 copy-start
  160.0 2.9 copy-done
  162.9 0.0 copy-start.1
  162.9 0.8 copy-done.1
  163.7 0.0 copy-start.2
  163.7 0.8 copy-done.2
  164.5 0.0 copy-start.3
  164.5 0.6 copy-done.3
  165.1 0.0 copy-start.5
  165.1 0.6 copy-done.5
  165.7 0.0 copy-start.4
  165.7 0.6 copy-done.4
  166.3 254.7 %finish.1 = (bf16[28736,128]{1,0:T(8,128)(2,1)}, f32[898,128]{1,0:T(8,128)}, f32[898,128]{1,0:T(8,128)}, f32[1,7680]{1,0:T(1,128)}, f32[1,1546]{1,0:T(1,128)}, /...) custom-call(bf16[28736,128]{1,0:T(8,128)(2,1)} %copy-done, f32[898,128]{1,0:T(8,128)} %copy-done.1, ...), custom_call_target="tpu_custom_call" | custom-call | tf_op jit(solution)/shard_map/finish/pallas_call | solution.py:1029
Async XLA Ops:
  160.0 2.9 copy-start
  162.9 0.8 copy-start.1
  163.7 0.8 copy-start.2
  164.5 0.6 copy-start.3
  165.1 0.6 copy-start.5
  165.7 0.6 copy-start.4

commit v5 on v4

--- a/solution.py
+++ b/solution.py
@@ -144,6 +144,23 @@
     return jnp.where(row < edges[0], scales[0], picked)
 
 
+def make_units(edges):
+    one, two, short = edges[0] // 16, edges[1] // 16, edges[2] // 16
+    units = []
+    at = one
+    for size, x_first in ((2, True), (2, False), (2, True), (3, False)):
+        units.append((at, size, x_first, 16 * size, (1, 1)))
+        at += 32 * size
+    assert at == two
+    at = 0
+    for size, x_first in ((2, True), (2, False)):
+        units.append((at, size, x_first, 16 * size, (0, 0)))
+        at += 32 * size
+    assert one - at == 16 and short - two == 16
+    units.append((at, 1, True, two - at, (0, 2)))
+    return units
+
+
 def settle_rows(sums, pixels, gain, shift):
     mean = sums[0] / pixels
     inv = lax.rsqrt(sums[1] / pixels - mean * mean + EPS_NORM)
@@ -268,6 +285,7 @@
 
 def step_kernel(
     edges,
+    units,
     root,
     images,
     one_hbm,
@@ -314,28 +332,31 @@
     tail_plane,
     tail_line,
     core_in,
-    ax_in,
-    by_in,
-    plane_in,
+    wide_in,
+    deep_in,
     line_in,
-    halo_in,
+    sum_low,
+    landed,
     total,
+    own_weight,
     weight,
     vote_flat,
     new_flat,
     fetch_sem,
     small_send,
     small_recv,
-    core_send,
-    core_recv,
     rs_send,
     rs_recv,
     line_send,
     line_recv,
-    halo_sem,
+    pass_send,
+    land_recv,
+    spread_send,
+    spread_recv,
     ag_send,
     ag_recv,
     free_sem,
+    load_sem,
 ):
     slots, in_width = xs.shape[4:]
     width = main_pre.shape[1]
@@ -354,8 +375,18 @@
     spot = lax.rem(me, 8)
     near = [z * 8 + lax.rem(spot + k, 8) for k in range(1, 8)]
     far = [lax.rem(z + k, 4) * 8 + spot for k in range(1, 4)]
-    ahead, behind = lax.rem(me + 31, 32), lax.rem(me + 1, 32)
-    partners = near + far + [ahead, behind]
+    others = [lax.rem(me + k, 32) for k in range(1, 32)]
+
+    count = images.shape[0]
+    loads = []
+    for half in range(2):
+        lanes = slice(128 * half, 128 * (half + 1))
+        loads.append(
+            pltpu.make_async_copy(
+                images.at[:, lanes], core_in.at[pl.ds(half * count, count)], load_sem.at[half]
+            )
+        )
+        loads[half].start()
 
     fetches = [
         pltpu.make_async_copy(source, target, fetch_sem.at[k])
@@ -366,7 +397,7 @@
     for fetch in fetches:
         fetch.start()
     barrier = pltpu.get_barrier_semaphore()
-    for partner in partners:
+    for partner in others:
         pl.semaphore_signal(barrier, inc=1, device_id=(partner,), device_id_type=MESH)
 
     def fetch_rows(row, count, place_at, sem):
@@ -389,10 +420,10 @@
         fetch_rows(first_row + k * PIECE, PIECE, k * PIECE, fetch_sem.at[3])
     fetch_rows(first_row + OWN, TAIL, OWN, fetch_sem.at[4])
 
-    lines = images.shape[0]
     for half in range(2):
         lanes = slice(128 * half, 128 * (half + 1))
-        level[:lines, :] = images[:, lanes].astype(f32)
+        loads[half].wait()
+        level[:count, :] = core_in[pl.ds(half * count, count), :].astype(f32)
         for h in range(2 * side):
             for w in range(2 * side):
                 rows = level[pl.ds(2 * side * h + w, slots, stride=4 * pixel_count), :]
@@ -446,192 +477,234 @@
             copy.wait()
         return (line_ref[0] + line_ref[1]) + (line_ref[2] + line_ref[3])
 
-    def block_rows(t, yy, xx, cc):
-        block = t * 8 + yy * 4 + xx * 2 + cc
-        return pl.ds(pl.multiple_of(block * SPAN, 16), SPAN)
-
-    def scatter_start(t):
-        return [
-            send(
-                out_ref.at[block_rows(t, yy, xx, 1 - core)],
-                core_in.at[t, yy, xx],
-                core_send.at[t, 2 * yy + xx],
-                core_recv.at[t, 2 * yy + xx],
-                flip_core,
-            )
-            for yy in range(2)
-            for xx in range(2)
-        ]
-
-    def scatter_one(t, copies):
-        for copy in copies:
-            copy.wait()
-        for yy in range(2):
-            for xx in range(2):
-                core_in[t, yy, xx] = core_in[t, yy, xx] + out_ref[block_rows(t, yy, xx, core), :]
+    def lines(start, count):
+        return pl.ds(pl.multiple_of(start, 16), count)
+
+    sizes = [GROUP * unit[1] for unit in units]
+    starts = [sum(sizes[:k]) for k in range(len(units) + 1)]
+
+    def part_of(ref, u, share, start, count):
+        return ref.at[lines(share * starts[u] + start, count)]
+
+    def places(u):
+        if units[u][2]:
+            return x, y, flip_x, flip_y
+        return y, x, flip_y, flip_x
+
+    def unit_start(u, cc):
+        return GROUP * units[u][0] + cc * (GROUP * units[u][3])
+
+    def own_group(u):
+        first, second, _, _ = places(u)
+        return units[u][0] + core * units[u][3] + (first * 8 + second * 4 + z) * units[u][1]
+
+    def halve(source, target, u, stage, partner):
+        return send(source, target, rs_send.at[u, stage], rs_recv.at[u, stage], partner)
+
+    def scatter_start(u):
+        size = 16 * sizes[u]
+        return halve(
+            out_ref.at[lines(unit_start(u, 1 - core), size)],
+            part_of(core_in, u, 16, 0, size),
+            u,
+            0,
+            flip_core,
+        )
+
+    def add_to(ref, u, share, source_ref, source_start):
+        size = share * sizes[u]
+        here = lines(share * starts[u], size)
+        ref[here, :] = ref[here, :] + source_ref[lines(source_start, size), :]
+
+    def scatter_one(u, copy):
+        copy.wait()
+        add_to(core_in, u, 16, out_ref, unit_start(u, core))
         pl.semaphore_signal(
-            free_sem.at[t], inc=1, device_id=(flip_core,), device_id_type=MESH
-        )
-        return (
-            send(
-                core_in.at[t, :, 1 - x, pl.ds(0, HALF)],
-                ax_in.at[t],
-                rs_send.at[0, t],
-                rs_recv.at[0, t],
-                flip_x,
-            ),
-            send(
-                core_in.at[t, 1 - y, :, pl.ds(HALF, HALF)],
-                by_in.at[t],
-                rs_send.at[1, t],
-                rs_recv.at[1, t],
-                flip_y,
-            ),
-        )
-
-    def scatter_two(t, copies):
-        copies[0].wait()
-        ax_in[t] = ax_in[t] + core_in[t, :, x, :HALF]
-        first = send(
-            ax_in.at[t, 1 - y],
-            plane_in.at[t, pl.ds(0, HALF)],
-            rs_send.at[2, t],
-            rs_recv.at[2, t],
-            flip_y,
-        )
-        copies[1].wait()
-        by_in[t] = by_in[t] + core_in[t, y, :, HALF:]
-        second = send(
-            by_in.at[t, 1 - x],
-            plane_in.at[t, pl.ds(HALF, HALF)],
-            rs_send.at[3, t],
-            rs_recv.at[3, t],
-            flip_x,
-        )
-        return first, second
-
-    def line_copy(t, slot):
+            free_sem.at[u], inc=1, device_id=(flip_core,), device_id_type=MESH
+        )
+        first, _, flip_first, _ = places(u)
+        size = 8 * sizes[u]
+        return halve(
+            part_of(core_in, u, 16, (1 - first) * size, size),
+            part_of(wide_in, u, 8, 0, size),
+            u,
+            1,
+            flip_first,
+        )
+
+    def scatter_two(u, copy):
+        copy.wait()
+        first, second, _, flip_second = places(u)
+        add_to(wide_in, u, 8, core_in, 16 * starts[u] + first * 8 * sizes[u])
+        size = 4 * sizes[u]
+        return halve(
+            part_of(wide_in, u, 8, (1 - second) * size, size),
+            part_of(deep_in, u, 4, 0, size),
+            u,
+            2,
+            flip_second,
+        )
+
+    def line_copy(u, k):
+        plane_to = lax.rem(z + k, 4)
         return pltpu.make_async_remote_copy(
-            src_ref=plane_in.at[t],
-            dst_ref=line_in.at[slot],
-            send_sem=line_send.at[t],
-            recv_sem=line_recv.at[slot],
-            device_id=(t * 8 + spot,),
+            src_ref=part_of(deep_in, u, 4, plane_to * sizes[u], sizes[u]),
+            dst_ref=part_of(line_in, u, 4, z * sizes[u], sizes[u]),
+            send_sem=line_send.at[u, k],
+            recv_sem=line_recv.at[u, k],
+            device_id=(plane_to * 8 + spot,),
             device_id_type=MESH,
         )
 
-    def scatter_three(t, copies):
-        copies[0].wait()
-        plane_in[t, :HALF] = plane_in[t, :HALF] + ax_in[t, y]
-        copies[1].wait()
-        plane_in[t, HALF:] = plane_in[t, HALF:] + by_in[t, x]
-
-        @pl.when(z != t)
-        def _():
-            line_copy(t, z).start()
-
-        @pl.when(z == t)
-        def _():
-            line_in[t] = plane_in[t]
-
-    own_rows = pl.ds(pl.multiple_of(me * SPAN, 16), SPAN)
+    def scatter_three(u, copy):
+        copy.wait()
+        _, second, _, _ = places(u)
+        add_to(deep_in, u, 4, wide_in, 8 * starts[u] + second * 4 * sizes[u])
+        for k in (3, 2, 1):
+            line_copy(u, k).start()
+        here = lines(4 * starts[u] + z * sizes[u], sizes[u])
+        line_in[here, :] = deep_in[here, :]
+
+    groups = (edges[2] + TAIL) // 16
+    spare = (groups - 1) // 32
+    passes = []
+
+    def land(local, group, to, slot, index):
+        source = sum_low.at[lines(local * GROUP, GROUP)]
+        target = landed.at[lines(slot * GROUP, GROUP)]
+        copy = pltpu.make_async_remote_copy(
+            src_ref=source,
+            dst_ref=target,
+            send_sem=pass_send.at[index],
+            recv_sem=land_recv.at[slot],
+            device_id=(to,),
+            device_id_type=MESH,
+        )
+        return copy, source, target
+
+    def pass_on(u):
+        for m in range(units[u][1]):
+            local = starts[u] // GROUP + m
+            group = own_group(u) + m
+            to, slot = lax.div(group, spare), lax.rem(group, spare)
+            for halo in range(2):
+                index = 2 * local + halo
+                if halo:
+                    receiver, at = lax.rem(to + 31, 32), spare
+                    wanted = jnp.logical_and(slot == 0, group > 0)
+                else:
+                    receiver, at, wanted = to, slot, group >= 0
+                away = jnp.logical_and(wanted, receiver != me)
+                here = jnp.logical_and(wanted, receiver == me)
+                copy, source, target = land(local, group, receiver, at, index)
+
+                @pl.when(away)
+                def _():
+                    copy.start()
+
+                @pl.when(here)
+                def _():
+                    target[...] = source[...]
+
+                passes.append((away, copy))
 
     def flat_rows(row, q, values, ref):
         ref[pl.ds(row * 4 + q, 8, stride=4), :] = values
 
+    def old_rows(u, cc):
+        matrix = units[u][4][cc]
+        base = edges[matrix - 1] if matrix else 0
+        return (one_hbm, two_hbm, short_hbm)[matrix], 16 * own_group(u) - base, 16 * units[u][1]
+
+    def own_fetch(u):
+        target = own_weight.at[pl.ds(starts[u] // 4, 16 * units[u][1])]
+        matrices = units[u][4]
+        for cc in range(2):
+            if cc and matrices[0] == matrices[1]:
+                continue
+
+            @pl.when((core == cc) if matrices[0] != matrices[1] else (core >= 0))
+            def _():
+                ref, row, count = old_rows(u, cc)
+                pltpu.make_async_copy(
+                    ref.at[pl.ds(pl.multiple_of(row, 16), count)], target, fetch_sem.at[5 + u]
+                ).start()
+
+    for u in range(len(units)):
+        own_fetch(u)
+
+    def spread_copy(u, k):
+        own = out_ref.at[lines(own_group(u) * GROUP, sizes[u])]
+        return pltpu.make_async_remote_copy(
+            src_ref=own,
+            dst_ref=own,
+            send_sem=spread_send.at[u, k],
+            recv_sem=spread_recv.at[u, k],
+            device_id=(far[k - 1],),
+            device_id_type=MESH,
+        )
+
+    def own_block(u):
+        size = sizes[u]
+        for k in range(1, 4):
+            line_copy(u, k).wait_recv()
+        here = pl.ds(starts[u], size)
+        low_sum = functools.reduce(
+            lambda a, b: a + b,
+            [line_in[pl.ds(4 * starts[u] + t * size, size), :].astype(f32) for t in range(4)],
+        ).astype(low)
+        sum_low[here, :] = low_sum
+        total[here, :] = low_sum.astype(f32)
+        target = own_weight.at[pl.ds(starts[u] // 4, 16 * units[u][1])]
+        pltpu.make_async_copy(target, target, fetch_sem.at[5 + u]).wait()
+        matrices = units[u][4]
+        scale = jnp.where(core == 0, scales[matrices[0]], scales[matrices[1]])
+        for m in range(units[u][1]):
+            row = starts[u] // 4 + 16 * m
+            for part in (0, 8):
+                for q in range(4):
+                    summed = total[pl.ds(row * 4 + 16 * q + part, 8), :]
+                    old = own_weight[pl.ds(row + part, 8), 128 * q : 128 * (q + 1)]
+                    fresh = old - scale * jnp.tanh(summed * root)
+                    flat_rows(row + part, q, fresh, new_flat)
+        out_ref[lines(own_group(u) * GROUP, size), :] = new_flat[here, :].astype(low)
+        for k in (3, 2, 1):
+            spread_copy(u, k).start()
+        pass_on(u)
+
+    def piece(rows, u, stage, partner):
+        return send(
+            out_ref.at[rows], out_ref.at[rows], ag_send.at[u, stage], ag_recv.at[u, stage], partner
+        )
+
+    def gather_one(u):
+        for k in range(1, 4):
+            spread_copy(u, k).wait_recv()
+        first, second, _, flip_second = places(u)
+        size = 4 * sizes[u]
+        start = unit_start(u, core) + (2 * first + second) * size
+        return piece(lines(start, size), u, 0, flip_second)
+
+    def gather_two(u, copy):
+        copy.wait()
+        first, _, flip_first, _ = places(u)
+        size = 8 * sizes[u]
+        return piece(lines(unit_start(u, core) + first * size, size), u, 1, flip_first)
+
+    def gather_three(u, copy):
+        copy.wait()
+        pl.semaphore_wait(free_sem.at[u], 1)
+        return piece(lines(unit_start(u, core), 16 * sizes[u]), u, 2, flip_core)
+
     def renew(row, at_row):
         scale = scale_of(at_row, [scales[k] for k in range(3)], edges)
-        for u in (0, 8):
+        for part in (0, 8):
             for q in range(4):
-                summed = total[pl.ds(row * 4 + 16 * q + u, 8), :]
-                old = weight[pl.ds(row + u, 8), 128 * q : 128 * (q + 1)]
+                summed = total[pl.ds(row * 4 + 16 * q + part, 8), :]
+                old = weight[pl.ds(row + part, 8), 128 * q : 128 * (q + 1)]
                 fresh = old - scale * jnp.tanh(summed * root)
-                flat_rows(row + u, q, summed, vote_flat)
-                flat_rows(row + u, q, fresh, new_flat)
-
-    def halo_copy():
-        return pltpu.make_async_remote_copy(
-            src_ref=total.at[pl.ds(0, GROUP)],
-            dst_ref=halo_in,
-            send_sem=halo_sem.at[0],
-            recv_sem=halo_sem.at[1],
-            device_id=(ahead,),
-            device_id_type=MESH,
-        )
-
-    def spread_copy(k):
-        return pltpu.make_async_remote_copy(
-            src_ref=out_ref.at[own_rows],
-            dst_ref=out_ref.at[own_rows],
-            send_sem=ag_send.at[0, k],
-            recv_sem=ag_recv.at[0, z],
-            device_id=(far[k],),
-            device_id_type=MESH,
-        )
-
-    def own_block():
-        for k in range(1, 4):
-            line_copy(0, lax.rem(z + k, 4)).wait_recv()
-        total[pl.ds(0, SPAN), :] = functools.reduce(
-            lambda a, b: a + b, [line_in[t].astype(f32) for t in range(4)]
-        )
-        halo_copy().start()
-        pltpu.make_async_copy(
-            weight.at[pl.ds(0, OWN)], weight.at[pl.ds(0, OWN)], fetch_sem.at[3]
-        ).wait()
-
-        @pl.loop(0, OWN // 16)
-        def _(k):
-            row = pl.multiple_of(k * 16, 16)
-            renew(row, first_row + row)
-
-        out_ref[own_rows, :] = new_flat[pl.ds(0, SPAN), :].astype(low)
-        for k in range(3):
-            spread_copy(k).start()
-
-    def piece(rows, kind, t, partner):
-        return send(
-            out_ref.at[rows], out_ref.at[rows], ag_send.at[kind, t], ag_recv.at[kind, t], partner
-        )
-
-    def half_rows(t, yy, xx, half):
-        block = t * 8 + yy * 4 + xx * 2 + core
-        return pl.ds(pl.multiple_of(block * SPAN + half * HALF, 16), HALF)
-
-    def gather_one(t):
-        @pl.when(z != t)
-        def _():
-            pltpu.make_async_remote_copy(
-                src_ref=out_ref.at[own_rows],
-                dst_ref=out_ref.at[own_rows],
-                send_sem=ag_send.at[0, 0],
-                recv_sem=ag_recv.at[0, t],
-                device_id=(far[0],),
-                device_id_type=MESH,
-            ).wait_recv()
-
-        return (
-            piece(half_rows(t, y, x, 0), 1, t, flip_y),
-            piece(half_rows(t, y, x, 1), 2, t, flip_x),
-        )
-
-    def gather_two(t, copies):
-        copies[0].wait()
-        sent = [piece(half_rows(t, yy, x, 0), 3 + yy, t, flip_x) for yy in range(2)]
-        copies[1].wait()
-        return sent + [piece(half_rows(t, y, xx, 1), 5 + xx, t, flip_y) for xx in range(2)]
-
-    def gather_three(t, copies):
-        for copy in copies:
-            copy.wait()
-        pl.semaphore_wait(free_sem.at[t], 1)
-        sent = []
-        for yy in range(2):
-            for xx in range(2):
-                block = t * 8 + yy * 4 + xx * 2 + core
-                rows = pl.ds(pl.multiple_of(block * SPAN, 16), SPAN)
-                sent.append(piece(rows, 7 + 2 * yy + xx, t, flip_core))
-        return sent
+                flat_rows(row + part, q, summed, vote_flat)
+                flat_rows(row + part, q, fresh, new_flat)
 
     valid_column = column_of(valid_ref[...].astype(f32), slots)
     weight_slot = jnp.broadcast_to(valid_column, (slots, width))
@@ -687,7 +760,7 @@
         side_sums = add_up(side_sums, moments(value))
 
     count = jnp.broadcast_to(jnp.sum(valid_column, axis=0, keepdims=True), (1, width))
-    pl.semaphore_wait(barrier, len(partners))
+    pl.semaphore_wait(barrier, len(others))
     copies = exchange_start(
         0, jnp.concatenate(main_sums + side_sums + [count, none, none, none], axis=0)
     )
@@ -821,7 +894,7 @@
 
     matrix_votes(2, grad_short, (nothing, nothing))
     matrix_votes(1, grad_two, (nothing, nothing))
-    stage = {t: scatter_start(t) for t in (2, 3)}
+    stage = {u: scatter_start(u) for u in range(4)}
 
     gain_one, shift_one = none, none
     for j in range(side):
@@ -848,8 +921,10 @@
         )
         back_one[j, :side] = (grad * slope_one).astype(low).reshape(side, slots, width)
         if j == 1:
+            stage[0] = scatter_one(0, stage[0])
+            stage[1] = scatter_one(1, stage[1])
+        if j == 2:
             stage[2] = scatter_one(2, stage[2])
-        if j == 2:
             stage[3] = scatter_one(3, stage[3])
 
     square_head = grad_head * grad_head + EPS_ROW
@@ -899,40 +974,50 @@
                 left, right.reshape(-1, width), preferred_element_type=f32
             )
         if b == 0:
-            stage[2] = scatter_two(2, stage[2])
+            stage[0] = scatter_two(0, stage[0])
+            stage[1] = scatter_two(1, stage[1])
         if b == 1:
             copies = exchange_middle(2, copies)
         if b == 2:
+            stage[2] = scatter_two(2, stage[2])
             stage[3] = scatter_two(3, stage[3])
 
-    matrix_votes(
-        0,
-        grad_one,
-        (lambda: scatter_three(2, stage[2]), lambda: scatter_three(3, stage[3])),
-    )
-    stage = {t: scatter_start(t) for t in (1, 0)}
-
-    @pl.when(z >= 2)
-    def _():
-        own_block()
-
+    def first_line():
+        scatter_three(0, stage[0])
+        scatter_three(1, stage[1])
+
+    def second_line():
+        scatter_three(2, stage[2])
+        scatter_three(3, stage[3])
+
+    matrix_votes(0, grad_one, (first_line, second_line))
+    last = (4, 5, 6)
+    stage = {u: scatter_start(u) for u in last}
     gathered = {}
-    for t in (1, 0):
-        stage[t] = scatter_one(t, stage[t])
-    for t in (2, 3):
-        gathered[t] = gather_one(t)
-    for t in (1, 0):
-        stage[t] = scatter_two(t, stage[t])
-    for t in (2, 3):
-        gathered[t] = gather_two(t, gathered[t])
-    for t in (1, 0):
-        scatter_three(t, stage[t])
-    for t in (2, 3):
-        gathered[t] = gather_three(t, gathered[t])
-
-    @pl.when(z < 2)
-    def _():
-        own_block()
+    own_block(0)
+    own_block(1)
+    for u in last:
+        stage[u] = scatter_one(u, stage[u])
+    own_block(2)
+    own_block(3)
+    for u in (0, 1):
+        gathered[u] = gather_one(u)
+    for u in last:
+        stage[u] = scatter_two(u, stage[u])
+    for u in (2, 3):
+        gathered[u] = gather_one(u)
+    for u in (0, 1):
+        gathered[u] = gather_two(u, gathered[u])
+    for u in last:
+        scatter_three(u, stage[u])
+    for u in (2, 3):
+        gathered[u] = gather_two(u, gathered[u])
+    for u in (0, 1):
+        gathered[u] = gather_three(u, gathered[u])
+    for u in last:
+        own_block(u)
+    for u in (2, 3):
+        gathered[u] = gather_three(u, gathered[u])
 
     sums = exchange_end(2, copies)
     loss_ref[...] = sums[TAIL:, :1][:1]
@@ -947,8 +1032,8 @@
     middle = rest.astype(low)
     parts = jnp.concatenate([high, middle, (rest - middle.astype(f32)).astype(low)], axis=0)
 
-    for t in (1, 0):
-        gathered[t] = gather_one(t)
+    for u in last:
+        gathered[u] = gather_one(u)
 
     flat_sums, flat_new = [], []
     window = 256
@@ -968,17 +1053,37 @@
     flat_sums = jnp.concatenate(flat_sums + [sums[classes:]], axis=0)
     flat_new = jnp.concatenate(flat_new + [fresh[classes:]], axis=0)
 
-    for t in (1, 0):
-        gathered[t] = gather_two(t, gathered[t])
-
-    halo_copy().wait()
+    for u in last:
+        gathered[u] = gather_two(u, gathered[u])
+
+    mine = [own_group(u) for u in range(len(units))]
+    for slot in range(spare + 1):
+        group = me * spare + slot
+        own = group < 0
+        for u, unit in enumerate(units):
+            inside = jnp.logical_and(group >= mine[u], group < mine[u] + unit[1])
+            own = jnp.logical_or(own, inside)
+
+        @pl.when(jnp.logical_and(jnp.logical_not(own), group < groups - 1))
+        def _():
+            land(0, group, me, slot, 0)[0].wait_recv()
+
+    pltpu.make_async_copy(
+        weight.at[pl.ds(0, OWN)], weight.at[pl.ds(0, OWN)], fetch_sem.at[3]
+    ).wait()
+    total[pl.ds(0, SPAN), :] = landed[pl.ds(0, SPAN), :].astype(f32)
+
+    @pl.loop(0, OWN // 16)
+    def _(k):
+        row = pl.multiple_of(k * 16, 16)
+        renew(row, first_row + row)
 
     @pl.when(me < 31)
     def _():
         pltpu.make_async_copy(
             weight.at[pl.ds(OWN, TAIL)], weight.at[pl.ds(OWN, TAIL)], fetch_sem.at[4]
         ).wait()
-        total[pl.ds(SPAN, GROUP), :] = halo_in[...]
+        total[pl.ds(SPAN, GROUP), :] = landed[pl.ds(SPAN, GROUP), :].astype(f32)
         renew(OWN, first_row + OWN)
 
     def tail_rows(values, ref):
@@ -998,42 +1103,47 @@
     tail_rows(flat_new, new_flat)
     out_ref[pl.ds(32 * SPAN, GROUP), :] = new_flat[pl.ds(SPAN, GROUP), :].astype(low)
 
-    for t in (1, 0):
-        gathered[t] = gather_three(t, gathered[t])
-    for t in range(4):
-        for copy in gathered[t]:
-            copy.wait()
-
-        @pl.when(z != t)
+    for u in last:
+        gathered[u] = gather_three(u, gathered[u])
+    for u in range(len(units)):
+        gathered[u].wait()
+        for k in range(1, 4):
+            line_copy(u, k).wait_send()
+            spread_copy(u, k).wait_send()
+    for away, copy in passes:
+
+        @pl.when(away)
         def _():
-            line_copy(t, z).wait_send()
-
-    for k in range(3):
-        spread_copy(k).wait_send()
+            copy.wait_send()
 
 
 def finish_kernel(count, *refs):
+    sources, targets, sem = refs[:count], refs[count : 2 * count], refs[2 * count]
     copies = [
-        pltpu.make_async_copy(refs[k], refs[count + k], refs[2 * count].at[k])
-        for k in range(count)
+        pltpu.make_async_copy(sources[k], targets[k], sem.at[k]) for k in range(count - 2)
     ]
     for copy in copies:
         copy.start()
+    for k in (count - 2, count - 1):
+        targets[k][...] = sources[k][...]
     for copy in copies:
         copy.wait()
 
 
 def finish(values):
+    vmem = pl.BlockSpec(memory_space=pltpu.VMEM)
+    hbm = pl.BlockSpec(memory_space=pl.ANY)
     count = len(values)
-    specs = [pl.BlockSpec(memory_space=pl.ANY)] * count
+    held = [pltpu.with_memory_space_constraint(value, pltpu.VMEM) for value in values[:-2]]
     return pl.pallas_call(
         functools.partial(finish_kernel, count),
         out_shape=[jax.ShapeDtypeStruct(value.shape, value.dtype) for value in values],
-        in_specs=specs,
-        out_specs=specs,
+        in_specs=[vmem] * count,
+        out_specs=[hbm] * (count - 2) + [vmem] * 2,
         scratch_shapes=[pltpu.SemaphoreType.DMA((count,))],
+        compiler_params=pltpu.CompilerParams(vmem_limit_bytes=1024 * 1024),
         name="finish",
-    )(*values)
+    )(*held, *values[-2:])
 
 
 def run_step(images, conv_one, conv_two, shortcut, head, norm_params, valid, labels, rows, cols, moment):
@@ -1049,10 +1159,11 @@
     edges = [conv_one.shape[0]]
     edges.append(edges[0] + conv_two.shape[0])
     edges.append(edges[1] + shortcut.shape[0])
+    units = make_units(edges)
     flat = (edges[2] + TAIL) * width // 128
     share = flat // workers
     return pl.pallas_call(
-        functools.partial(step_kernel, tuple(edges), 1.0 / math.sqrt(workers)),
+        functools.partial(step_kernel, tuple(edges), tuple(units), 1.0 / math.sqrt(workers)),
         out_shape=(
             shape((share, 128), f32),
             shape((share, 128), f32),
@@ -1060,10 +1171,10 @@
             shape(rows.shape, f32),
             shape(cols.shape, f32),
             shape(moment.shape, f32),
-            shape((1, 1), f32),
-            shape((1, 1), f32),
+            jax.ShapeDtypeStruct((1, 1), f32),
+            jax.ShapeDtypeStruct((1, 1), f32),
         ),
-        in_specs=[vmem] + [hbm] * 3 + [vmem] * 7,
+        in_specs=[hbm] * 4 + [vmem] * 7,
         out_specs=(vmem,) * 8,
         scratch_shapes=[
             pltpu.VMEM((2, 4, 2, 4, slots, in_width), low),
@@ -1091,32 +1202,35 @@
             pltpu.VMEM((TAIL + 8, width), f32),
             pltpu.VMEM((8, TAIL + 8, width), f32),
             pltpu.VMEM((4, TAIL + 8, width), f32),
-            pltpu.VMEM((4, 2, 2, SPAN, 128), low),
-            pltpu.VMEM((4, 2, HALF, 128), low),
-            pltpu.VMEM((4, 2, HALF, 128), low),
-            pltpu.VMEM((4, SPAN, 128), low),
-            pltpu.VMEM((4, SPAN, 128), low),
-            pltpu.VMEM((GROUP, 128), f32),
+            pltpu.VMEM((16 * SPAN, 128), low),
+            pltpu.VMEM((8 * SPAN, 128), low),
+            pltpu.VMEM((4 * SPAN, 128), low),
+            pltpu.VMEM((4 * SPAN, 128), low),
+            pltpu.VMEM((SPAN, 128), low),
+            pltpu.VMEM((SPAN + GROUP, 128), low),
             pltpu.VMEM((SPAN + GROUP, 128), f32),
+            pltpu.VMEM((OWN, width), f32),
             pltpu.VMEM((OWN + TAIL, width), f32),
             pltpu.VMEM((SPAN + GROUP, 128), f32),
             pltpu.VMEM((SPAN + GROUP, 128), f32),
-            dma((5,)),
+            dma((5 + len(units),)),
             dma((3, 10)),
             dma((3, 10)),
-            dma((4, 4)),
-            dma((4, 4)),
-            dma((4, 4)),
-            dma((4, 4)),
-            dma((4,)),
-            dma((4,)),
+            dma((len(units), 3)),
+            dma((len(units), 3)),
+            dma((len(units), 4)),
+            dma((len(units), 4)),
+            dma((2 * OWN // 16,)),
+            dma((OWN // 16 + 1,)),
+            dma((len(units), 4)),
+            dma((len(units), 4)),
+            dma((len(units), 3)),
+            dma((len(units), 3)),
+            pltpu.SemaphoreType.REGULAR((len(units),)),
             dma((2,)),
-            dma((11, 4)),
-            dma((11, 4)),
-            pltpu.SemaphoreType.REGULAR((4,)),
         ],
         compiler_params=pltpu.CompilerParams(
-            collective_id=1, has_side_effects=True, vmem_limit_bytes=54 * 1024 * 1024
+            collective_id=1, has_side_effects=True, vmem_limit_bytes=52 * 1024 * 1024
         ),
         name="step",
     )(images, conv_one, conv_two, shortcut, head, norm_params, valid, labels, rows, cols, moment)

time: 430 us -> 153 us (0.36); the launches traced: 421 us -> 153 us
  Pallas kernels: 414 us -> 152 us
  local copies, waits for them, and re-layouts: 6.32 us -> 0 us
    pallas_call x1, Pallas kernels: 255 us -> 5.18 us  [finish(): pl.pallas_call(functools.partial(finish_kernel, count), out_shape=[jax.Sh...]
    pallas_call x1, Pallas kernels: 159 us -> 147 us  [run_step(): pl.pallas_call(functools.partial(step_kernel, tuple(edges), tuple(units),...]
    unnamed x12 -> x0, local copies, waits for them, and re-layouts: 6.32 us -> none
where the time goes in v5:
time: 153 us
  Pallas kernels  152 us (99%)
    pallas_call x1, Pallas kernels, run_step(): pl.pallas_call(functools.partial(step_kernel, tuple(edges), tuple(units),...  147 us
    pallas_call x1, Pallas kernels, finish(): pl.pallas_call(functools.partial(finish_kernel, count), out_shape=[jax.Sh...  5.18 us

profile of v5, /device:TPU:0, one launch (start us, length us, event | category | flops | bytes accessed | tf_op | source)
XLA Modules:
  0.0 152.8 jit_solution(14631973733960434327)
XLA Ops:
  0.6 146.8 %step.1 = (f32[898,128]{1,0:T(8,128)S(1)}, f32[898,128]{1,0:T(8,128)S(1)}, bf16[28736,128]{1,0:T(8,128)(2,1)S(1)}, f32[1,7680]{1,0:T(1,128)S(1)}, f32[1,1546]{1,...) custom-call(bf16[4096,256]{1,0:T(8,128)(2,1)} %bitcast.9, f32[2304,512]{1,0:T(8,128)} %one_hbm.1, ...), custom_call_target="tpu_custom_call" | custom-call | tf_op jit(solution)/shard_map/step/pallas_call | solution.py:1165
  147.5 5.2 %finish.1 = (bf16[28736,128]{1,0:T(8,128)(2,1)}, f32[898,128]{1,0:T(8,128)}, f32[898,128]{1,0:T(8,128)}, f32[1,7680]{1,0:T(1,128)}, f32[1,1546]{1,0:T(1,128)}, /...) custom-call(bf16[28736,128]{1,0:T(8,128)(2,1)S(1)} %get-tuple-element.24.refs_0_, ...), custom_call_target="tpu_custom_call" | custom-call | tf_op jit(solution)/shard_map/finish/pallas_call | solution.py:1138

commit v6 on v5

--- a/solution.py
+++ b/solution.py
@@ -116,6 +116,33 @@
     return (grad_gain, grad_shift, grad_pre)
 
 
+SCHEDULE = (
+    (),
+    (),
+    (),
+    (
+        (1, 0), (1, 1), (1, 3), (1, 4), (1, 5), (1, 7), (1, 2),
+    ),
+    (),
+    (),
+    (),
+    (),
+    (),
+    (),
+    (
+        (1, 6), (2, 1), (2, 3), (1, 8), (2, 0), (2, 7), (1, 9), (3, 0), (1, 10), (1, 12),
+        (1, 11), (2, 2), (2, 4), (4, 0), (3, 1), (5, 0), (3, 3), (3, 2), (2, 5), (2, 6), (4, 1),
+        (1, 13), (4, 3), (3, 4), (3, 7), (3, 5), (2, 8), (5, 1), (2, 10), (2, 9), (2, 12),
+        (4, 2), (6, 0), (3, 9), (2, 11), (4, 5), (6, 1), (2, 13), (4, 7), (3, 6), (4, 4),
+        (3, 11), (3, 10), (3, 13), (5, 2), (3, 8), (5, 3), (6, 3), (6, 2), (5, 5), (4, 6),
+        (7, 0), (5, 4), (4, 9), (6, 5), (7, 1), (4, 10), (4, 8), (5, 7), (7, 3), (6, 7), (6, 4),
+        (7, 5), (4, 13), (7, 2), (5, 10), (3, 12), (4, 11), (5, 6), (5, 9), (6, 6), (4, 12),
+        (5, 8), (6, 8), (6, 9), (5, 11), (7, 7), (7, 4), (7, 9), (6, 10), (5, 12), (5, 13),
+        (6, 11), (7, 6), (7, 11), (6, 12), (7, 8), (6, 13), (7, 10), (7, 13), (7, 12),
+    ),
+)
+
+
 def place():
     me = lax.axis_index("dp")
     core = lax.rem(me, 2)
@@ -147,17 +174,13 @@
 def make_units(edges):
     one, two, short = edges[0] // 16, edges[1] // 16, edges[2] // 16
     units = []
-    at = one
-    for size, x_first in ((2, True), (2, False), (2, True), (3, False)):
-        units.append((at, size, x_first, 16 * size, (1, 1)))
-        at += 32 * size
-    assert at == two
-    at = 0
-    for size, x_first in ((2, True), (2, False)):
-        units.append((at, size, x_first, 16 * size, (0, 0)))
-        at += 32 * size
+    for k in range((two - one) // 32):
+        units.append((one + 32 * k, 1, k % 2 == 0, 16, (1, 1)))
+    for k in range(one // 32):
+        units.append((32 * k, 1, k % 2 == 1, 16, (0, 0)))
+    at = one // 32 * 32
     assert one - at == 16 and short - two == 16
-    units.append((at, 1, True, two - at, (0, 2)))
+    units.append((at, 1, False, two - at, (0, 2)))
     return units
 
 
@@ -190,10 +213,12 @@
     return jnp.sum(values.reshape(values.shape[0] // 8, 8, values.shape[1]), axis=0)
 
 
-def cast_weight(source, target, square_ref, taps, depth):
+def cast_weight(source, target, square_ref, taps, depth, fetches):
     step = 128
     square_ref[...] = jnp.zeros_like(square_ref)
     for tap in range(taps):
+        if tap % (taps // len(fetches)) == 0:
+            fetches[tap * len(fetches) // taps].wait()
         new_tap = (tap % 3) * 3 + tap // 3
 
         @pl.loop(0, depth // step)
@@ -204,7 +229,7 @@
             square_ref[...] += fold(values * values)
 
 
-def factored_votes(grad, rows, row_at, rows_old, rows_new, col_old, level, votes, vote_at, between):
+def factored_votes(grad, rows, row_at, rows_old, rows_new, col_old, level, votes, vote_at, between, after):
     width = grad.shape[1]
     keep = 1.0 - STEP ** (-0.8)
     step = 128
@@ -272,14 +297,16 @@
             here = pl.ds(start + 16 * m, 16)
             factor = level[here, :]
             factor = jnp.concatenate([factor] * quarters, axis=1)
-            vote = jnp.tanh(grad[here, :] * factor * scale)
-            vote = vote.astype(jnp.bfloat16)
+            vote = jnp.tanh(grad[here, :] * factor * scale).astype(jnp.bfloat16)
             at = pl.multiple_of((vote_at + start) * 4 + GROUP * m, GROUP)
             for q in range(quarters):
                 votes[pl.ds(at + 16 * q, 16), :] = vote[:, 128 * q : 128 * (q + 1)]
         return 0
 
-    lax.fori_loop(0, rows // step, third, 0)
+    part = 512 // step
+    for k in range(0, rows // step, part):
+        lax.fori_loop(k, min(k + part, rows // step), third, 0)
+        after(k // part)
     return col_new
 
 
@@ -325,9 +352,12 @@
     head_pad,
     level,
     square,
-    post,
-    plane,
-    line,
+    post_one,
+    plane_one,
+    line_one,
+    post_two,
+    plane_two,
+    line_two,
     tail_post,
     tail_plane,
     tail_line,
@@ -388,13 +418,21 @@
         )
         loads[half].start()
 
-    fetches = [
-        pltpu.make_async_copy(source, target, fetch_sem.at[k])
-        for k, (source, target) in enumerate(
-            ((one_hbm, grad_one), (short_hbm, grad_short), (two_hbm, grad_two))
-        )
-    ]
-    for fetch in fetches:
+    def chunks_of(source, target, first, count):
+        rows = source.shape[0] // count
+        return [
+            pltpu.make_async_copy(
+                source.at[pl.ds(k * rows, rows)],
+                target.at[pl.ds(k * rows, rows)],
+                fetch_sem.at[first + k],
+            )
+            for k in range(count)
+        ]
+
+    fetch_one = chunks_of(one_hbm, grad_one, 0, 3)
+    fetch_short = chunks_of(short_hbm, grad_short, 3, 1)
+    fetch_two = chunks_of(two_hbm, grad_two, 4, 3)
+    for fetch in fetch_one + fetch_short:
         fetch.start()
     barrier = pltpu.get_barrier_semaphore()
     for partner in others:
@@ -416,9 +454,6 @@
                 ).start()
 
     first_row = me * OWN
-    for k in range(OWN // PIECE):
-        fetch_rows(first_row + k * PIECE, PIECE, k * PIECE, fetch_sem.at[3])
-    fetch_rows(first_row + OWN, TAIL, OWN, fetch_sem.at[4])
 
     for half in range(2):
         lanes = slice(128 * half, 128 * (half + 1))
@@ -435,8 +470,8 @@
         return jnp.maximum(EPS_SCALE, jnp.sqrt(total_of(weight_square) / size))
 
     exchanges = (
-        (post.at[0], plane.at[0], line.at[0]),
-        (post.at[1], plane.at[1], line.at[1]),
+        (post_one, plane_one, line_one),
+        (post_two, plane_two, line_two),
         (tail_post, tail_plane, tail_line),
     )
 
@@ -454,6 +489,16 @@
             )
             for k, partner in enumerate(near)
         ]
+
+    def pack_rows(rows):
+        pieces = [row[:, 128 * q : 128 * (q + 1)] for row in rows for q in range(4)]
+        pad = -len(pieces) % 8
+        if pad:
+            pieces.append(jnp.zeros((pad, 128), f32))
+        return jnp.concatenate(pieces, axis=0)
+
+    def unpack_row(lines_in, k):
+        return jnp.concatenate([lines_in[4 * k + q : 4 * k + q + 1] for q in range(4)], axis=1)
 
     def exchange_middle(which, copies):
         _, plane_ref, line_ref = exchanges[which]
@@ -627,11 +672,8 @@
             def _():
                 ref, row, count = old_rows(u, cc)
                 pltpu.make_async_copy(
-                    ref.at[pl.ds(pl.multiple_of(row, 16), count)], target, fetch_sem.at[5 + u]
+                    ref.at[pl.ds(pl.multiple_of(row, 16), count)], target, fetch_sem.at[9 + u]
                 ).start()
-
-    for u in range(len(units)):
-        own_fetch(u)
 
     def spread_copy(u, k):
         own = out_ref.at[lines(own_group(u) * GROUP, sizes[u])]
@@ -656,7 +698,7 @@
         sum_low[here, :] = low_sum
         total[here, :] = low_sum.astype(f32)
         target = own_weight.at[pl.ds(starts[u] // 4, 16 * units[u][1])]
-        pltpu.make_async_copy(target, target, fetch_sem.at[5 + u]).wait()
+        pltpu.make_async_copy(target, target, fetch_sem.at[9 + u]).wait()
         matrices = units[u][4]
         scale = jnp.where(core == 0, scales[matrices[0]], scales[matrices[1]])
         for m in range(units[u][1]):
@@ -710,12 +752,17 @@
     weight_slot = jnp.broadcast_to(valid_column, (slots, width))
     weight_band = jnp.concatenate([weight_slot] * side, axis=0)
 
-    fetches[0].wait()
-    cast_weight(grad_one, low_one, square, 9, in_width)
+    cast_weight(grad_one, low_one, square, 9, in_width, fetch_one)
     scales[0] = scale_from(square[...], grad_one.size)
-    fetches[1].wait()
-    cast_weight(grad_short, low_short, square, 1, in_width)
+    cast_weight(grad_short, low_short, square, 1, in_width, fetch_short)
     scales[2] = scale_from(square[...], grad_short.size)
+    for fetch in fetch_two:
+        fetch.start()
+    for k in range(OWN // PIECE):
+        fetch_rows(first_row + k * PIECE, PIECE, k * PIECE, fetch_sem.at[7])
+    fetch_rows(first_row + OWN, TAIL, OWN, fetch_sem.at[8])
+    for u in range(len(units)):
+        own_fetch(u)
 
     def image_taps(j):
         pieces = []
@@ -762,10 +809,9 @@
     count = jnp.broadcast_to(jnp.sum(valid_column, axis=0, keepdims=True), (1, width))
     pl.semaphore_wait(barrier, len(others))
     copies = exchange_start(
-        0, jnp.concatenate(main_sums + side_sums + [count, none, none, none], axis=0)
-    )
-    fetches[2].wait()
-    cast_weight(grad_two, low_two, square, 9, width)
+        0, pack_rows(main_sums + side_sums + [count])
+    )
+    cast_weight(grad_two, low_two, square, 9, width, fetch_two)
     scales[1] = scale_from(square[...], grad_two.size)
     copies = exchange_middle(0, copies)
     for across in range(2):
@@ -786,17 +832,18 @@
     params = norm_ref[...]
     scales[4] = scale_from(params * params, norm_ref.size)
     sums = exchange_end(0, copies)
-
-    valid_count = sums[4:5]
+    sums = [unpack_row(sums, k) for k in range(5)]
+
+    valid_count = sums[4]
     count_ref[...] = valid_count[:, :1]
     denominator = jnp.maximum(valid_count, 1.0)
     pixels = denominator * pixel_count
     gains = [norm_ref[k : k + 1, :] for k in range(6)]
     mean_one, inv_one, slope_one, base_one = settle_rows(
-        (sums[0:1], sums[1:2]), pixels, gains[0], gains[1]
+        (sums[0], sums[1]), pixels, gains[0], gains[1]
     )
     mean_side, inv_side, slope_side, base_side = settle_rows(
-        (sums[2:3], sums[3:4]), pixels, gains[4], gains[5]
+        (sums[2], sums[3]), pixels, gains[4], gains[5]
     )
 
     for j in range(side):
@@ -814,14 +861,15 @@
         value = jnp.dot(jnp.concatenate(pieces, axis=1), low_rows, preferred_element_type=f32)
         main_two[pl.ds(j * band, band), :] = value
         two_sums = add_up(two_sums, moments(value))
-    copies = exchange_start(1, jnp.concatenate(two_sums + [none] * 6, axis=0))
+    copies = exchange_start(1, pack_rows(two_sums))
     for j in range(side):
         block = active[j, 1 : side + 1].reshape(band, width)
         active_t[:, j * band : (j + 1) * band] = block.T
     copies = exchange_middle(1, copies)
     sums = exchange_end(1, copies)
+    sums = [unpack_row(sums, k) for k in range(2)]
     mean_two, inv_two, slope_two, base_two = settle_rows(
-        (sums[0:1], sums[1:2]), pixels, gains[2], gains[3]
+        (sums[0], sums[1]), pixels, gains[2], gains[3]
     )
 
     base_joined = base_two + base_side
@@ -871,7 +919,6 @@
         back_two[p // side, 1 + p % side] = (grad * slope_two).astype(low)
         back_side[here, :] = (grad * slope_side).astype(low)
 
-    grad_short[...] = jnp.dot(xs_t[0, 0], back_side[...], preferred_element_type=f32)
     for b in range(3):
         first, last = max(0, b - 1), min(side, side + b - 1)
         left = active_t[:, first * band : last * band]
@@ -881,20 +928,50 @@
                 left, right.reshape(-1, width), preferred_element_type=f32
             )
 
-
     def nothing():
         pass
 
-    def matrix_votes(k, grad, between):
+    def matrix_votes(k, grad, between, after):
         here = pl.ds(k * width, width)
         start = edges[k - 1] if k else 0
         col_new[:, here] = factored_votes(
-            grad, grad.shape[0], start, row_ref, row_new, col_ref[:, here], level, out_ref, start, between
-        )
-
-    matrix_votes(2, grad_short, (nothing, nothing))
-    matrix_votes(1, grad_two, (nothing, nothing))
-    stage = {u: scatter_start(u) for u in range(4)}
+            grad,
+            grad.shape[0],
+            start,
+            row_ref,
+            row_new,
+            col_ref[:, here],
+            level,
+            out_ref,
+            start,
+            between,
+            after,
+        )
+
+    in_flight = {}
+    steps = (
+        lambda u, copy: scatter_start(u),
+        scatter_one,
+        scatter_two,
+        scatter_three,
+        lambda u, copy: own_block(u),
+        lambda u, copy: gather_one(u),
+        gather_two,
+        gather_three,
+    )
+
+    def go(number, u):
+        in_flight[u] = steps[number](u, in_flight.get(u))
+
+    def turn(number):
+        for step_number, u in SCHEDULE[number]:
+            go(step_number, u)
+
+    early = edges[1] // 512 - edges[0] // 512
+    matrix_votes(1, grad_two, (nothing, nothing), lambda k: go(0, k))
+    turn(0)
+    grad_short[...] = jnp.dot(xs_t[0, 0], back_side[...], preferred_element_type=f32)
+    matrix_votes(2, grad_short, (nothing, nothing), lambda k: None)
 
     gain_one, shift_one = none, none
     for j in range(side):
@@ -920,12 +997,7 @@
             grad * ((before - mean_one) * inv_one), axis=0, keepdims=True
         )
         back_one[j, :side] = (grad * slope_one).astype(low).reshape(side, slots, width)
-        if j == 1:
-            stage[0] = scatter_one(0, stage[0])
-            stage[1] = scatter_one(1, stage[1])
-        if j == 2:
-            stage[2] = scatter_one(2, stage[2])
-            stage[3] = scatter_one(3, stage[3])
+        turn(1 + j)
 
     square_head = grad_head * grad_head + EPS_ROW
     real = lax.broadcasted_iota(jnp.int32, square_head.shape, 0) < classes
@@ -957,9 +1029,14 @@
     raw = jnp.concatenate(raws, axis=0)
     clip = jnp.maximum(1.0, jnp.sqrt(total_of(raw * raw) / raw.size))
     norm_votes = jnp.tanh(raw / clip)
+    tail_votes = jnp.concatenate([head_votes, norm_votes], axis=0)
     copies = exchange_start(
         2,
-        jnp.concatenate([head_votes, norm_votes, jnp.broadcast_to(loss, (8, width))], axis=0),
+        jnp.concatenate(
+            [tail_votes[:, 128 * q : 128 * (q + 1)] for q in range(4)]
+            + [jnp.broadcast_to(loss, (8, 128))],
+            axis=0,
+        ),
     )
 
 
@@ -973,67 +1050,34 @@
             grad_one[pl.ds((a * 3 + b) * in_width, in_width), :] = jnp.dot(
                 left, right.reshape(-1, width), preferred_element_type=f32
             )
-        if b == 0:
-            stage[0] = scatter_two(0, stage[0])
-            stage[1] = scatter_two(1, stage[1])
         if b == 1:
             copies = exchange_middle(2, copies)
-        if b == 2:
-            stage[2] = scatter_two(2, stage[2])
-            stage[3] = scatter_two(3, stage[3])
-
-    def first_line():
-        scatter_three(0, stage[0])
-        scatter_three(1, stage[1])
-
-    def second_line():
-        scatter_three(2, stage[2])
-        scatter_three(3, stage[3])
-
-    matrix_votes(0, grad_one, (first_line, second_line))
-    last = (4, 5, 6)
-    stage = {u: scatter_start(u) for u in last}
-    gathered = {}
-    own_block(0)
-    own_block(1)
-    for u in last:
-        stage[u] = scatter_one(u, stage[u])
-    own_block(2)
-    own_block(3)
-    for u in (0, 1):
-        gathered[u] = gather_one(u)
-    for u in last:
-        stage[u] = scatter_two(u, stage[u])
-    for u in (2, 3):
-        gathered[u] = gather_one(u)
-    for u in (0, 1):
-        gathered[u] = gather_two(u, gathered[u])
-    for u in last:
-        scatter_three(u, stage[u])
-    for u in (2, 3):
-        gathered[u] = gather_two(u, gathered[u])
-    for u in (0, 1):
-        gathered[u] = gather_three(u, gathered[u])
-    for u in last:
-        own_block(u)
-    for u in (2, 3):
-        gathered[u] = gather_three(u, gathered[u])
+        turn(5 + b)
+
+    matrix_votes(
+        0,
+        grad_one,
+        (lambda: turn(8), lambda: turn(9)),
+        lambda k: go(0, early + k),
+    )
+    last_turn = SCHEDULE[10]
+    cut = [k for k, (number, _) in enumerate(last_turn) if number == 4][-1] + 1
+    ending = len(last_turn) - 3
+    for number, u in last_turn[:cut]:
+        go(number, u)
 
     sums = exchange_end(2, copies)
-    loss_ref[...] = sums[TAIL:, :1][:1]
+    loss_ref[...] = sums[4 * TAIL : 4 * TAIL + 1, :1]
     old = jnp.concatenate([head_ref[...], norm_ref[...]], axis=0)
     is_head = lax.broadcasted_iota(jnp.int32, (TAIL, width), 0) < classes
     scale = jnp.where(is_head, scales[3], scales[4])
-    sums = sums[:TAIL]
+    sums = jnp.concatenate([sums[TAIL * q : TAIL * (q + 1)] for q in range(4)], axis=1)
     fresh = old - scale * jnp.tanh(sums * root)
     both = jnp.concatenate([sums, fresh], axis=0)
     high = both.astype(low)
     rest = both - high.astype(f32)
     middle = rest.astype(low)
     parts = jnp.concatenate([high, middle, (rest - middle.astype(f32)).astype(low)], axis=0)
-
-    for u in last:
-        gathered[u] = gather_one(u)
 
     flat_sums, flat_new = [], []
     window = 256
@@ -1053,8 +1097,8 @@
     flat_sums = jnp.concatenate(flat_sums + [sums[classes:]], axis=0)
     flat_new = jnp.concatenate(flat_new + [fresh[classes:]], axis=0)
 
-    for u in last:
-        gathered[u] = gather_two(u, gathered[u])
+    for number, u in last_turn[cut:ending]:
+        go(number, u)
 
     mine = [own_group(u) for u in range(len(units))]
     for slot in range(spare + 1):
@@ -1069,7 +1113,7 @@
             land(0, group, me, slot, 0)[0].wait_recv()
 
     pltpu.make_async_copy(
-        weight.at[pl.ds(0, OWN)], weight.at[pl.ds(0, OWN)], fetch_sem.at[3]
+        weight.at[pl.ds(0, OWN)], weight.at[pl.ds(0, OWN)], fetch_sem.at[7]
     ).wait()
     total[pl.ds(0, SPAN), :] = landed[pl.ds(0, SPAN), :].astype(f32)
 
@@ -1081,7 +1125,7 @@
     @pl.when(me < 31)
     def _():
         pltpu.make_async_copy(
-            weight.at[pl.ds(OWN, TAIL)], weight.at[pl.ds(OWN, TAIL)], fetch_sem.at[4]
+            weight.at[pl.ds(OWN, TAIL)], weight.at[pl.ds(OWN, TAIL)], fetch_sem.at[8]
         ).wait()
         total[pl.ds(SPAN, GROUP), :] = landed[pl.ds(SPAN, GROUP), :].astype(f32)
         renew(OWN, first_row + OWN)
@@ -1103,10 +1147,10 @@
     tail_rows(flat_new, new_flat)
     out_ref[pl.ds(32 * SPAN, GROUP), :] = new_flat[pl.ds(SPAN, GROUP), :].astype(low)
 
-    for u in last:
-        gathered[u] = gather_three(u, gathered[u])
+    for number, u in last_turn[ending:]:
+        go(number, u)
     for u in range(len(units)):
-        gathered[u].wait()
+        in_flight[u].wait()
         for k in range(1, 4):
             line_copy(u, k).wait_send()
             spread_copy(u, k).wait_send()
@@ -1117,11 +1161,18 @@
             copy.wait_send()
 
 
-def finish_kernel(count, *refs):
+def finish_kernel(count, chunks, *refs):
     sources, targets, sem = refs[:count], refs[count : 2 * count], refs[2 * count]
-    copies = [
-        pltpu.make_async_copy(sources[k], targets[k], sem.at[k]) for k in range(count - 2)
-    ]
+    rows = sources[0].shape[0]
+    step = -(-rows // chunks // 16) * 16
+    copies = []
+    for k in range(chunks):
+        here = pl.ds(k * step, min(step, rows - k * step))
+        copies.append(
+            pltpu.make_async_copy(sources[0].at[here], targets[0].at[here], sem.at[k])
+        )
+    for k in range(1, count - 2):
+        copies.append(pltpu.make_async_copy(sources[k], targets[k], sem.at[chunks + k]))
     for copy in copies:
         copy.start()
     for k in (count - 2, count - 1):
@@ -1133,14 +1184,14 @@
 def finish(values):
     vmem = pl.BlockSpec(memory_space=pltpu.VMEM)
     hbm = pl.BlockSpec(memory_space=pl.ANY)
-    count = len(values)
+    count, chunks = len(values), 8
     held = [pltpu.with_memory_space_constraint(value, pltpu.VMEM) for value in values[:-2]]
     return pl.pallas_call(
-        functools.partial(finish_kernel, count),
+        functools.partial(finish_kernel, count, chunks),
         out_shape=[jax.ShapeDtypeStruct(value.shape, value.dtype) for value in values],
         in_specs=[vmem] * count,
         out_specs=[hbm] * (count - 2) + [vmem] * 2,
-        scratch_shapes=[pltpu.SemaphoreType.DMA((count,))],
+        scratch_shapes=[pltpu.SemaphoreType.DMA((chunks + count,))],
         compiler_params=pltpu.CompilerParams(vmem_limit_bytes=1024 * 1024),
         name="finish",
     )(*held, *values[-2:])
@@ -1196,12 +1247,15 @@
             pltpu.VMEM((128, width), f32),
             pltpu.VMEM((conv_two.shape[0], 128), f32),
             pltpu.VMEM((8, width), f32),
-            pltpu.VMEM((2, 8, width), f32),
-            pltpu.VMEM((2, 8, 8, width), f32),
-            pltpu.VMEM((2, 4, 8, width), f32),
-            pltpu.VMEM((TAIL + 8, width), f32),
-            pltpu.VMEM((8, TAIL + 8, width), f32),
-            pltpu.VMEM((4, TAIL + 8, width), f32),
+            pltpu.VMEM((24, 128), f32),
+            pltpu.VMEM((8, 24, 128), f32),
+            pltpu.VMEM((4, 24, 128), f32),
+            pltpu.VMEM((8, 128), f32),
+            pltpu.VMEM((8, 8, 128), f32),
+            pltpu.VMEM((4, 8, 128), f32),
+            pltpu.VMEM((GROUP + 8, 128), f32),
+            pltpu.VMEM((8, GROUP + 8, 128), f32),
+            pltpu.VMEM((4, GROUP + 8, 128), f32),
             pltpu.VMEM((16 * SPAN, 128), low),
             pltpu.VMEM((8 * SPAN, 128), low),
             pltpu.VMEM((4 * SPAN, 128), low),
@@ -1213,7 +1267,7 @@
             pltpu.VMEM((OWN + TAIL, width), f32),
             pltpu.VMEM((SPAN + GROUP, 128), f32),
             pltpu.VMEM((SPAN + GROUP, 128), f32),
-            dma((5 + len(units),)),
+            dma((9 + len(units),)),
             dma((3, 10)),
             dma((3, 10)),
             dma((len(units), 3)),
@@ -1230,7 +1284,7 @@
             dma((2,)),
         ],
         compiler_params=pltpu.CompilerParams(
-            collective_id=1, has_side_effects=True, vmem_limit_bytes=52 * 1024 * 1024
+            collective_id=1, has_side_effects=True, vmem_limit_bytes=54 * 1024 * 1024
         ),
         name="step",
     )(images, conv_one, conv_two, shortcut, head, norm_params, valid, labels, rows, cols, moment)

time: 153 us -> 157 us (1.026)
  Pallas kernels: 152 us -> 156 us
    pallas_call x1, Pallas kernels: 147 us -> 151 us  [run_step(): pl.pallas_call(functools.partial(step_kernel, tuple(edges), tuple(units),...]
where the time goes in v6:
time: 157 us
  Pallas kernels  156 us (99%)
    pallas_call x1, Pallas kernels, run_step(): pl.pallas_call(functools.partial(step_kernel, tuple(edges), tuple(units),...  151 us
    pallas_call x1, Pallas kernels, finish(): pl.pallas_call(functools.partial(finish_kernel, count, chunks), out_shape...  5.17 us

profile of v6, /device:TPU:0, one launch (start us, length us, event | category | flops | bytes accessed | tf_op | source)
XLA Modules:
  0.0 156.9 jit_solution(1285838223229958507)
XLA Ops:
  0.6 150.9 %step.1 = (f32[898,128]{1,0:T(8,128)S(1)}, f32[898,128]{1,0:T(8,128)S(1)}, bf16[28736,128]{1,0:T(8,128)(2,1)S(1)}, f32[1,7680]{1,0:T(1,128)S(1)}, f32[1,1546]{1,...) custom-call(bf16[4096,256]{1,0:T(8,128)(2,1)} %bitcast.9, f32[2304,512]{1,0:T(8,128)} %one_hbm.1, ...), custom_call_target="tpu_custom_call" | custom-call | tf_op jit(solution)/shard_map/step/pallas_call | solution.py:1216
  151.5 5.2 %finish.1 = (bf16[28736,128]{1,0:T(8,128)(2,1)}, f32[898,128]{1,0:T(8,128)}, f32[898,128]{1,0:T(8,128)}, f32[1,7680]{1,0:T(1,128)}, f32[1,1546]{1,0:T(1,128)}, /...) custom-call(bf16[28736,128]{1,0:T(8,128)(2,1)S(1)} %get-tuple-element.24.refs_0_, ...), custom_call_target="tpu_custom_call" | custom-call | tf_op jit(solution)/shard_map/finish/pallas_call | solution.py:1189

commit v7 on v6

--- a/solution.py
+++ b/solution.py
@@ -117,29 +117,18 @@
 
 
 SCHEDULE = (
-    (),
-    (),
-    (),
-    (
-        (1, 0), (1, 1), (1, 3), (1, 4), (1, 5), (1, 7), (1, 2),
-    ),
-    (),
-    (),
-    (),
-    (),
-    (),
-    (),
-    (
-        (1, 6), (2, 1), (2, 3), (1, 8), (2, 0), (2, 7), (1, 9), (3, 0), (1, 10), (1, 12),
-        (1, 11), (2, 2), (2, 4), (4, 0), (3, 1), (5, 0), (3, 3), (3, 2), (2, 5), (2, 6), (4, 1),
-        (1, 13), (4, 3), (3, 4), (3, 7), (3, 5), (2, 8), (5, 1), (2, 10), (2, 9), (2, 12),
-        (4, 2), (6, 0), (3, 9), (2, 11), (4, 5), (6, 1), (2, 13), (4, 7), (3, 6), (4, 4),
-        (3, 11), (3, 10), (3, 13), (5, 2), (3, 8), (5, 3), (6, 3), (6, 2), (5, 5), (4, 6),
-        (7, 0), (5, 4), (4, 9), (6, 5), (7, 1), (4, 10), (4, 8), (5, 7), (7, 3), (6, 7), (6, 4),
-        (7, 5), (4, 13), (7, 2), (5, 10), (3, 12), (4, 11), (5, 6), (5, 9), (6, 6), (4, 12),
-        (5, 8), (6, 8), (6, 9), (5, 11), (7, 7), (7, 4), (7, 9), (6, 10), (5, 12), (5, 13),
-        (6, 11), (7, 6), (7, 11), (6, 12), (7, 8), (6, 13), (7, 10), (7, 13), (7, 12),
-    ),
+        (0, 10), (0, 1), (0, 8), (0, 2), (0, 0), (0, 5), (1, 0), (0, 4), (0, 11), (1, 5),
+        (0, 13), (0, 7), (1, 2), (1, 8), (1, 1), (0, 3), (1, 4), (0, 6), (0, 9), (0, 12), (1, 3),
+        (1, 9), (2, 1), (1, 7), (1, 11), (1, 12), (1, 6), (2, 0), (2, 2), (2, 4), (1, 13),
+        (2, 5), (3, 2), (2, 3), (3, 0), (2, 8), (2, 6), (2, 12), (3, 1), (1, 10), (2, 9), (4, 0),
+        (3, 3), (4, 1), (3, 5), (3, 9), (2, 7), (4, 3), (5, 0), (2, 11), (3, 4), (4, 5), (5, 1),
+        (3, 7), (2, 13), (3, 11), (5, 3), (2, 10), (6, 1), (3, 6), (4, 2), (3, 13), (3, 10),
+        (3, 12), (6, 0), (3, 8), (7, 1), (7, 0), (4, 7), (4, 11), (5, 5), (4, 4), (6, 3), (4, 9),
+        (7, 3), (6, 5), (4, 13), (4, 10), (5, 2), (5, 7), (5, 9), (7, 5), (5, 4), (6, 2), (6, 4),
+        (6, 7), (4, 6), (4, 8), (5, 6), (4, 12), (5, 13), (6, 9), (7, 2), (5, 11), (5, 8),
+        (7, 4), (6, 6), (6, 11), (5, 10), (7, 7), (6, 8), (6, 13), (7, 8), (6, 10), (7, 9),
+        (7, 6), (5, 12), (7, 13), (7, 11), (7, 10), (6, 12), (7, 12),
+
 )
 
 
@@ -229,7 +218,7 @@
             square_ref[...] += fold(values * values)
 
 
-def factored_votes(grad, rows, row_at, rows_old, rows_new, col_old, level, votes, vote_at, between, after):
+def factored_votes(grad, rows, row_at, rows_old, rows_new, col_old, level, votes, vote_at):
     width = grad.shape[1]
     keep = 1.0 - STEP ** (-0.8)
     step = 128
@@ -285,9 +274,7 @@
             carry = carry + part * (factor * factor)
         return carry
 
-    between[0]()
     power = lax.fori_loop(0, rows // step, second, jnp.zeros((8, 128), jnp.float32))
-    between[1]()
     clip = jnp.maximum(1.0, jnp.sqrt(total_of(power) / (rows * width)))
     scale = scale / clip
 
@@ -303,17 +290,12 @@
                 votes[pl.ds(at + 16 * q, 16), :] = vote[:, 128 * q : 128 * (q + 1)]
         return 0
 
-    part = 512 // step
-    for k in range(0, rows // step, part):
-        lax.fori_loop(k, min(k + part, rows // step), third, 0)
-        after(k // part)
+    lax.fori_loop(0, rows // step, third, 0)
     return col_new
 
 
-def step_kernel(
+def worker_kernel(
     edges,
-    units,
-    root,
     images,
     one_hbm,
     two_hbm,
@@ -325,13 +307,12 @@
     row_ref,
     col_ref,
     moment_ref,
-    new_ref,
-    vote_ref,
-    out_ref,
+    votes_ref,
+    tail_ref,
+    scale_ref,
     row_new,
     col_new,
     moment_new,
-    loss_ref,
     count_ref,
     xs,
     grad_one,
@@ -352,6 +333,7 @@
     head_pad,
     level,
     square,
+    image_in,
     post_one,
     plane_one,
     line_one,
@@ -361,31 +343,9 @@
     tail_post,
     tail_plane,
     tail_line,
-    core_in,
-    wide_in,
-    deep_in,
-    line_in,
-    sum_low,
-    landed,
-    total,
-    own_weight,
-    weight,
-    vote_flat,
-    new_flat,
     fetch_sem,
     small_send,
     small_recv,
-    rs_send,
-    rs_recv,
-    line_send,
-    line_recv,
-    pass_send,
-    land_recv,
-    spread_send,
-    spread_recv,
-    ag_send,
-    ag_recv,
-    free_sem,
     load_sem,
 ):
     slots, in_width = xs.shape[4:]
@@ -398,14 +358,11 @@
     low = jnp.bfloat16
     f32 = jnp.float32
 
-    me, core, x, y, z = place()
-    flip_core = me + 1 - 2 * core
-    flip_x = me + 2 - 4 * x
-    flip_y = me + 4 - 8 * y
+    me = lax.axis_index("dp")
+    z = lax.div(me, 8)
     spot = lax.rem(me, 8)
     near = [z * 8 + lax.rem(spot + k, 8) for k in range(1, 8)]
     far = [lax.rem(z + k, 4) * 8 + spot for k in range(1, 4)]
-    others = [lax.rem(me + k, 32) for k in range(1, 32)]
 
     count = images.shape[0]
     loads = []
@@ -413,7 +370,7 @@
         lanes = slice(128 * half, 128 * (half + 1))
         loads.append(
             pltpu.make_async_copy(
-                images.at[:, lanes], core_in.at[pl.ds(half * count, count)], load_sem.at[half]
+                images.at[:, lanes], image_in.at[pl.ds(half * count, count)], load_sem.at[half]
             )
         )
         loads[half].start()
@@ -435,30 +392,13 @@
     for fetch in fetch_one + fetch_short:
         fetch.start()
     barrier = pltpu.get_barrier_semaphore()
-    for partner in others:
+    for partner in near + far:
         pl.semaphore_signal(barrier, inc=1, device_id=(partner,), device_id_type=MESH)
-
-    def fetch_rows(row, count, place_at, sem):
-        parts = (
-            (one_hbm, 0, edges[0]),
-            (two_hbm, edges[0], edges[1]),
-            (short_hbm, edges[1], edges[2]),
-        )
-        for ref, first, last in parts:
-
-            @pl.when(jnp.logical_and(row >= first, row < last))
-            def _():
-                start = pl.multiple_of(row - first, count)
-                pltpu.make_async_copy(
-                    ref.at[pl.ds(start, count)], weight.at[pl.ds(place_at, count)], sem
-                ).start()
-
-    first_row = me * OWN
 
     for half in range(2):
         lanes = slice(128 * half, 128 * (half + 1))
         loads[half].wait()
-        level[:count, :] = core_in[pl.ds(half * count, count), :].astype(f32)
+        level[:count, :] = image_in[pl.ds(half * count, count), :].astype(f32)
         for h in range(2 * side):
             for w in range(2 * side):
                 rows = level[pl.ds(2 * side * h + w, slots, stride=4 * pixel_count), :]
@@ -522,232 +462,6 @@
             copy.wait()
         return (line_ref[0] + line_ref[1]) + (line_ref[2] + line_ref[3])
 
-    def lines(start, count):
-        return pl.ds(pl.multiple_of(start, 16), count)
-
-    sizes = [GROUP * unit[1] for unit in units]
-    starts = [sum(sizes[:k]) for k in range(len(units) + 1)]
-
-    def part_of(ref, u, share, start, count):
-        return ref.at[lines(share * starts[u] + start, count)]
-
-    def places(u):
-        if units[u][2]:
-            return x, y, flip_x, flip_y
-        return y, x, flip_y, flip_x
-
-    def unit_start(u, cc):
-        return GROUP * units[u][0] + cc * (GROUP * units[u][3])
-
-    def own_group(u):
-        first, second, _, _ = places(u)
-        return units[u][0] + core * units[u][3] + (first * 8 + second * 4 + z) * units[u][1]
-
-    def halve(source, target, u, stage, partner):
-        return send(source, target, rs_send.at[u, stage], rs_recv.at[u, stage], partner)
-
-    def scatter_start(u):
-        size = 16 * sizes[u]
-        return halve(
-            out_ref.at[lines(unit_start(u, 1 - core), size)],
-            part_of(core_in, u, 16, 0, size),
-            u,
-            0,
-            flip_core,
-        )
-
-    def add_to(ref, u, share, source_ref, source_start):
-        size = share * sizes[u]
-        here = lines(share * starts[u], size)
-        ref[here, :] = ref[here, :] + source_ref[lines(source_start, size), :]
-
-    def scatter_one(u, copy):
-        copy.wait()
-        add_to(core_in, u, 16, out_ref, unit_start(u, core))
-        pl.semaphore_signal(
-            free_sem.at[u], inc=1, device_id=(flip_core,), device_id_type=MESH
-        )
-        first, _, flip_first, _ = places(u)
-        size = 8 * sizes[u]
-        return halve(
-            part_of(core_in, u, 16, (1 - first) * size, size),
-            part_of(wide_in, u, 8, 0, size),
-            u,
-            1,
-            flip_first,
-        )
-
-    def scatter_two(u, copy):
-        copy.wait()
-        first, second, _, flip_second = places(u)
-        add_to(wide_in, u, 8, core_in, 16 * starts[u] + first * 8 * sizes[u])
-        size = 4 * sizes[u]
-        return halve(
-            part_of(wide_in, u, 8, (1 - second) * size, size),
-            part_of(deep_in, u, 4, 0, size),
-            u,
-            2,
-            flip_second,
-        )
-
-    def line_copy(u, k):
-        plane_to = lax.rem(z + k, 4)
-        return pltpu.make_async_remote_copy(
-            src_ref=part_of(deep_in, u, 4, plane_to * sizes[u], sizes[u]),
-            dst_ref=part_of(line_in, u, 4, z * sizes[u], sizes[u]),
-            send_sem=line_send.at[u, k],
-            recv_sem=line_recv.at[u, k],
-            device_id=(plane_to * 8 + spot,),
-            device_id_type=MESH,
-        )
-
-    def scatter_three(u, copy):
-        copy.wait()
-        _, second, _, _ = places(u)
-        add_to(deep_in, u, 4, wide_in, 8 * starts[u] + second * 4 * sizes[u])
-        for k in (3, 2, 1):
-            line_copy(u, k).start()
-        here = lines(4 * starts[u] + z * sizes[u], sizes[u])
-        line_in[here, :] = deep_in[here, :]
-
-    groups = (edges[2] + TAIL) // 16
-    spare = (groups - 1) // 32
-    passes = []
-
-    def land(local, group, to, slot, index):
-        source = sum_low.at[lines(local * GROUP, GROUP)]
-        target = landed.at[lines(slot * GROUP, GROUP)]
-        copy = pltpu.make_async_remote_copy(
-            src_ref=source,
-            dst_ref=target,
-            send_sem=pass_send.at[index],
-            recv_sem=land_recv.at[slot],
-            device_id=(to,),
-            device_id_type=MESH,
-        )
-        return copy, source, target
-
-    def pass_on(u):
-        for m in range(units[u][1]):
-            local = starts[u] // GROUP + m
-            group = own_group(u) + m
-            to, slot = lax.div(group, spare), lax.rem(group, spare)
-            for halo in range(2):
-                index = 2 * local + halo
-                if halo:
-                    receiver, at = lax.rem(to + 31, 32), spare
-                    wanted = jnp.logical_and(slot == 0, group > 0)
-                else:
-                    receiver, at, wanted = to, slot, group >= 0
-                away = jnp.logical_and(wanted, receiver != me)
-                here = jnp.logical_and(wanted, receiver == me)
-                copy, source, target = land(local, group, receiver, at, index)
-
-                @pl.when(away)
-                def _():
-                    copy.start()
-
-                @pl.when(here)
-                def _():
-                    target[...] = source[...]
-
-                passes.append((away, copy))
-
-    def flat_rows(row, q, values, ref):
-        ref[pl.ds(row * 4 + q, 8, stride=4), :] = values
-
-    def old_rows(u, cc):
-        matrix = units[u][4][cc]
-        base = edges[matrix - 1] if matrix else 0
-        return (one_hbm, two_hbm, short_hbm)[matrix], 16 * own_group(u) - base, 16 * units[u][1]
-
-    def own_fetch(u):
-        target = own_weight.at[pl.ds(starts[u] // 4, 16 * units[u][1])]
-        matrices = units[u][4]
-        for cc in range(2):
-            if cc and matrices[0] == matrices[1]:
-                continue
-
-            @pl.when((core == cc) if matrices[0] != matrices[1] else (core >= 0))
-            def _():
-                ref, row, count = old_rows(u, cc)
-                pltpu.make_async_copy(
-                    ref.at[pl.ds(pl.multiple_of(row, 16), count)], target, fetch_sem.at[9 + u]
-                ).start()
-
-    def spread_copy(u, k):
-        own = out_ref.at[lines(own_group(u) * GROUP, sizes[u])]
-        return pltpu.make_async_remote_copy(
-            src_ref=own,
-            dst_ref=own,
-            send_sem=spread_send.at[u, k],
-            recv_sem=spread_recv.at[u, k],
-            device_id=(far[k - 1],),
-            device_id_type=MESH,
-        )
-
-    def own_block(u):
-        size = sizes[u]
-        for k in range(1, 4):
-            line_copy(u, k).wait_recv()
-        here = pl.ds(starts[u], size)
-        low_sum = functools.reduce(
-            lambda a, b: a + b,
-            [line_in[pl.ds(4 * starts[u] + t * size, size), :].astype(f32) for t in range(4)],
-        ).astype(low)
-        sum_low[here, :] = low_sum
-        total[here, :] = low_sum.astype(f32)
-        target = own_weight.at[pl.ds(starts[u] // 4, 16 * units[u][1])]
-        pltpu.make_async_copy(target, target, fetch_sem.at[9 + u]).wait()
-        matrices = units[u][4]
-        scale = jnp.where(core == 0, scales[matrices[0]], scales[matrices[1]])
-        for m in range(units[u][1]):
-            row = starts[u] // 4 + 16 * m
-            for part in (0, 8):
-                for q in range(4):
-                    summed = total[pl.ds(row * 4 + 16 * q + part, 8), :]
-                    old = own_weight[pl.ds(row + part, 8), 128 * q : 128 * (q + 1)]
-                    fresh = old - scale * jnp.tanh(summed * root)
-                    flat_rows(row + part, q, fresh, new_flat)
-        out_ref[lines(own_group(u) * GROUP, size), :] = new_flat[here, :].astype(low)
-        for k in (3, 2, 1):
-            spread_copy(u, k).start()
-        pass_on(u)
-
-    def piece(rows, u, stage, partner):
-        return send(
-            out_ref.at[rows], out_ref.at[rows], ag_send.at[u, stage], ag_recv.at[u, stage], partner
-        )
-
-    def gather_one(u):
-        for k in range(1, 4):
-            spread_copy(u, k).wait_recv()
-        first, second, _, flip_second = places(u)
-        size = 4 * sizes[u]
-        start = unit_start(u, core) + (2 * first + second) * size
-        return piece(lines(start, size), u, 0, flip_second)
-
-    def gather_two(u, copy):
-        copy.wait()
-        first, _, flip_first, _ = places(u)
-        size = 8 * sizes[u]
-        return piece(lines(unit_start(u, core) + first * size, size), u, 1, flip_first)
-
-    def gather_three(u, copy):
-        copy.wait()
-        pl.semaphore_wait(free_sem.at[u], 1)
-        return piece(lines(unit_start(u, core), 16 * sizes[u]), u, 2, flip_core)
-
-    def renew(row, at_row):
-        scale = scale_of(at_row, [scales[k] for k in range(3)], edges)
-        for part in (0, 8):
-            for q in range(4):
-                summed = total[pl.ds(row * 4 + 16 * q + part, 8), :]
-                old = weight[pl.ds(row + part, 8), 128 * q : 128 * (q + 1)]
-                fresh = old - scale * jnp.tanh(summed * root)
-                flat_rows(row + part, q, summed, vote_flat)
-                flat_rows(row + part, q, fresh, new_flat)
-
     valid_column = column_of(valid_ref[...].astype(f32), slots)
     weight_slot = jnp.broadcast_to(valid_column, (slots, width))
     weight_band = jnp.concatenate([weight_slot] * side, axis=0)
@@ -758,11 +472,6 @@
     scales[2] = scale_from(square[...], grad_short.size)
     for fetch in fetch_two:
         fetch.start()
-    for k in range(OWN // PIECE):
-        fetch_rows(first_row + k * PIECE, PIECE, k * PIECE, fetch_sem.at[7])
-    fetch_rows(first_row + OWN, TAIL, OWN, fetch_sem.at[8])
-    for u in range(len(units)):
-        own_fetch(u)
 
     def image_taps(j):
         pieces = []
@@ -807,7 +516,7 @@
         side_sums = add_up(side_sums, moments(value))
 
     count = jnp.broadcast_to(jnp.sum(valid_column, axis=0, keepdims=True), (1, width))
-    pl.semaphore_wait(barrier, len(others))
+    pl.semaphore_wait(barrier, len(near) + len(far))
     copies = exchange_start(
         0, pack_rows(main_sums + side_sums + [count])
     )
@@ -928,10 +637,7 @@
                 left, right.reshape(-1, width), preferred_element_type=f32
             )
 
-    def nothing():
-        pass
-
-    def matrix_votes(k, grad, between, after):
+    def matrix_votes(k, grad):
         here = pl.ds(k * width, width)
         start = edges[k - 1] if k else 0
         col_new[:, here] = factored_votes(
@@ -942,36 +648,13 @@
             row_new,
             col_ref[:, here],
             level,
-            out_ref,
+            votes_ref,
             start,
-            between,
-            after,
-        )
-
-    in_flight = {}
-    steps = (
-        lambda u, copy: scatter_start(u),
-        scatter_one,
-        scatter_two,
-        scatter_three,
-        lambda u, copy: own_block(u),
-        lambda u, copy: gather_one(u),
-        gather_two,
-        gather_three,
-    )
-
-    def go(number, u):
-        in_flight[u] = steps[number](u, in_flight.get(u))
-
-    def turn(number):
-        for step_number, u in SCHEDULE[number]:
-            go(step_number, u)
-
-    early = edges[1] // 512 - edges[0] // 512
-    matrix_votes(1, grad_two, (nothing, nothing), lambda k: go(0, k))
-    turn(0)
+        )
+
     grad_short[...] = jnp.dot(xs_t[0, 0], back_side[...], preferred_element_type=f32)
-    matrix_votes(2, grad_short, (nothing, nothing), lambda k: None)
+    matrix_votes(2, grad_short)
+    matrix_votes(1, grad_two)
 
     gain_one, shift_one = none, none
     for j in range(side):
@@ -997,7 +680,6 @@
             grad * ((before - mean_one) * inv_one), axis=0, keepdims=True
         )
         back_one[j, :side] = (grad * slope_one).astype(low).reshape(side, slots, width)
-        turn(1 + j)
 
     square_head = grad_head * grad_head + EPS_ROW
     real = lax.broadcasted_iota(jnp.int32, square_head.shape, 0) < classes
@@ -1052,21 +734,340 @@
             )
         if b == 1:
             copies = exchange_middle(2, copies)
-        turn(5 + b)
-
-    matrix_votes(
-        0,
-        grad_one,
-        (lambda: turn(8), lambda: turn(9)),
-        lambda k: go(0, early + k),
-    )
-    last_turn = SCHEDULE[10]
+
+    matrix_votes(0, grad_one)
+    tail_ref[...] = exchange_end(2, copies)
+    scale_ref[...] = jnp.concatenate(
+        [jnp.broadcast_to(scales[k], (1, 128)) for k in range(5)]
+        + [jnp.zeros((3, 128), f32)],
+        axis=0,
+    )
+
+
+def share_kernel(
+    edges,
+    units,
+    root,
+    votes_ref,
+    tail_ref,
+    scale_ref,
+    one_hbm,
+    two_hbm,
+    short_hbm,
+    head_ref,
+    norm_ref,
+    new_ref,
+    vote_ref,
+    out_ref,
+    loss_ref,
+    core_in,
+    wide_in,
+    deep_in,
+    line_in,
+    sum_low,
+    landed,
+    total,
+    own_weight,
+    weight,
+    vote_flat,
+    new_flat,
+    fetch_sem,
+    rs_send,
+    rs_recv,
+    line_send,
+    line_recv,
+    pass_send,
+    land_recv,
+    spread_send,
+    spread_recv,
+    ag_send,
+    ag_recv,
+):
+    width = norm_ref.shape[1]
+    classes = head_ref.shape[0]
+    low = jnp.bfloat16
+    f32 = jnp.float32
+
+    me, core, x, y, z = place()
+    flip_core = me + 1 - 2 * core
+    flip_x = me + 2 - 4 * x
+    flip_y = me + 4 - 8 * y
+    spot = lax.rem(me, 8)
+    far = [lax.rem(z + k, 4) * 8 + spot for k in range(1, 4)]
+    others = [lax.rem(me + k, 32) for k in range(1, 32)]
+    barrier = pltpu.get_barrier_semaphore()
+    for partner in others:
+        pl.semaphore_signal(barrier, inc=1, device_id=(partner,), device_id_type=MESH)
+    scales = [scale_ref[k : k + 1, :1] for k in range(5)]
+
+    def fetch_rows(row, count, place_at, sem):
+        parts = (
+            (one_hbm, 0, edges[0]),
+            (two_hbm, edges[0], edges[1]),
+            (short_hbm, edges[1], edges[2]),
+        )
+        for ref, first, last in parts:
+
+            @pl.when(jnp.logical_and(row >= first, row < last))
+            def _():
+                start = pl.multiple_of(row - first, count)
+                pltpu.make_async_copy(
+                    ref.at[pl.ds(start, count)], weight.at[pl.ds(place_at, count)], sem
+                ).start()
+
+    first_row = me * OWN
+
+    def lines(start, count):
+        return pl.ds(pl.multiple_of(start, 16), count)
+
+    sizes = [GROUP * unit[1] for unit in units]
+    starts = [sum(sizes[:k]) for k in range(len(units) + 1)]
+
+    def part_of(ref, u, share, start, count):
+        return ref.at[lines(share * starts[u] + start, count)]
+
+    def places(u):
+        if units[u][2]:
+            return x, y, flip_x, flip_y
+        return y, x, flip_y, flip_x
+
+    def unit_start(u, cc):
+        return GROUP * units[u][0] + cc * (GROUP * units[u][3])
+
+    def own_group(u):
+        first, second, _, _ = places(u)
+        return units[u][0] + core * units[u][3] + (first * 8 + second * 4 + z) * units[u][1]
+
+    def halve(source, target, u, stage, partner):
+        return send(source, target, rs_send.at[u, stage], rs_recv.at[u, stage], partner)
+
+    def scatter_start(u):
+        size = 16 * sizes[u]
+        return halve(
+            votes_ref.at[lines(unit_start(u, 1 - core), size)],
+            part_of(core_in, u, 16, 0, size),
+            u,
+            0,
+            flip_core,
+        )
+
+    def add_to(ref, u, share, source_ref, source_start):
+        size = share * sizes[u]
+        here = lines(share * starts[u], size)
+        ref[here, :] = ref[here, :] + source_ref[lines(source_start, size), :]
+
+    def scatter_one(u, copy):
+        copy.wait()
+        add_to(core_in, u, 16, votes_ref, unit_start(u, core))
+        first, _, flip_first, _ = places(u)
+        size = 8 * sizes[u]
+        return halve(
+            part_of(core_in, u, 16, (1 - first) * size, size),
+            part_of(wide_in, u, 8, 0, size),
+            u,
+            1,
+            flip_first,
+        )
+
+    def scatter_two(u, copy):
+        copy.wait()
+        first, second, _, flip_second = places(u)
+        add_to(wide_in, u, 8, core_in, 16 * starts[u] + first * 8 * sizes[u])
+        size = 4 * sizes[u]
+        return halve(
+            part_of(wide_in, u, 8, (1 - second) * size, size),
+            part_of(deep_in, u, 4, 0, size),
+            u,
+            2,
+            flip_second,
+        )
+
+    def line_copy(u, k):
+        plane_to = lax.rem(z + k, 4)
+        return pltpu.make_async_remote_copy(
+            src_ref=part_of(deep_in, u, 4, plane_to * sizes[u], sizes[u]),
+            dst_ref=part_of(line_in, u, 4, z * sizes[u], sizes[u]),
+            send_sem=line_send.at[u, k],
+            recv_sem=line_recv.at[u, k],
+            device_id=(plane_to * 8 + spot,),
+            device_id_type=MESH,
+        )
+
+    def scatter_three(u, copy):
+        copy.wait()
+        _, second, _, _ = places(u)
+        add_to(deep_in, u, 4, wide_in, 8 * starts[u] + second * 4 * sizes[u])
+        for k in (3, 2, 1):
+            line_copy(u, k).start()
+        here = lines(4 * starts[u] + z * sizes[u], sizes[u])
+        line_in[here, :] = deep_in[here, :]
+
+    groups = (edges[2] + TAIL) // 16
+    spare = (groups - 1) // 32
+    passes = []
+
+    def land(local, group, to, slot, index):
+        source = sum_low.at[lines(local * GROUP, GROUP)]
+        target = landed.at[lines(slot * GROUP, GROUP)]
+        copy = pltpu.make_async_remote_copy(
+            src_ref=source,
+            dst_ref=target,
+            send_sem=pass_send.at[index],
+            recv_sem=land_recv.at[slot],
+            device_id=(to,),
+            device_id_type=MESH,
+        )
+        return copy, source, target
+
+    def pass_on(u):
+        for m in range(units[u][1]):
+            local = starts[u] // GROUP + m
+            group = own_group(u) + m
+            to, slot = lax.div(group, spare), lax.rem(group, spare)
+            for halo in range(2):
+                index = 2 * local + halo
+                if halo:
+                    receiver, at = lax.rem(to + 31, 32), spare
+                    wanted = jnp.logical_and(slot == 0, group > 0)
+                else:
+                    receiver, at, wanted = to, slot, group >= 0
+                away = jnp.logical_and(wanted, receiver != me)
+                here = jnp.logical_and(wanted, receiver == me)
+                copy, source, target = land(local, group, receiver, at, index)
+
+                @pl.when(away)
+                def _():
+                    copy.start()
+
+                @pl.when(here)
+                def _():
+                    target[...] = source[...]
+
+                passes.append((away, copy))
+
+    def flat_rows(row, q, values, ref):
+        ref[pl.ds(row * 4 + q, 8, stride=4), :] = values
+
+    def old_rows(u, cc):
+        matrix = units[u][4][cc]
+        base = edges[matrix - 1] if matrix else 0
+        return (one_hbm, two_hbm, short_hbm)[matrix], 16 * own_group(u) - base, 16 * units[u][1]
+
+    def own_fetch(u):
+        target = own_weight.at[pl.ds(starts[u] // 4, 16 * units[u][1])]
+        matrices = units[u][4]
+        for cc in range(2):
+            if cc and matrices[0] == matrices[1]:
+                continue
+
+            @pl.when((core == cc) if matrices[0] != matrices[1] else (core >= 0))
+            def _():
+                ref, row, count = old_rows(u, cc)
+                pltpu.make_async_copy(
+                    ref.at[pl.ds(pl.multiple_of(row, 16), count)], target, fetch_sem.at[2 + u]
+                ).start()
+
+    def spread_copy(u, k):
+        own = out_ref.at[lines(own_group(u) * GROUP, sizes[u])]
+        return pltpu.make_async_remote_copy(
+            src_ref=own,
+            dst_ref=own,
+            send_sem=spread_send.at[u, k],
+            recv_sem=spread_recv.at[u, k],
+            device_id=(far[k - 1],),
+            device_id_type=MESH,
+        )
+
+    def own_block(u):
+        size = sizes[u]
+        for k in range(1, 4):
+            line_copy(u, k).wait_recv()
+        here = pl.ds(starts[u], size)
+        low_sum = functools.reduce(
+            lambda a, b: a + b,
+            [line_in[pl.ds(4 * starts[u] + t * size, size), :].astype(f32) for t in range(4)],
+        ).astype(low)
+        sum_low[here, :] = low_sum
+        total[here, :] = low_sum.astype(f32)
+        target = own_weight.at[pl.ds(starts[u] // 4, 16 * units[u][1])]
+        pltpu.make_async_copy(target, target, fetch_sem.at[2 + u]).wait()
+        matrices = units[u][4]
+        scale = jnp.where(core == 0, scales[matrices[0]], scales[matrices[1]])
+        for m in range(units[u][1]):
+            row = starts[u] // 4 + 16 * m
+            for part in (0, 8):
+                for q in range(4):
+                    summed = total[pl.ds(row * 4 + 16 * q + part, 8), :]
+                    old = own_weight[pl.ds(row + part, 8), 128 * q : 128 * (q + 1)]
+                    fresh = old - scale * jnp.tanh(summed * root)
+                    flat_rows(row + part, q, fresh, new_flat)
+        out_ref[lines(own_group(u) * GROUP, size), :] = new_flat[here, :].astype(low)
+        for k in (3, 2, 1):
+            spread_copy(u, k).start()
+        pass_on(u)
+
+    def piece(rows, u, stage, partner):
+        return send(
+            out_ref.at[rows], out_ref.at[rows], ag_send.at[u, stage], ag_recv.at[u, stage], partner
+        )
+
+    def gather_one(u):
+        for k in range(1, 4):
+            spread_copy(u, k).wait_recv()
+        first, second, _, flip_second = places(u)
+        size = 4 * sizes[u]
+        start = unit_start(u, core) + (2 * first + second) * size
+        return piece(lines(start, size), u, 0, flip_second)
+
+    def gather_two(u, copy):
+        copy.wait()
+        first, _, flip_first, _ = places(u)
+        size = 8 * sizes[u]
+        return piece(lines(unit_start(u, core) + first * size, size), u, 1, flip_first)
+
+    def gather_three(u, copy):
+        copy.wait()
+        return piece(lines(unit_start(u, core), 16 * sizes[u]), u, 2, flip_core)
+
+    def renew(row, at_row):
+        scale = scale_of(at_row, [scales[k] for k in range(3)], edges)
+        for part in (0, 8):
+            for q in range(4):
+                summed = total[pl.ds(row * 4 + 16 * q + part, 8), :]
+                old = weight[pl.ds(row + part, 8), 128 * q : 128 * (q + 1)]
+                fresh = old - scale * jnp.tanh(summed * root)
+                flat_rows(row + part, q, summed, vote_flat)
+                flat_rows(row + part, q, fresh, new_flat)
+
+    in_flight = {}
+    steps = (
+        lambda u, copy: scatter_start(u),
+        scatter_one,
+        scatter_two,
+        scatter_three,
+        lambda u, copy: own_block(u),
+        lambda u, copy: gather_one(u),
+        gather_two,
+        gather_three,
+    )
+
+    def go(number, u):
+        in_flight[u] = steps[number](u, in_flight.get(u))
+
+    for k in range(OWN // PIECE):
+        fetch_rows(first_row + k * PIECE, PIECE, k * PIECE, fetch_sem.at[0])
+    fetch_rows(first_row + OWN, TAIL, OWN, fetch_sem.at[1])
+    for u in range(len(units)):
+        own_fetch(u)
+    pl.semaphore_wait(barrier, len(others))
+
+    last_turn = SCHEDULE
     cut = [k for k, (number, _) in enumerate(last_turn) if number == 4][-1] + 1
     ending = len(last_turn) - 3
     for number, u in last_turn[:cut]:
         go(number, u)
 
-    sums = exchange_end(2, copies)
+    sums = tail_ref[...]
     loss_ref[...] = sums[4 * TAIL : 4 * TAIL + 1, :1]
     old = jnp.concatenate([head_ref[...], norm_ref[...]], axis=0)
     is_head = lax.broadcasted_iota(jnp.int32, (TAIL, width), 0) < classes
@@ -1113,7 +1114,7 @@
             land(0, group, me, slot, 0)[0].wait_recv()
 
     pltpu.make_async_copy(
-        weight.at[pl.ds(0, OWN)], weight.at[pl.ds(0, OWN)], fetch_sem.at[7]
+        weight.at[pl.ds(0, OWN)], weight.at[pl.ds(0, OWN)], fetch_sem.at[0]
     ).wait()
     total[pl.ds(0, SPAN), :] = landed[pl.ds(0, SPAN), :].astype(f32)
 
@@ -1125,7 +1126,7 @@
     @pl.when(me < 31)
     def _():
         pltpu.make_async_copy(
-            weight.at[pl.ds(OWN, TAIL)], weight.at[pl.ds(OWN, TAIL)], fetch_sem.at[8]
+            weight.at[pl.ds(OWN, TAIL)], weight.at[pl.ds(OWN, TAIL)], fetch_sem.at[1]
         ).wait()
         total[pl.ds(SPAN, GROUP), :] = landed[pl.ds(SPAN, GROUP), :].astype(f32)
         renew(OWN, first_row + OWN)
@@ -1197,36 +1198,29 @@
     )(*held, *values[-2:])
 
 
-def run_step(images, conv_one, conv_two, shortcut, head, norm_params, valid, labels, rows, cols, moment):
+def run_worker(images, conv_one, conv_two, shortcut, head, norm_params, valid, labels, rows, cols, moment):
     vmem = pl.BlockSpec(memory_space=pltpu.VMEM)
     hbm = pl.BlockSpec(memory_space=pl.ANY)
     low, f32 = jnp.bfloat16, jnp.float32
     dma = pltpu.SemaphoreType.DMA
-    workers = lax.axis_size("dp")
     slots, in_width = valid.shape[1], images.shape[1]
     width = conv_one.shape[1]
     pixels = images.shape[0] // 4
     shape = pltpu.VMEM
-    edges = [conv_one.shape[0]]
-    edges.append(edges[0] + conv_two.shape[0])
-    edges.append(edges[1] + shortcut.shape[0])
-    units = make_units(edges)
-    flat = (edges[2] + TAIL) * width // 128
-    share = flat // workers
+    edges = edges_of(conv_one, conv_two, shortcut)
     return pl.pallas_call(
-        functools.partial(step_kernel, tuple(edges), tuple(units), 1.0 / math.sqrt(workers)),
+        functools.partial(worker_kernel, edges),
         out_shape=(
-            shape((share, 128), f32),
-            shape((share, 128), f32),
-            shape((flat, 128), low),
+            shape((edges[2] * 4, 128), low),
+            shape((GROUP + 8, 128), f32),
+            shape((8, 128), f32),
             shape(rows.shape, f32),
             shape(cols.shape, f32),
             shape(moment.shape, f32),
             jax.ShapeDtypeStruct((1, 1), f32),
-            jax.ShapeDtypeStruct((1, 1), f32),
         ),
         in_specs=[hbm] * 4 + [vmem] * 7,
-        out_specs=(vmem,) * 8,
+        out_specs=(vmem,) * 7,
         scratch_shapes=[
             pltpu.VMEM((2, 4, 2, 4, slots, in_width), low),
             pltpu.VMEM(conv_one.shape, f32),
@@ -1247,6 +1241,7 @@
             pltpu.VMEM((128, width), f32),
             pltpu.VMEM((conv_two.shape[0], 128), f32),
             pltpu.VMEM((8, width), f32),
+            pltpu.VMEM((2 * images.shape[0], 128), low),
             pltpu.VMEM((24, 128), f32),
             pltpu.VMEM((8, 24, 128), f32),
             pltpu.VMEM((4, 24, 128), f32),
@@ -1256,6 +1251,42 @@
             pltpu.VMEM((GROUP + 8, 128), f32),
             pltpu.VMEM((8, GROUP + 8, 128), f32),
             pltpu.VMEM((4, GROUP + 8, 128), f32),
+            dma((7,)),
+            dma((3, 10)),
+            dma((3, 10)),
+            dma((2,)),
+        ],
+        compiler_params=pltpu.CompilerParams(
+            collective_id=1, has_side_effects=True, vmem_limit_bytes=50 * 1024 * 1024
+        ),
+        name="worker",
+    )(images, conv_one, conv_two, shortcut, head, norm_params, valid, labels, rows, cols, moment)
+
+
+def run_share(votes, tail, scales, conv_one, conv_two, shortcut, head, norm_params):
+    vmem = pl.BlockSpec(memory_space=pltpu.VMEM)
+    hbm = pl.BlockSpec(memory_space=pl.ANY)
+    low, f32 = jnp.bfloat16, jnp.float32
+    dma = pltpu.SemaphoreType.DMA
+    workers = lax.axis_size("dp")
+    width = conv_one.shape[1]
+    shape = pltpu.VMEM
+    edges = edges_of(conv_one, conv_two, shortcut)
+    units = tuple(make_units(edges))
+    flat = (edges[2] + TAIL) * width // 128
+    share = flat // workers
+    held = [pltpu.with_memory_space_constraint(value, pltpu.VMEM) for value in (votes, tail, scales)]
+    return pl.pallas_call(
+        functools.partial(share_kernel, edges, units, 1.0 / math.sqrt(workers)),
+        out_shape=(
+            shape((share, 128), f32),
+            shape((share, 128), f32),
+            shape((flat, 128), low),
+            jax.ShapeDtypeStruct((1, 1), f32),
+        ),
+        in_specs=[vmem] * 3 + [hbm] * 3 + [vmem] * 2,
+        out_specs=(vmem,) * 4,
+        scratch_shapes=[
             pltpu.VMEM((16 * SPAN, 128), low),
             pltpu.VMEM((8 * SPAN, 128), low),
             pltpu.VMEM((4 * SPAN, 128), low),
@@ -1267,9 +1298,7 @@
             pltpu.VMEM((OWN + TAIL, width), f32),
             pltpu.VMEM((SPAN + GROUP, 128), f32),
             pltpu.VMEM((SPAN + GROUP, 128), f32),
-            dma((9 + len(units),)),
-            dma((3, 10)),
-            dma((3, 10)),
+            dma((2 + len(units),)),
             dma((len(units), 3)),
             dma((len(units), 3)),
             dma((len(units), 4)),
@@ -1280,14 +1309,16 @@
             dma((len(units), 4)),
             dma((len(units), 3)),
             dma((len(units), 3)),
-            pltpu.SemaphoreType.REGULAR((len(units),)),
-            dma((2,)),
         ],
         compiler_params=pltpu.CompilerParams(
-            collective_id=1, has_side_effects=True, vmem_limit_bytes=54 * 1024 * 1024
+            collective_id=2, has_side_effects=True, vmem_limit_bytes=20 * 1024 * 1024
         ),
-        name="step",
-    )(images, conv_one, conv_two, shortcut, head, norm_params, valid, labels, rows, cols, moment)
+        name="share",
+    )(*held, conv_one, conv_two, shortcut, head, norm_params)
+
+
+def edges_of(*weights):
+    return tuple(sum(weight.shape[0] for weight in weights[: k + 1]) for k in range(3))
 
 
 def scale_for(weight):
@@ -1432,18 +1463,22 @@
     col_state,
     bn_moment,
 ):
-    new_mine, vote_mine, copies, rows_new, cols_new, moment_new, loss_sum, valid_count = run_step(
+    head = classifier.T
+    votes, tail, scales, rows_new, cols_new, moment_new, valid_count = run_worker(
         images.reshape(-1, images.shape[-1]),
         conv_one,
         conv_two,
         shortcut,
-        classifier.T,
+        head,
         norm_params,
         valid_slot.reshape(1, -1),
         labels.reshape(1, -1),
         row_state,
         col_state,
         bn_moment,
+    )
+    new_mine, vote_mine, copies, loss_sum = run_share(
+        votes, tail, scales, conv_one, conv_two, shortcut, head, norm_params
     )
     copies, new_mine, vote_mine, rows_new, cols_new, moment_new, loss_sum, valid_count = finish(
         (copies, new_mine, vote_mine, rows_new, cols_new, moment_new, loss_sum, valid_count)

time: 157 us -> 174 us (1.11)
  Pallas kernels: 156 us -> 169 us
  local copies, waits for them, and re-layouts: 0 us -> 3.69 us
    pallas_call x1 -> x2, Pallas kernels: 151 us -> 163 us  [the longest x1 102 us: run_share(): pl.pallas_call(functools.partial(share_kernel, edges, units, 1.0 / math.s...]
    unnamed x0 -> x10, local copies, waits for them, and re-layouts: none -> 3.69 us
where the time goes in v7:
time: 174 us; the launch traced here: 173 us
  Pallas kernels  169 us (97%)
  local copies, waits for them, and re-layouts  3.69 us (2%)
    pallas_call x1, Pallas kernels, run_share(): pl.pallas_call(functools.partial(share_kernel, edges, units, 1.0 / math.s...  102 us
    pallas_call x1, Pallas kernels, run_worker(): pl.pallas_call(functools.partial(worker_kernel, edges), out_shape=(shape(...  61.2 us
    pallas_call x1, Pallas kernels, finish(): pl.pallas_call(functools.partial(finish_kernel, count, chunks), out_shape...  5.15 us
    unnamed x10, local copies, waits for them, and re-layouts  3.69 us

profile of v7, /device:TPU:0, one launch (start us, length us, event | category | flops | bytes accessed | tf_op | source)
XLA Modules:
  0.0 173.1 jit_solution(2441733797467117928)
XLA Ops:
  0.6 0.0 copy-start.1
  0.6 0.0 copy-start.2
  0.7 0.0 copy-start.3
  0.7 0.0 copy-start.4
  0.7 61.2 %worker.1 = (bf16[28672,128]{1,0:T(8,128)(2,1)S(1)}, f32[72,128]{1,0:T(8,128)S(1)}, f32[8,128]{1,0:T(8,128)S(1)}, f32[1,7680]{1,0:T(1,128)S(1)}, f32[1,1546]{1,0...) custom-call(bf16[4096,256]{1,0:T(8,128)(2,1)} %bitcast.11, f32[2304,512]{1,0:T(8,128)} %one_hbm.3, ...), custom_call_target="tpu_custom_call" | custom-call | tf_op jit(solution)/shard_map/worker/pallas_call | solution.py:1211
  61.8 0.0 copy-done.1
  61.9 0.0 copy-done.2
  61.9 0.0 copy-done.3
  61.9 0.0 copy-done.4
  61.9 0.0 copy-start
  61.9 3.7 %copy-done = f32[4608,512]{1,0:T(8,128)S(1)} copy-done((f32[4608,512]{1,0:T(8,128)S(1)}, f32[4608,512]{1,0:T(8,128)}, u32[]{:S(2)}) %copy-start) | copy-done | bytes 9437208
  65.6 102.2 %share.1 = (f32[898,128]{1,0:T(8,128)S(1)}, f32[898,128]{1,0:T(8,128)S(1)}, bf16[28736,128]{1,0:T(8,128)(2,1)S(1)}, f32[1,1]{1,0:T(1,128)}) custom-call(bf16[28672,128]{1,0:T(8,128)(2,1)S(1)} %get-tuple-element.27.votes_ref, f32[72,128]{1,0:T(8,128)S(1)} %get-tuple-element.28.tail_ref, f32[8,128]{1,0:T(8,128)S(1)} %get-tuple-element.29.scale_ref, ...), custom_call_target="tpu_custom_call" | custom-call | tf_op jit(solution)/shard_map/share/pallas_call | solution.py:1279
  167.8 5.1 %finish.1 = (bf16[28736,128]{1,0:T(8,128)(2,1)}, f32[898,128]{1,0:T(8,128)}, f32[898,128]{1,0:T(8,128)}, f32[1,7680]{1,0:T(1,128)}, f32[1,1546]{1,0:T(1,128)}, /...) custom-call(bf16[28736,128]{1,0:T(8,128)(2,1)S(1)} %get-tuple-element.30.refs_0_, ...), custom_call_target="tpu_custom_call" | custom-call | tf_op jit(solution)/shard_map/finish/pallas_call | solution.py:1190
Async XLA Ops:
  0.6 61.2 %copy-start.1 = (f32[2304,512]{1,0:T(8,128)S(1)}, f32[2304,512]{1,0:T(8,128)}, u32[]{:S(2)}) copy-start(f32[2304,512]{1,0:T(8,128)} %one_hbm.3) | copy-start | bytes 14155780
  0.6 61.2 %copy-start.2 = (f32[256,512]{1,0:T(8,128)S(1)}, f32[256,512]{1,0:T(8,128)}, u32[]{:S(2)}) copy-start(f32[256,512]{1,0:T(8,128)} %short_hbm.3) | copy-start | bytes 1572868
  0.7 61.2 %copy-start.3 = (f32[512,10]{0,1:T(8,128)S(1)}, f32[512,10]{0,1:T(8,128)}, u32[]{:S(2)}) copy-start(f32[512,10]{0,1:T(8,128)} %param.17) | copy-start | bytes 61444
  0.7 61.2 %copy-start.4 = (f32[6,512]{1,0:T(8,128)S(1)}, f32[6,512]{1,0:T(8,128)}, u32[]{:S(2)}) copy-start(f32[6,512]{1,0:T(8,128)} %norm_ref.3) | copy-start | bytes 36868
  61.9 3.7 %copy-start = (f32[4608,512]{1,0:T(8,128)S(1)}, f32[4608,512]{1,0:T(8,128)}, u32[]{:S(2)}) copy-start(f32[4608,512]{1,0:T(8,128)} %two_hbm.3) | copy-start | bytes 28311556

commit v8 on v6

--- a/solution.py
+++ b/solution.py
@@ -118,27 +118,39 @@
 
 SCHEDULE = (
     (),
-    (),
+    (
+        (1, 0),
+    ),
+    (
+        (0, 2), (1, 1),
+    ),
+    (
+        (0, 3), (1, 2), (2, 0), (0, 4), (1, 3), (2, 1),
+    ),
+    (
+        (0, 5), (1, 4), (2, 2), (3, 0),
+    ),
+    (
+        (0, 6), (1, 5), (2, 3), (3, 1),
+    ),
+    (
+        (0, 7), (1, 6), (2, 4), (3, 2), (4, 0),
+    ),
     (),
     (
-        (1, 0), (1, 1), (1, 3), (1, 4), (1, 5), (1, 7), (1, 2),
+        (0, 8), (1, 7), (2, 5), (3, 3), (4, 1),
     ),
     (),
-    (),
-    (),
-    (),
-    (),
-    (),
     (
-        (1, 6), (2, 1), (2, 3), (1, 8), (2, 0), (2, 7), (1, 9), (3, 0), (1, 10), (1, 12),
-        (1, 11), (2, 2), (2, 4), (4, 0), (3, 1), (5, 0), (3, 3), (3, 2), (2, 5), (2, 6), (4, 1),
-        (1, 13), (4, 3), (3, 4), (3, 7), (3, 5), (2, 8), (5, 1), (2, 10), (2, 9), (2, 12),
-        (4, 2), (6, 0), (3, 9), (2, 11), (4, 5), (6, 1), (2, 13), (4, 7), (3, 6), (4, 4),
-        (3, 11), (3, 10), (3, 13), (5, 2), (3, 8), (5, 3), (6, 3), (6, 2), (5, 5), (4, 6),
-        (7, 0), (5, 4), (4, 9), (6, 5), (7, 1), (4, 10), (4, 8), (5, 7), (7, 3), (6, 7), (6, 4),
-        (7, 5), (4, 13), (7, 2), (5, 10), (3, 12), (4, 11), (5, 6), (5, 9), (6, 6), (4, 12),
-        (5, 8), (6, 8), (6, 9), (5, 11), (7, 7), (7, 4), (7, 9), (6, 10), (5, 12), (5, 13),
-        (6, 11), (7, 6), (7, 11), (6, 12), (7, 8), (6, 13), (7, 10), (7, 13), (7, 12),
+        (1, 8), (2, 6), (3, 4), (4, 2), (1, 9), (2, 7), (3, 5), (4, 3), (5, 0), (0, 11), (1, 10),
+        (2, 8), (3, 6), (4, 4), (5, 1), (0, 12), (1, 11), (2, 9), (3, 7), (4, 5), (5, 2), (6, 0),
+        (0, 13), (1, 12), (2, 10), (3, 8), (4, 6), (5, 3), (6, 1), (1, 13), (2, 11), (3, 9),
+        (4, 7), (8, 0), (5, 4), (6, 2), (2, 12), (3, 10), (4, 8), (5, 5), (6, 3), (7, 0),
+        (2, 13), (3, 11), (4, 9), (5, 6), (6, 4), (7, 1), (3, 12), (4, 10), (5, 7), (6, 5),
+        (7, 2), (3, 13), (4, 11), (5, 8), (6, 6), (7, 3), (4, 12), (5, 9), (6, 7), (7, 4),
+        (4, 13), (5, 10), (6, 8), (7, 5), (5, 11), (6, 9), (7, 6), (5, 12), (6, 10), (7, 7),
+        (5, 13), (6, 11), (7, 8), (6, 12), (7, 9), (6, 13), (9, 0), (7, 10), (7, 11), (7, 12),
+        (7, 13),
     ),
 )
 
@@ -948,6 +960,88 @@
             after,
         )
 
+    kept = {}
+
+    def tail_step():
+        sums = exchange_end(2, kept["tail"])
+        loss_ref[...] = sums[4 * TAIL : 4 * TAIL + 1, :1]
+        old = jnp.concatenate([head_ref[...], norm_ref[...]], axis=0)
+        is_head = lax.broadcasted_iota(jnp.int32, (TAIL, width), 0) < classes
+        scale = jnp.where(is_head, scales[3], scales[4])
+        sums = jnp.concatenate([sums[TAIL * q : TAIL * (q + 1)] for q in range(4)], axis=1)
+        fresh = old - scale * jnp.tanh(sums * root)
+        both = jnp.concatenate([sums, fresh], axis=0)
+        high = both.astype(low)
+        rest = both - high.astype(f32)
+        middle = rest.astype(low)
+        parts = jnp.concatenate([high, middle, (rest - middle.astype(f32)).astype(low)], axis=0)
+
+        flat_sums, flat_new = [], []
+        window = 256
+        for q in range(classes):
+            start = min(q * width // classes // 128 * 128, width - window)
+            down = lax.broadcasted_iota(jnp.int32, (window, width), 0)
+            across = lax.broadcasted_iota(jnp.int32, (window, width), 1)
+            gap = across - classes * down + (q * width - classes * start)
+            chosen = jnp.where(jnp.logical_and(gap >= 0, gap < classes), 1.0, 0.0).astype(low)
+            moved = jnp.dot(parts[:, start : start + window], chosen, preferred_element_type=f32)
+            moved = moved[: 2 * TAIL] + moved[2 * TAIL : 4 * TAIL] + moved[4 * TAIL :]
+            spot_of = lax.broadcasted_iota(jnp.int32, (TAIL, width), 1).astype(f32) + q * width
+            class_of = spot_of - classes * jnp.floor((spot_of + 0.5) / classes)
+            here = lax.broadcasted_iota(jnp.int32, (TAIL, width), 0).astype(f32) == class_of
+            flat_sums.append(jnp.sum(jnp.where(here, moved[:TAIL], 0.0), axis=0, keepdims=True))
+            flat_new.append(jnp.sum(jnp.where(here, moved[TAIL:], 0.0), axis=0, keepdims=True))
+        kept["sums"] = jnp.concatenate(flat_sums + [sums[classes:]], axis=0)
+        kept["new"] = jnp.concatenate(flat_new + [fresh[classes:]], axis=0)
+
+    def return_step():
+        mine = [own_group(u) for u in range(len(units))]
+        for slot in range(spare + 1):
+            group = me * spare + slot
+            own = group < 0
+            for u, unit in enumerate(units):
+                inside = jnp.logical_and(group >= mine[u], group < mine[u] + unit[1])
+                own = jnp.logical_or(own, inside)
+
+            @pl.when(jnp.logical_and(jnp.logical_not(own), group < groups - 1))
+            def _():
+                land(0, group, me, slot, 0)[0].wait_recv()
+
+        pltpu.make_async_copy(
+            weight.at[pl.ds(0, OWN)], weight.at[pl.ds(0, OWN)], fetch_sem.at[7]
+        ).wait()
+        total[pl.ds(0, SPAN), :] = landed[pl.ds(0, SPAN), :].astype(f32)
+
+        @pl.loop(0, OWN // 16)
+        def _(k):
+            row = pl.multiple_of(k * 16, 16)
+            renew(row, first_row + row)
+
+        @pl.when(me < 31)
+        def _():
+            pltpu.make_async_copy(
+                weight.at[pl.ds(OWN, TAIL)], weight.at[pl.ds(OWN, TAIL)], fetch_sem.at[8]
+            ).wait()
+            total[pl.ds(SPAN, GROUP), :] = landed[pl.ds(SPAN, GROUP), :].astype(f32)
+            renew(OWN, first_row + OWN)
+
+        def tail_rows(values, ref):
+            for u in (0, 8):
+                for q in range(4):
+                    flat_rows(OWN + u, q, values[u : u + 8, 128 * q : 128 * (q + 1)], ref)
+
+        @pl.when(me == 31)
+        def _():
+            tail_rows(kept["sums"], vote_flat)
+            tail_rows(kept["new"], new_flat)
+
+        shift = 2 * me
+        share = vote_ref.shape[0]
+        vote_ref[...] = vote_flat[pl.ds(shift, share), :]
+        new_ref[...] = new_flat[pl.ds(shift, share), :]
+        tail_rows(kept["new"], new_flat)
+        out_ref[pl.ds(32 * SPAN, GROUP), :] = new_flat[pl.ds(SPAN, GROUP), :].astype(low)
+
     in_flight = {}
     steps = (
         lambda u, copy: scatter_start(u),
@@ -958,17 +1052,21 @@
         lambda u, copy: gather_one(u),
         gather_two,
         gather_three,
+        lambda u, copy: tail_step(),
+        lambda u, copy: return_step(),
     )
 
     def go(number, u):
-        in_flight[u] = steps[number](u, in_flight.get(u))
+        got = steps[number](u, in_flight.get(u))
+        if number < 8:
+            in_flight[u] = got
 
     def turn(number):
         for step_number, u in SCHEDULE[number]:
             go(step_number, u)
 
     early = edges[1] // 512 - edges[0] // 512
-    matrix_votes(1, grad_two, (nothing, nothing), lambda k: go(0, k))
+    matrix_votes(1, grad_two, (nothing, nothing), lambda k: go(0, k) if k < 2 else None)
     turn(0)
     grad_short[...] = jnp.dot(xs_t[0, 0], back_side[...], preferred_element_type=f32)
     matrix_votes(2, grad_short, (nothing, nothing), lambda k: None)
@@ -1030,7 +1128,7 @@
     clip = jnp.maximum(1.0, jnp.sqrt(total_of(raw * raw) / raw.size))
     norm_votes = jnp.tanh(raw / clip)
     tail_votes = jnp.concatenate([head_votes, norm_votes], axis=0)
-    copies = exchange_start(
+    kept["tail"] = exchange_start(
         2,
         jnp.concatenate(
             [tail_votes[:, 128 * q : 128 * (q + 1)] for q in range(4)]
@@ -1051,104 +1149,16 @@
                 left, right.reshape(-1, width), preferred_element_type=f32
             )
         if b == 1:
-            copies = exchange_middle(2, copies)
+            kept["tail"] = exchange_middle(2, kept["tail"])
         turn(5 + b)
 
     matrix_votes(
         0,
         grad_one,
         (lambda: turn(8), lambda: turn(9)),
-        lambda k: go(0, early + k),
-    )
-    last_turn = SCHEDULE[10]
-    cut = [k for k, (number, _) in enumerate(last_turn) if number == 4][-1] + 1
-    ending = len(last_turn) - 3
-    for number, u in last_turn[:cut]:
-        go(number, u)
-
-    sums = exchange_end(2, copies)
-    loss_ref[...] = sums[4 * TAIL : 4 * TAIL + 1, :1]
-    old = jnp.concatenate([head_ref[...], norm_ref[...]], axis=0)
-    is_head = lax.broadcasted_iota(jnp.int32, (TAIL, width), 0) < classes
-    scale = jnp.where(is_head, scales[3], scales[4])
-    sums = jnp.concatenate([sums[TAIL * q : TAIL * (q + 1)] for q in range(4)], axis=1)
-    fresh = old - scale * jnp.tanh(sums * root)
-    both = jnp.concatenate([sums, fresh], axis=0)
-    high = both.astype(low)
-    rest = both - high.astype(f32)
-    middle = rest.astype(low)
-    parts = jnp.concatenate([high, middle, (rest - middle.astype(f32)).astype(low)], axis=0)
-
-    flat_sums, flat_new = [], []
-    window = 256
-    for q in range(classes):
-        start = min(q * width // classes // 128 * 128, width - window)
-        down = lax.broadcasted_iota(jnp.int32, (window, width), 0)
-        across = lax.broadcasted_iota(jnp.int32, (window, width), 1)
-        gap = across - classes * down + (q * width - classes * start)
-        chosen = jnp.where(jnp.logical_and(gap >= 0, gap < classes), 1.0, 0.0).astype(low)
-        moved = jnp.dot(parts[:, start : start + window], chosen, preferred_element_type=f32)
-        moved = moved[: 2 * TAIL] + moved[2 * TAIL : 4 * TAIL] + moved[4 * TAIL :]
-        spot_of = lax.broadcasted_iota(jnp.int32, (TAIL, width), 1).astype(f32) + q * width
-        class_of = spot_of - classes * jnp.floor((spot_of + 0.5) / classes)
-        here = lax.broadcasted_iota(jnp.int32, (TAIL, width), 0).astype(f32) == class_of
-        flat_sums.append(jnp.sum(jnp.where(here, moved[:TAIL], 0.0), axis=0, keepdims=True))
-        flat_new.append(jnp.sum(jnp.where(here, moved[TAIL:], 0.0), axis=0, keepdims=True))
-    flat_sums = jnp.concatenate(flat_sums + [sums[classes:]], axis=0)
-    flat_new = jnp.concatenate(flat_new + [fresh[classes:]], axis=0)
-
-    for number, u in last_turn[cut:ending]:
-        go(number, u)
-
-    mine = [own_group(u) for u in range(len(units))]
-    for slot in range(spare + 1):
-        group = me * spare + slot
-        own = group < 0
-        for u, unit in enumerate(units):
-            inside = jnp.logical_and(group >= mine[u], group < mine[u] + unit[1])
-            own = jnp.logical_or(own, inside)
-
-        @pl.when(jnp.logical_and(jnp.logical_not(own), group < groups - 1))
-        def _():
-            land(0, group, me, slot, 0)[0].wait_recv()
-
-    pltpu.make_async_copy(
-        weight.at[pl.ds(0, OWN)], weight.at[pl.ds(0, OWN)], fetch_sem.at[7]
-    ).wait()
-    total[pl.ds(0, SPAN), :] = landed[pl.ds(0, SPAN), :].astype(f32)
-
-    @pl.loop(0, OWN // 16)
-    def _(k):
-        row = pl.multiple_of(k * 16, 16)
-        renew(row, first_row + row)
-
-    @pl.when(me < 31)
-    def _():
-        pltpu.make_async_copy(
-            weight.at[pl.ds(OWN, TAIL)], weight.at[pl.ds(OWN, TAIL)], fetch_sem.at[8]
-        ).wait()
-        total[pl.ds(SPAN, GROUP), :] = landed[pl.ds(SPAN, GROUP), :].astype(f32)
-        renew(OWN, first_row + OWN)
-
-    def tail_rows(values, ref):
-        for u in (0, 8):
-            for q in range(4):
-                flat_rows(OWN + u, q, values[u : u + 8, 128 * q : 128 * (q + 1)], ref)
-
-    @pl.when(me == 31)
-    def _():
-        tail_rows(flat_sums, vote_flat)
-        tail_rows(flat_new, new_flat)
-
-    shift = 2 * me
-    share = vote_ref.shape[0]
-    vote_ref[...] = vote_flat[pl.ds(shift, share), :]
-    new_ref[...] = new_flat[pl.ds(shift, share), :]
-    tail_rows(flat_new, new_flat)
-    out_ref[pl.ds(32 * SPAN, GROUP), :] = new_flat[pl.ds(SPAN, GROUP), :].astype(low)
-
-    for number, u in last_turn[ending:]:
-        go(number, u)
+        lambda k: go(0, early + k) if k < 2 else None,
+    )
+    turn(10)
     for u in range(len(units)):
         in_flight[u].wait()
         for k in range(1, 4):

time: 157 us -> 138 us (0.88)
  Pallas kernels: 156 us -> 137 us
    pallas_call x1, Pallas kernels: 151 us -> 132 us  [run_step(): pl.pallas_call(functools.partial(step_kernel, tuple(edges), tuple(units),...]
where the time goes in v8:
time: 138 us
  Pallas kernels  137 us (99%)
    pallas_call x1, Pallas kernels, run_step(): pl.pallas_call(functools.partial(step_kernel, tuple(edges), tuple(units),...  132 us
    pallas_call x1, Pallas kernels, finish(): pl.pallas_call(functools.partial(finish_kernel, count, chunks), out_shape...  5.17 us

profile of v8, /device:TPU:0, one launch (start us, length us, event | category | flops | bytes accessed | tf_op | source)
XLA Modules:
  0.0 137.9 jit_solution(15457526995292533415)
XLA Ops:
  0.6 131.9 %step.1 = (f32[898,128]{1,0:T(8,128)S(1)}, f32[898,128]{1,0:T(8,128)S(1)}, bf16[28736,128]{1,0:T(8,128)(2,1)S(1)}, f32[1,7680]{1,0:T(1,128)S(1)}, f32[1,1546]{1,...) custom-call(bf16[4096,256]{1,0:T(8,128)(2,1)} %bitcast.9, f32[2304,512]{1,0:T(8,128)} %one_hbm.1, ...), custom_call_target="tpu_custom_call" | custom-call | tf_op jit(solution)/shard_map/step/pallas_call | solution.py:1226
  132.6 5.2 %finish.1 = (bf16[28736,128]{1,0:T(8,128)(2,1)}, f32[898,128]{1,0:T(8,128)}, f32[898,128]{1,0:T(8,128)}, f32[1,7680]{1,0:T(1,128)}, f32[1,1546]{1,0:T(1,128)}, /...) custom-call(bf16[28736,128]{1,0:T(8,128)(2,1)S(1)} %get-tuple-element.24.refs_0_, ...), custom_call_target="tpu_custom_call" | custom-call | tf_op jit(solution)/shard_map/finish/pallas_call | solution.py:1199

commit v9 on v8

--- a/solution.py
+++ b/solution.py
@@ -237,7 +237,7 @@
         def _(k):
             start = pl.multiple_of(k * step, step)
             values = source[pl.ds(tap * depth + start, step), :]
-            target[new_tap, pl.ds(start, step), :] = values.astype(jnp.bfloat16)
+            target[pl.ds(new_tap * depth + start, step), :] = values.astype(jnp.bfloat16)
             square_ref[...] += fold(values * values)
 
 
@@ -356,8 +356,6 @@
     side_pre,
     main_two,
     active,
-    back_two,
-    back_one,
     back_side,
     active_t,
     xs_t,
@@ -762,7 +760,6 @@
 
     valid_column = column_of(valid_ref[...].astype(f32), slots)
     weight_slot = jnp.broadcast_to(valid_column, (slots, width))
-    weight_band = jnp.concatenate([weight_slot] * side, axis=0)
 
     cast_weight(grad_one, low_one, square, 9, in_width, fetch_one)
     scales[0] = scale_from(square[...], grad_one.size)
@@ -776,52 +773,53 @@
     for u in range(len(units)):
         own_fetch(u)
 
-    def image_taps(j):
-        pieces = []
-        for b in range(3):
-            column = j if b else j - 1
-            if column < 0:
-                continue
-            across = 0 if b == 1 else 1
-            for a in range(3):
-                if a == 1:
-                    piece = xs[across, column, 0].reshape(band, in_width)
-                elif a == 2:
-                    piece = xs[across, column, 1].reshape(band, in_width)
-                else:
-                    piece = xs[across, column, 1, : side - 1].reshape(band - slots, in_width)
-                    piece = jnp.concatenate([jnp.zeros((slots, in_width), low), piece], axis=0)
-                pieces.append(piece)
-        return jnp.concatenate(pieces, axis=1)
+    def image_taps(b):
+        across, last = (0, side) if b == 1 else (1, side - 1 if b == 0 else side)
+        even = xs[across, :last, 0].reshape(-1, in_width)
+        odd = xs[across, :last, 1].reshape(-1, in_width)
+        above = []
+        for j in range(last):
+            above.append(jnp.zeros((slots, in_width), low))
+            above.append(xs[across, j, 1, : side - 1].reshape(band - slots, in_width))
+        return jnp.concatenate([jnp.concatenate(above, axis=0), even, odd], axis=1)
 
     def moments(values):
-        weighted = values * weight_band
-        return (
-            jnp.sum(weighted, axis=0, keepdims=True),
-            jnp.sum(weighted * values, axis=0, keepdims=True),
-        )
-
-    def add_up(old, new):
-        return [a + b for a, b in zip(old, new)]
-
+        count, columns = values.shape
+        values = values.reshape(count // slots, slots, columns)
+        weighted = values * weight_slot[:, :columns]
+        return [
+            jnp.sum(jnp.sum(each, axis=0), axis=0, keepdims=True)
+            for each in (weighted, weighted * values)
+        ]
+
+    def side_by_side(pairs):
+        return [jnp.concatenate(each, axis=1) for each in zip(*pairs)]
+
+    half = width // 2
+    halves = [slice(0, half), slice(half, width)]
     none = jnp.zeros((1, width), f32)
-    main_sums, side_sums = [none, none], [none, none]
-    for j in range(side):
-        here = pl.ds(j * band, band)
-        low_rows = low_one[3 if j == 0 else 0 :].reshape(-1, width)
-        value = jnp.dot(image_taps(j), low_rows, preferred_element_type=f32)
-        main_pre[here, :] = value
-        main_sums = add_up(main_sums, moments(value))
-        value = jnp.dot(
-            xs[0, j, 0].reshape(band, in_width), low_short[0], preferred_element_type=f32
-        )
-        side_pre[here, :] = value
-        side_sums = add_up(side_sums, moments(value))
+
+    def product(left, right):
+        return jnp.dot(left, right, preferred_element_type=f32)
+
+    main_sums, side_sums = [], []
+    deep = 3 * in_width
+    for cols in halves:
+        main_pre[:band, cols] = jnp.zeros((band, half), f32)
+        main_pre[band:, cols] = product(image_taps(0), low_one[:deep, cols])
+        main_pre[:, cols] += product(image_taps(1), low_one[deep : 2 * deep, cols])
+        value = main_pre[:, cols] + product(image_taps(2), low_one[2 * deep :, cols])
+        main_pre[:, cols] = value
+        main_sums.append(moments(value))
+        value = product(xs[0, :, 0].reshape(-1, in_width), low_short[:, cols])
+        side_pre[:, cols] = value
+        side_sums.append(moments(value))
+    main_sums, side_sums = side_by_side(main_sums), side_by_side(side_sums)
 
     count = jnp.broadcast_to(jnp.sum(valid_column, axis=0, keepdims=True), (1, width))
     pl.semaphore_wait(barrier, len(others))
     copies = exchange_start(
-        0, pack_rows(main_sums + side_sums + [count])
+        0, pack_rows(list(main_sums) + list(side_sums) + [count])
     )
     cast_weight(grad_two, low_two, square, 9, width, fetch_two)
     scales[1] = scale_from(square[...], grad_two.size)
@@ -834,9 +832,10 @@
     border = jnp.zeros((side, 1, slots, width), low)
     active[:, 0:1] = border
     active[:, side + 1 :] = border
-    back_two[:, 0:1] = border
-    back_two[:, side + 1 :] = border
-    back_one[:, side:] = border
+    no_rows = jnp.zeros((slots, width), low)
+    for j in range(side):
+        for i in (0, side + 1):
+            low_one[pl.ds(((side + 2) * j + i) * slots, slots), :] = no_rows
     head_pad[...] = jnp.zeros_like(head_pad)
     head_pad[:classes, :] = head_ref[...]
     head = head_pad[:16, :]
@@ -863,16 +862,21 @@
         active[j, 1 : side + 1] = (
             (hidden * gate(hidden)).astype(low).reshape(side, slots, width)
         )
-    two_sums = [none, none]
-    for j in range(side):
-        taps = [b for b in range(3) if 0 <= j + b - 1 < side]
-        pieces = [
-            active[j + b - 1, a : a + side].reshape(band, width) for b in taps for a in range(3)
-        ]
-        low_rows = low_two[3 * taps[0] : 3 * taps[-1] + 3].reshape(-1, width)
-        value = jnp.dot(jnp.concatenate(pieces, axis=1), low_rows, preferred_element_type=f32)
-        main_two[pl.ds(j * band, band), :] = value
-        two_sums = add_up(two_sums, moments(value))
+
+    def active_taps(first, last):
+        pieces = [active[first:last, a : a + side].reshape(-1, width) for a in range(3)]
+        return jnp.concatenate(pieces, axis=1)
+
+    two_sums = []
+    deep = 3 * width
+    for cols in halves:
+        main_two[:band, cols] = jnp.zeros((band, half), f32)
+        main_two[band:, cols] = product(active_taps(0, side - 1), low_two[:deep, cols])
+        main_two[: 3 * band, cols] += product(active_taps(1, side), low_two[2 * deep :, cols])
+        value = main_two[:, cols] + product(active_taps(0, side), low_two[deep : 2 * deep, cols])
+        main_two[:, cols] = value
+        two_sums.append(moments(value))
+    two_sums = side_by_side(two_sums)
     copies = exchange_start(1, pack_rows(two_sums))
     for j in range(side):
         block = active[j, 1 : side + 1].reshape(band, width)
@@ -886,13 +890,23 @@
 
     base_joined = base_two + base_side
 
-    def joined_of(here):
-        return main_two[here, :] * slope_two + side_pre[here, :] * slope_side + base_joined
-
-    pooled = jnp.zeros((slots, width), f32)
-    for p in range(pixel_count):
-        joined = joined_of(pl.ds(p * slots, slots))
-        pooled = pooled + joined * gate(joined)
+    quarters = [slice(128 * q, 128 * (q + 1)) for q in range(width // 128)]
+
+    def joined_of(here, lanes):
+        return (
+            main_two[here, lanes] * slope_two[:, lanes]
+            + side_pre[here, lanes] * slope_side[:, lanes]
+            + base_joined[:, lanes]
+        )
+
+    pooled = []
+    for lanes in quarters:
+        total_joined = jnp.zeros((slots, 128), f32)
+        for p in range(pixel_count):
+            joined = joined_of(pl.ds(p * slots, slots), lanes)
+            total_joined = total_joined + joined * gate(joined)
+        pooled.append(total_joined)
+    pooled = jnp.concatenate(pooled, axis=1)
     pooled = (pooled / pixel_count).astype(low)
     head_low = head_pad[...].astype(low)
     logits = lax.dot_general(
@@ -915,29 +929,35 @@
     )[:16]
     grad_pooled = jnp.dot(grad_logits, head_low, preferred_element_type=f32) / pixel_count
 
-    gain_two, gain_side, shift_two = none, none, none
-    for p in range(pixel_count):
-        here = pl.ds(p * slots, slots)
-        joined = joined_of(here)
-        opened = gate(joined)
-        grad = grad_pooled * (opened * (1.0 + joined * (1.0 - opened)))
-        shift_two = shift_two + jnp.sum(grad, axis=0, keepdims=True)
-        gain_two = gain_two + jnp.sum(
-            grad * ((main_two[here, :] - mean_two) * inv_two), axis=0, keepdims=True
-        )
-        gain_side = gain_side + jnp.sum(
-            grad * ((side_pre[here, :] - mean_side) * inv_side), axis=0, keepdims=True
-        )
-        back_two[p // side, 1 + p % side] = (grad * slope_two).astype(low)
-        back_side[here, :] = (grad * slope_side).astype(low)
+    def back_rows(j, i, count):
+        return low_one[pl.ds(((side + 2) * j + i) * slots, count * slots), :]
+
+    join_sums = []
+    for lanes in quarters:
+        three = [jnp.zeros((8, 128), f32)] * 3
+        for p in range(pixel_count):
+            here = pl.ds(p * slots, slots)
+            joined = joined_of(here, lanes)
+            opened = gate(joined)
+            grad = grad_pooled[:, lanes] * (opened * (1.0 + joined * (1.0 - opened)))
+            normed_two = (main_two[here, lanes] - mean_two[:, lanes]) * inv_two[:, lanes]
+            normed_side = (side_pre[here, lanes] - mean_side[:, lanes]) * inv_side[:, lanes]
+            three = [
+                old + fold(new) for old, new in zip(three, (grad * normed_two, grad * normed_side, grad))
+            ]
+            at = ((side + 2) * (p // side) + 1 + p % side) * slots
+            low_one[pl.ds(at, slots), lanes] = (grad * slope_two[:, lanes]).astype(low)
+            back_side[here, lanes] = (grad * slope_side[:, lanes]).astype(low)
+        join_sums.append([jnp.sum(each, axis=0, keepdims=True) for each in three])
+    gain_two, gain_side, shift_two = side_by_side(join_sums)
 
     for b in range(3):
         first, last = max(0, b - 1), min(side, side + b - 1)
         left = active_t[:, first * band : last * band]
         for a in range(3):
-            right = back_two[first - b + 1 : last - b + 1, 2 - a : 2 - a + side]
-            grad_two[pl.ds((a * 3 + b) * width, width), :] = jnp.dot(
-                left, right.reshape(-1, width), preferred_element_type=f32
+            right = [back_rows(j, 2 - a, side) for j in range(first - b + 1, last - b + 1)]
+            grad_two[pl.ds((a * 3 + b) * width, width), :] = product(
+                left, jnp.concatenate(right, axis=0)
             )
 
     def nothing():
@@ -1071,31 +1091,56 @@
     grad_short[...] = jnp.dot(xs_t[0, 0], back_side[...], preferred_element_type=f32)
     matrix_votes(2, grad_short, (nothing, nothing), lambda k: None)
 
-    gain_one, shift_one = none, none
-    for j in range(side):
-        taps = [b for b in range(3) if 0 <= j - b + 1 < side]
+    def back_taps(first, last):
         pieces = [
-            back_two[j - b + 1, 2 - a : 2 - a + side].reshape(band, width)
-            for b in taps
+            jnp.concatenate([back_rows(j, 2 - a, side) for j in range(first, last)], axis=0)
             for a in range(3)
         ]
-        weights = jnp.concatenate([low_two[b * 3 + a] for b in taps for a in range(3)], axis=1)
-        grad = lax.dot_general(
-            jnp.concatenate(pieces, axis=1),
-            weights,
-            (((1,), (1,)), ((), ())),
-            preferred_element_type=f32,
+        return jnp.concatenate(pieces, axis=1)
+
+    def back_weights(b, cols):
+        pieces = [
+            low_two[pl.ds((3 * b + a) * width + cols.start, half), :] for a in range(3)
+        ]
+        return jnp.concatenate(pieces, axis=1)
+
+    def product_turned(left, right):
+        return lax.dot_general(left, right, (((1,), (1,)), ((), ())), preferred_element_type=f32)
+
+    for k, cols in enumerate(halves):
+        main_two[: 3 * band, cols] = product_turned(back_taps(1, side), back_weights(0, cols))
+        main_two[3 * band :, cols] = jnp.zeros((band, half), f32)
+        main_two[band:, cols] += product_turned(back_taps(0, side - 1), back_weights(2, cols))
+        main_two[:, cols] += product_turned(back_taps(0, side), back_weights(1, cols))
+        turn(1 + k)
+
+    active[:, side : side + 1] = border
+    first_sums = [[], []]
+    for j in range(side):
+        for lanes in quarters:
+            here = pl.ds(j * band, band)
+            before = main_pre[here, lanes]
+            hidden = before * slope_one[:, lanes] + base_one[:, lanes]
+            opened = gate(hidden)
+            grad = main_two[here, lanes] * (opened * (1.0 + hidden * (1.0 - opened)))
+            normed = (before - mean_one[:, lanes]) * inv_one[:, lanes]
+            first_sums[0].append(fold(grad * normed))
+            first_sums[1].append(fold(grad))
+            active[j, :side, :, lanes] = (
+                (grad * slope_one[:, lanes]).astype(low).reshape(side, slots, 128)
+            )
+        if j % 2:
+            turn(3 + j // 2)
+    gain_one, shift_one = [
+        jnp.concatenate(
+            [
+                jnp.sum(functools.reduce(lambda a, b: a + b, sums[q::4]), axis=0, keepdims=True)
+                for q in range(4)
+            ],
+            axis=1,
         )
-        before = main_pre[pl.ds(j * band, band), :]
-        hidden = before * slope_one + base_one
-        opened = gate(hidden)
-        grad = grad * (opened * (1.0 + hidden * (1.0 - opened)))
-        shift_one = shift_one + jnp.sum(grad, axis=0, keepdims=True)
-        gain_one = gain_one + jnp.sum(
-            grad * ((before - mean_one) * inv_one), axis=0, keepdims=True
-        )
-        back_one[j, :side] = (grad * slope_one).astype(low).reshape(side, slots, width)
-        turn(1 + j)
+        for sums in first_sums
+    ]
 
     square_head = grad_head * grad_head + EPS_ROW
     real = lax.broadcasted_iota(jnp.int32, square_head.shape, 0) < classes
@@ -1144,7 +1189,7 @@
         for a in range(3):
             left = xs_t[0 if b == 1 else 1, 0 if a == 1 else 1, :, first * band : last * band]
             start = 1 if a == 0 else 0
-            right = back_one[first + shift : last + shift, start : start + side]
+            right = active[first + shift : last + shift, start : start + side]
             grad_one[pl.ds((a * 3 + b) * in_width, in_width), :] = jnp.dot(
                 left, right.reshape(-1, width), preferred_element_type=f32
             )
@@ -1181,30 +1226,26 @@
         copies.append(
             pltpu.make_async_copy(sources[0].at[here], targets[0].at[here], sem.at[k])
         )
-    for k in range(1, count - 2):
+    for k in range(1, count):
         copies.append(pltpu.make_async_copy(sources[k], targets[k], sem.at[chunks + k]))
     for copy in copies:
         copy.start()
-    for k in (count - 2, count - 1):
-        targets[k][...] = sources[k][...]
     for copy in copies:
         copy.wait()
 
 
 def finish(values):
-    vmem = pl.BlockSpec(memory_space=pltpu.VMEM)
-    hbm = pl.BlockSpec(memory_space=pl.ANY)
-    count, chunks = len(values), 8
-    held = [pltpu.with_memory_space_constraint(value, pltpu.VMEM) for value in values[:-2]]
+    count, chunks = len(values), 4
+    held = [pltpu.with_memory_space_constraint(value, pltpu.VMEM) for value in values]
     return pl.pallas_call(
         functools.partial(finish_kernel, count, chunks),
         out_shape=[jax.ShapeDtypeStruct(value.shape, value.dtype) for value in values],
-        in_specs=[vmem] * count,
-        out_specs=[hbm] * (count - 2) + [vmem] * 2,
+        in_specs=[pl.BlockSpec(memory_space=pltpu.VMEM)] * count,
+        out_specs=[pl.BlockSpec(memory_space=pl.ANY)] * count,
         scratch_shapes=[pltpu.SemaphoreType.DMA((chunks + count,))],
         compiler_params=pltpu.CompilerParams(vmem_limit_bytes=1024 * 1024),
         name="finish",
-    )(*held, *values[-2:])
+    )(*held)
 
 
 def run_step(images, conv_one, conv_two, shortcut, head, norm_params, valid, labels, rows, cols, moment):
@@ -1232,8 +1273,8 @@
             shape(rows.shape, f32),
             shape(cols.shape, f32),
             shape(moment.shape, f32),
-            jax.ShapeDtypeStruct((1, 1), f32),
-            jax.ShapeDtypeStruct((1, 1), f32),
+            shape((1, 1), f32),
+            shape((1, 1), f32),
         ),
         in_specs=[hbm] * 4 + [vmem] * 7,
         out_specs=(vmem,) * 8,
@@ -1242,15 +1283,13 @@
             pltpu.VMEM(conv_one.shape, f32),
             pltpu.VMEM(conv_two.shape, f32),
             pltpu.VMEM(shortcut.shape, f32),
-            pltpu.VMEM((9, in_width, width), low),
-            pltpu.VMEM((9, width, width), low),
-            pltpu.VMEM((1, in_width, width), low),
+            pltpu.VMEM(conv_one.shape, low),
+            pltpu.VMEM(conv_two.shape, low),
+            pltpu.VMEM(shortcut.shape, low),
             pltpu.VMEM((pixels, width), f32),
             pltpu.VMEM((pixels, width), f32),
             pltpu.VMEM((pixels, width), f32),
             pltpu.VMEM((4, 6, slots, width), low),
-            pltpu.VMEM((4, 6, slots, width), low),
-            pltpu.VMEM((4, 5, slots, width), low),
             pltpu.VMEM((pixels, width), low),
             pltpu.VMEM((width, pixels), low),
             pltpu.VMEM((2, 2, in_width, pixels), low),

time: 138 us -> 144 us (1.043)
  Pallas kernels: 137 us -> 143 us
    pallas_call x1, Pallas kernels: 132 us -> 139 us  [run_step(): pl.pallas_call(functools.partial(step_kernel, tuple(edges), tuple(units),...]
where the time goes in v9:
time: 144 us
  Pallas kernels  143 us (99%)
    pallas_call x1, Pallas kernels, run_step(): pl.pallas_call(functools.partial(step_kernel, tuple(edges), tuple(units),...  139 us
    pallas_call x1, Pallas kernels, finish(): pl.pallas_call(functools.partial(finish_kernel, count, chunks), out_shape...  4.65 us

profile of v9, /device:TPU:0, one launch (start us, length us, event | category | flops | bytes accessed | tf_op | source)
XLA Modules:
  0.0 144.0 jit_solution(17004708196299714659)
XLA Ops:
  0.6 138.5 %step.1 = (f32[898,128]{1,0:T(8,128)S(1)}, f32[898,128]{1,0:T(8,128)S(1)}, bf16[28736,128]{1,0:T(8,128)(2,1)S(1)}, f32[1,7680]{1,0:T(1,128)S(1)}, f32[1,1546]{1,...) custom-call(bf16[4096,256]{1,0:T(8,128)(2,1)} %bitcast.9, f32[2304,512]{1,0:T(8,128)} %one_hbm.1, ...), custom_call_target="tpu_custom_call" | custom-call | tf_op jit(solution)/shard_map/step/pallas_call | solution.py:1267
  139.1 4.7 %finish.1 = (bf16[28736,128]{1,0:T(8,128)(2,1)}, f32[898,128]{1,0:T(8,128)}, f32[898,128]{1,0:T(8,128)}, f32[1,7680]{1,0:T(1,128)}, f32[1,1546]{1,0:T(1,128)}, /...) custom-call(bf16[28736,128]{1,0:T(8,128)(2,1)S(1)} %get-tuple-element.24.refs_0_, ...), custom_call_target="tpu_custom_call" | custom-call | tf_op jit(solution)/shard_map/finish/pallas_call | solution.py:1240

commit v10 on v8

--- a/solution.py
+++ b/solution.py
@@ -227,10 +227,10 @@
 
 def cast_weight(source, target, square_ref, taps, depth, fetches):
     step = 128
-    square_ref[...] = jnp.zeros_like(square_ref)
-    for tap in range(taps):
-        if tap % (taps // len(fetches)) == 0:
-            fetches[tap * len(fetches) // taps].wait()
+    for tap in taps:
+        chunk = source.shape[0] // depth // len(fetches)
+        if tap % chunk == 0:
+            fetches[tap // chunk].wait()
         new_tap = (tap % 3) * 3 + tap // 3
 
         @pl.loop(0, depth // step)
@@ -764,9 +764,11 @@
     weight_slot = jnp.broadcast_to(valid_column, (slots, width))
     weight_band = jnp.concatenate([weight_slot] * side, axis=0)
 
-    cast_weight(grad_one, low_one, square, 9, in_width, fetch_one)
+    square[...] = jnp.zeros_like(square)
+    cast_weight(grad_one, low_one, square, range(9), in_width, fetch_one)
     scales[0] = scale_from(square[...], grad_one.size)
-    cast_weight(grad_short, low_short, square, 1, in_width, fetch_short)
+    square[...] = jnp.zeros_like(square)
+    cast_weight(grad_short, low_short, square, range(1), in_width, fetch_short)
     scales[2] = scale_from(square[...], grad_short.size)
     for fetch in fetch_two:
         fetch.start()
@@ -823,14 +825,11 @@
     copies = exchange_start(
         0, pack_rows(main_sums + side_sums + [count])
     )
-    cast_weight(grad_two, low_two, square, 9, width, fetch_two)
+    square[...] = jnp.zeros_like(square)
+    cast_weight(grad_two, low_two, square, range(5), width, fetch_two)
+    copies = exchange_middle(0, copies)
+    cast_weight(grad_two, low_two, square, range(5, 9), width, fetch_two)
     scales[1] = scale_from(square[...], grad_two.size)
-    copies = exchange_middle(0, copies)
-    for across in range(2):
-        for down in range(2):
-            for j in range(side):
-                block = xs[across, j, down].reshape(band, in_width)
-                xs_t[across, down, :, j * band : (j + 1) * band] = block.T
     border = jnp.zeros((side, 1, slots, width), low)
     active[:, 0:1] = border
     active[:, side + 1 :] = border
@@ -877,7 +876,14 @@
     for j in range(side):
         block = active[j, 1 : side + 1].reshape(band, width)
         active_t[:, j * band : (j + 1) * band] = block.T
+    label_column = column_of(label_ref[...].astype(f32), slots).astype(jnp.int32)
+    head_low = head_pad[...].astype(low)
     copies = exchange_middle(1, copies)
+    for across in range(2):
+        for down in range(2):
+            for j in range(side):
+                block = xs[across, j, down].reshape(band, in_width)
+                xs_t[across, down, :, j * band : (j + 1) * band] = block.T
     sums = exchange_end(1, copies)
     sums = [unpack_row(sums, k) for k in range(2)]
     mean_two, inv_two, slope_two, base_two = settle_rows(
@@ -886,15 +892,24 @@
 
     base_joined = base_two + base_side
 
-    def joined_of(here):
-        return main_two[here, :] * slope_two + side_pre[here, :] * slope_side + base_joined
-
-    pooled = jnp.zeros((slots, width), f32)
-    for p in range(pixel_count):
-        joined = joined_of(pl.ds(p * slots, slots))
-        pooled = pooled + joined * gate(joined)
+    quarters = [slice(128 * q, 128 * (q + 1)) for q in range(width // 128)]
+
+    def joined_of(here, lanes):
+        return (
+            main_two[here, lanes] * slope_two[:, lanes]
+            + side_pre[here, lanes] * slope_side[:, lanes]
+            + base_joined[:, lanes]
+        )
+
+    pooled = []
+    for lanes in quarters:
+        total_joined = jnp.zeros((slots, 128), f32)
+        for p in range(pixel_count):
+            joined = joined_of(pl.ds(p * slots, slots), lanes)
+            total_joined = total_joined + joined * gate(joined)
+        pooled.append(total_joined)
+    pooled = jnp.concatenate(pooled, axis=1)
     pooled = (pooled / pixel_count).astype(low)
-    head_low = head_pad[...].astype(low)
     logits = lax.dot_general(
         pooled, head_low, (((1,), (1,)), ((), ())), preferred_element_type=f32
     )
@@ -903,7 +918,6 @@
     largest = jnp.max(jnp.where(real, logits, -jnp.inf), axis=1, keepdims=True)
     powers = jnp.where(real, jnp.exp(jnp.where(real, logits - largest, 0.0)), 0.0)
     total_power = jnp.sum(powers, axis=1, keepdims=True)
-    label_column = column_of(label_ref[...].astype(f32), slots).astype(jnp.int32)
     onehot = jnp.where(lane == label_column, 1.0, 0.0)
     entropy = largest + jnp.log(total_power) - jnp.sum(onehot * logits, axis=1, keepdims=True)
     loss = jnp.sum(entropy * valid_column, axis=0, keepdims=True)
@@ -915,21 +929,22 @@
     )[:16]
     grad_pooled = jnp.dot(grad_logits, head_low, preferred_element_type=f32) / pixel_count
 
-    gain_two, gain_side, shift_two = none, none, none
-    for p in range(pixel_count):
-        here = pl.ds(p * slots, slots)
-        joined = joined_of(here)
-        opened = gate(joined)
-        grad = grad_pooled * (opened * (1.0 + joined * (1.0 - opened)))
-        shift_two = shift_two + jnp.sum(grad, axis=0, keepdims=True)
-        gain_two = gain_two + jnp.sum(
-            grad * ((main_two[here, :] - mean_two) * inv_two), axis=0, keepdims=True
-        )
-        gain_side = gain_side + jnp.sum(
-            grad * ((side_pre[here, :] - mean_side) * inv_side), axis=0, keepdims=True
-        )
-        back_two[p // side, 1 + p % side] = (grad * slope_two).astype(low)
-        back_side[here, :] = (grad * slope_side).astype(low)
+    join_sums = []
+    for lanes in quarters:
+        three = [jnp.zeros((8, 128), f32)] * 3
+        for p in range(pixel_count):
+            here = pl.ds(p * slots, slots)
+            joined = joined_of(here, lanes)
+            opened = gate(joined)
+            grad = grad_pooled[:, lanes] * (opened * (1.0 + joined * (1.0 - opened)))
+            normed_two = (main_two[here, lanes] - mean_two[:, lanes]) * inv_two[:, lanes]
+            normed_side = (side_pre[here, lanes] - mean_side[:, lanes]) * inv_side[:, lanes]
+            new = (grad * normed_two, grad * normed_side, grad)
+            three = [old + fold(each) for old, each in zip(three, new)]
+            back_two[p // side, 1 + p % side, :, lanes] = (grad * slope_two[:, lanes]).astype(low)
+            back_side[here, lanes] = (grad * slope_side[:, lanes]).astype(low)
+        join_sums.append([jnp.sum(each, axis=0, keepdims=True) for each in three])
+    gain_two, gain_side, shift_two = [jnp.concatenate(each, axis=1) for each in zip(*join_sums)]
 
     for b in range(3):
         first, last = max(0, b - 1), min(side, side + b - 1)
@@ -1181,30 +1196,26 @@
         copies.append(
             pltpu.make_async_copy(sources[0].at[here], targets[0].at[here], sem.at[k])
         )
-    for k in range(1, count - 2):
+    for k in range(1, count):
         copies.append(pltpu.make_async_copy(sources[k], targets[k], sem.at[chunks + k]))
     for copy in copies:
         copy.start()
-    for k in (count - 2, count - 1):
-        targets[k][...] = sources[k][...]
     for copy in copies:
         copy.wait()
 
 
 def finish(values):
-    vmem = pl.BlockSpec(memory_space=pltpu.VMEM)
-    hbm = pl.BlockSpec(memory_space=pl.ANY)
-    count, chunks = len(values), 8
-    held = [pltpu.with_memory_space_constraint(value, pltpu.VMEM) for value in values[:-2]]
+    count, chunks = len(values), 4
+    held = [pltpu.with_memory_space_constraint(value, pltpu.VMEM) for value in values]
     return pl.pallas_call(
         functools.partial(finish_kernel, count, chunks),
         out_shape=[jax.ShapeDtypeStruct(value.shape, value.dtype) for value in values],
-        in_specs=[vmem] * count,
-        out_specs=[hbm] * (count - 2) + [vmem] * 2,
+        in_specs=[pl.BlockSpec(memory_space=pltpu.VMEM)] * count,
+        out_specs=[pl.BlockSpec(memory_space=pl.ANY)] * count,
         scratch_shapes=[pltpu.SemaphoreType.DMA((chunks + count,))],
         compiler_params=pltpu.CompilerParams(vmem_limit_bytes=1024 * 1024),
         name="finish",
-    )(*held, *values[-2:])
+    )(*held)
 
 
 def run_step(images, conv_one, conv_two, shortcut, head, norm_params, valid, labels, rows, cols, moment):
@@ -1232,8 +1243,8 @@
             shape(rows.shape, f32),
             shape(cols.shape, f32),
             shape(moment.shape, f32),
-            jax.ShapeDtypeStruct((1, 1), f32),
-            jax.ShapeDtypeStruct((1, 1), f32),
+            shape((1, 1), f32),
+            shape((1, 1), f32),
         ),
         in_specs=[hbm] * 4 + [vmem] * 7,
         out_specs=(vmem,) * 8,

time: 138 us -> 138 us (level)
  no operation moved by 1% of the time
where the time goes in v10:
time: 138 us; the launch traced here: 137 us
  Pallas kernels  137 us (99%)
    pallas_call x1, Pallas kernels, run_step(): pl.pallas_call(functools.partial(step_kernel, tuple(edges), tuple(units),...  132 us
    pallas_call x1, Pallas kernels, finish(): pl.pallas_call(functools.partial(finish_kernel, count, chunks), out_shape...  4.65 us

profile of v10, /device:TPU:0, one launch (start us, length us, event | category | flops | bytes accessed | tf_op | source)
XLA Modules:
  0.0 137.5 jit_solution(6852145902070623070)
XLA Ops:
  0.6 132.0 %step.1 = (f32[898,128]{1,0:T(8,128)S(1)}, f32[898,128]{1,0:T(8,128)S(1)}, bf16[28736,128]{1,0:T(8,128)(2,1)S(1)}, f32[1,7680]{1,0:T(1,128)S(1)}, f32[1,1546]{1,...) custom-call(bf16[4096,256]{1,0:T(8,128)(2,1)} %bitcast.9, f32[2304,512]{1,0:T(8,128)} %one_hbm.1, ...), custom_call_target="tpu_custom_call" | custom-call | tf_op jit(solution)/shard_map/step/pallas_call | solution.py:1237
  132.6 4.7 %finish.1 = (bf16[28736,128]{1,0:T(8,128)(2,1)}, f32[898,128]{1,0:T(8,128)}, f32[898,128]{1,0:T(8,128)}, f32[1,7680]{1,0:T(1,128)}, f32[1,1546]{1,0:T(1,128)}, /...) custom-call(bf16[28736,128]{1,0:T(8,128)(2,1)S(1)} %get-tuple-element.24.refs_0_, ...), custom_call_target="tpu_custom_call" | custom-call | tf_op jit(solution)/shard_map/finish/pallas_call | solution.py:1210

commit v11 on v10

--- a/solution.py
+++ b/solution.py
@@ -762,7 +762,7 @@
 
     valid_column = column_of(valid_ref[...].astype(f32), slots)
     weight_slot = jnp.broadcast_to(valid_column, (slots, width))
-    weight_band = jnp.concatenate([weight_slot] * side, axis=0)
+    weight_pair = jnp.concatenate([weight_slot] * 2, axis=0)
 
     square[...] = jnp.zeros_like(square)
     cast_weight(grad_one, low_one, square, range(9), in_width, fetch_one)
@@ -778,7 +778,9 @@
     for u in range(len(units)):
         own_fetch(u)
 
-    def image_taps(j):
+    pair = 2 * slots
+
+    def image_taps(j, i):
         pieces = []
         for b in range(3):
             column = j if b else j - 1
@@ -787,17 +789,20 @@
             across = 0 if b == 1 else 1
             for a in range(3):
                 if a == 1:
-                    piece = xs[across, column, 0].reshape(band, in_width)
+                    piece = xs[across, column, 0, i : i + 2].reshape(pair, in_width)
                 elif a == 2:
-                    piece = xs[across, column, 1].reshape(band, in_width)
+                    piece = xs[across, column, 1, i : i + 2].reshape(pair, in_width)
+                elif i:
+                    piece = xs[across, column, 1, i - 1 : i + 1].reshape(pair, in_width)
                 else:
-                    piece = xs[across, column, 1, : side - 1].reshape(band - slots, in_width)
-                    piece = jnp.concatenate([jnp.zeros((slots, in_width), low), piece], axis=0)
+                    piece = jnp.concatenate(
+                        [jnp.zeros((slots, in_width), low), xs[across, column, 1, 0]], axis=0
+                    )
                 pieces.append(piece)
         return jnp.concatenate(pieces, axis=1)
 
     def moments(values):
-        weighted = values * weight_band
+        weighted = values * weight_pair
         return (
             jnp.sum(weighted, axis=0, keepdims=True),
             jnp.sum(weighted * values, axis=0, keepdims=True),
@@ -809,16 +814,19 @@
     none = jnp.zeros((1, width), f32)
     main_sums, side_sums = [none, none], [none, none]
     for j in range(side):
-        here = pl.ds(j * band, band)
         low_rows = low_one[3 if j == 0 else 0 :].reshape(-1, width)
-        value = jnp.dot(image_taps(j), low_rows, preferred_element_type=f32)
-        main_pre[here, :] = value
-        main_sums = add_up(main_sums, moments(value))
-        value = jnp.dot(
-            xs[0, j, 0].reshape(band, in_width), low_short[0], preferred_element_type=f32
-        )
-        side_pre[here, :] = value
-        side_sums = add_up(side_sums, moments(value))
+        for i in range(0, side, 2):
+            here = pl.ds(j * band + i * slots, pair)
+            value = jnp.dot(image_taps(j, i), low_rows, preferred_element_type=f32)
+            main_pre[here, :] = value
+            main_sums = add_up(main_sums, moments(value))
+            value = jnp.dot(
+                xs[0, j, 0, i : i + 2].reshape(pair, in_width),
+                low_short[0],
+                preferred_element_type=f32,
+            )
+            side_pre[here, :] = value
+            side_sums = add_up(side_sums, moments(value))
 
     count = jnp.broadcast_to(jnp.sum(valid_column, axis=0, keepdims=True), (1, width))
     pl.semaphore_wait(barrier, len(others))
@@ -865,13 +873,16 @@
     two_sums = [none, none]
     for j in range(side):
         taps = [b for b in range(3) if 0 <= j + b - 1 < side]
-        pieces = [
-            active[j + b - 1, a : a + side].reshape(band, width) for b in taps for a in range(3)
-        ]
         low_rows = low_two[3 * taps[0] : 3 * taps[-1] + 3].reshape(-1, width)
-        value = jnp.dot(jnp.concatenate(pieces, axis=1), low_rows, preferred_element_type=f32)
-        main_two[pl.ds(j * band, band), :] = value
-        two_sums = add_up(two_sums, moments(value))
+        for i in range(0, side, 2):
+            pieces = [
+                active[j + b - 1, a + i : a + i + 2].reshape(pair, width)
+                for b in taps
+                for a in range(3)
+            ]
+            value = jnp.dot(jnp.concatenate(pieces, axis=1), low_rows, preferred_element_type=f32)
+            main_two[pl.ds(j * band + i * slots, pair), :] = value
+            two_sums = add_up(two_sums, moments(value))
     copies = exchange_start(1, pack_rows(two_sums))
     for j in range(side):
         block = active[j, 1 : side + 1].reshape(band, width)
@@ -946,13 +957,22 @@
         join_sums.append([jnp.sum(each, axis=0, keepdims=True) for each in three])
     gain_two, gain_side, shift_two = [jnp.concatenate(each, axis=1) for each in zip(*join_sums)]
 
+    def turned_product(left_ref, columns, right, target, at):
+        for m in range(0, left_ref.shape[0], 128):
+            target[pl.ds(at + m, 128), :] = jnp.dot(
+                left_ref[m : m + 128, columns], right, preferred_element_type=f32
+            )
+
     for b in range(3):
         first, last = max(0, b - 1), min(side, side + b - 1)
-        left = active_t[:, first * band : last * band]
         for a in range(3):
             right = back_two[first - b + 1 : last - b + 1, 2 - a : 2 - a + side]
-            grad_two[pl.ds((a * 3 + b) * width, width), :] = jnp.dot(
-                left, right.reshape(-1, width), preferred_element_type=f32
+            turned_product(
+                active_t,
+                slice(first * band, last * band),
+                right.reshape(-1, width),
+                grad_two,
+                (a * 3 + b) * width,
             )
 
     def nothing():
@@ -1157,11 +1177,14 @@
         first, last = (0, side - 1) if b == 0 else (0, side)
         shift = 1 if b == 0 else 0
         for a in range(3):
-            left = xs_t[0 if b == 1 else 1, 0 if a == 1 else 1, :, first * band : last * band]
             start = 1 if a == 0 else 0
             right = back_one[first + shift : last + shift, start : start + side]
-            grad_one[pl.ds((a * 3 + b) * in_width, in_width), :] = jnp.dot(
-                left, right.reshape(-1, width), preferred_element_type=f32
+            turned_product(
+                xs_t.at[0 if b == 1 else 1, 0 if a == 1 else 1],
+                slice(first * band, last * band),
+                right.reshape(-1, width),
+                grad_one,
+                (a * 3 + b) * in_width,
             )
         if b == 1:
             kept["tail"] = exchange_middle(2, kept["tail"])

time: 138 us -> 138 us (level)
  no operation moved by 1% of the time
where the time goes in v11:
time: 138 us
  Pallas kernels  137 us (99%)
    pallas_call x1, Pallas kernels, run_step(): pl.pallas_call(functools.partial(step_kernel, tuple(edges), tuple(units),...  132 us
    pallas_call x1, Pallas kernels, finish(): pl.pallas_call(functools.partial(finish_kernel, count, chunks), out_shape...  4.65 us

profile of v11, /device:TPU:0, one launch (start us, length us, event | category | flops | bytes accessed | tf_op | source)
XLA Modules:
  0.0 137.8 jit_solution(55183832605239371)
XLA Ops:
  0.6 132.4 %step.1 = (f32[898,128]{1,0:T(8,128)S(1)}, f32[898,128]{1,0:T(8,128)S(1)}, bf16[28736,128]{1,0:T(8,128)(2,1)S(1)}, f32[1,7680]{1,0:T(1,128)S(1)}, f32[1,1546]{1,...) custom-call(bf16[4096,256]{1,0:T(8,128)(2,1)} %bitcast.9, f32[2304,512]{1,0:T(8,128)} %one_hbm.1, ...), custom_call_target="tpu_custom_call" | custom-call | tf_op jit(solution)/shard_map/step/pallas_call | solution.py:1260
  133.0 4.7 %finish.1 = (bf16[28736,128]{1,0:T(8,128)(2,1)}, f32[898,128]{1,0:T(8,128)}, f32[898,128]{1,0:T(8,128)}, f32[1,7680]{1,0:T(1,128)}, f32[1,1546]{1,0:T(1,128)}, /...) custom-call(bf16[28736,128]{1,0:T(8,128)(2,1)S(1)} %get-tuple-element.24.refs_0_, ...), custom_call_target="tpu_custom_call" | custom-call | tf_op jit(solution)/shard_map/finish/pallas_call | solution.py:1233

commit v12 on v10

--- a/solution.py
+++ b/solution.py
@@ -149,8 +149,8 @@
         (2, 13), (3, 11), (4, 9), (5, 6), (6, 4), (7, 1), (3, 12), (4, 10), (5, 7), (6, 5),
         (7, 2), (3, 13), (4, 11), (5, 8), (6, 6), (7, 3), (4, 12), (5, 9), (6, 7), (7, 4),
         (4, 13), (5, 10), (6, 8), (7, 5), (5, 11), (6, 9), (7, 6), (5, 12), (6, 10), (7, 7),
-        (5, 13), (6, 11), (7, 8), (6, 12), (7, 9), (6, 13), (9, 0), (7, 10), (7, 11), (7, 12),
-        (7, 13),
+        (5, 13), (6, 11), (7, 8), (6, 12), (7, 9), (9, 0), (6, 13), (7, 10), (7, 11), (7, 12),
+        (9, 1), (7, 13), (9, 2),
     ),
 )
 
@@ -384,18 +384,17 @@
     weight,
     vote_flat,
     new_flat,
+    tail_vote,
+    tail_new,
     fetch_sem,
     small_send,
     small_recv,
-    rs_send,
+    sent,
     rs_recv,
-    line_send,
     line_recv,
     pass_send,
     land_recv,
-    spread_send,
     spread_recv,
-    ag_send,
     ag_recv,
     free_sem,
     load_sem,
@@ -556,7 +555,7 @@
         return units[u][0] + core * units[u][3] + (first * 8 + second * 4 + z) * units[u][1]
 
     def halve(source, target, u, stage, partner):
-        return send(source, target, rs_send.at[u, stage], rs_recv.at[u, stage], partner)
+        return send(source, target, sent.at[stage], rs_recv.at[u, stage], partner)
 
     def scatter_start(u):
         size = 16 * sizes[u]
@@ -573,12 +572,22 @@
         here = lines(share * starts[u], size)
         ref[here, :] = ref[here, :] + source_ref[lines(source_start, size), :]
 
+    def sent_all(kind, ref):
+        pltpu.make_async_remote_copy(
+            src_ref=ref,
+            dst_ref=ref,
+            send_sem=sent.at[kind],
+            recv_sem=rs_recv.at[0, 0],
+            device_id=(flip_core,),
+            device_id_type=MESH,
+        ).wait_send()
+
     def scatter_one(u, copy):
-        copy.wait()
+        copy.wait_recv()
         add_to(core_in, u, 16, out_ref, unit_start(u, core))
-        pl.semaphore_signal(
-            free_sem.at[u], inc=1, device_id=(flip_core,), device_id_type=MESH
-        )
+        if u == len(units) - 1:
+            sent_all(0, core_in)
+            pl.semaphore_signal(free_sem, inc=1, device_id=(flip_core,), device_id_type=MESH)
         first, _, flip_first, _ = places(u)
         size = 8 * sizes[u]
         return halve(
@@ -590,7 +599,7 @@
         )
 
     def scatter_two(u, copy):
-        copy.wait()
+        copy.wait_recv()
         first, second, _, flip_second = places(u)
         add_to(wide_in, u, 8, core_in, 16 * starts[u] + first * 8 * sizes[u])
         size = 4 * sizes[u]
@@ -607,20 +616,31 @@
         return pltpu.make_async_remote_copy(
             src_ref=part_of(deep_in, u, 4, plane_to * sizes[u], sizes[u]),
             dst_ref=part_of(line_in, u, 4, z * sizes[u], sizes[u]),
-            send_sem=line_send.at[u, k],
-            recv_sem=line_recv.at[u, k],
+            send_sem=sent.at[3],
+            recv_sem=line_recv.at[u],
             device_id=(plane_to * 8 + spot,),
             device_id_type=MESH,
         )
 
     def scatter_three(u, copy):
-        copy.wait()
+        copy.wait_recv()
         _, second, _, _ = places(u)
         add_to(deep_in, u, 4, wide_in, 8 * starts[u] + second * 4 * sizes[u])
         for k in (3, 2, 1):
             line_copy(u, k).start()
         here = lines(4 * starts[u] + z * sizes[u], sizes[u])
         line_in[here, :] = deep_in[here, :]
+
+    def three_landed(u, sem):
+        ref = part_of(line_in, u, 4, 0, 3 * sizes[u])
+        pltpu.make_async_remote_copy(
+            src_ref=ref,
+            dst_ref=ref,
+            send_sem=sent.at[3],
+            recv_sem=sem.at[u],
+            device_id=(far[0],),
+            device_id_type=MESH,
+        ).wait_recv()
 
     groups = (edges[2] + TAIL) // 16
     spare = (groups - 1) // 32
@@ -644,26 +664,30 @@
             local = starts[u] // GROUP + m
             group = own_group(u) + m
             to, slot = lax.div(group, spare), lax.rem(group, spare)
-            for halo in range(2):
-                index = 2 * local + halo
-                if halo:
-                    receiver, at = lax.rem(to + 31, 32), spare
-                    wanted = jnp.logical_and(slot == 0, group > 0)
-                else:
-                    receiver, at, wanted = to, slot, group >= 0
-                away = jnp.logical_and(wanted, receiver != me)
-                here = jnp.logical_and(wanted, receiver == me)
+
+            def one(receiver, at, index):
                 copy, source, target = land(local, group, receiver, at, index)
 
-                @pl.when(away)
+                @pl.when(receiver != me)
                 def _():
                     copy.start()
 
-                @pl.when(here)
+                @pl.when(receiver == me)
                 def _():
                     target[...] = source[...]
 
-                passes.append((away, copy))
+                return copy
+
+            first = jnp.logical_and(slot == 0, group > 0)
+            ahead = lax.rem(to + 31, 32)
+            passes.append((to != me, one(to, slot, 2 * local)))
+
+            @pl.when(first)
+            def _():
+                one(ahead, spare, 2 * local + 1)
+
+            copy = land(local, group, ahead, spare, 2 * local + 1)[0]
+            passes.append((jnp.logical_and(first, ahead != me), copy))
 
     def flat_rows(row, q, values, ref):
         ref[pl.ds(row * 4 + q, 8, stride=4), :] = values
@@ -692,16 +716,15 @@
         return pltpu.make_async_remote_copy(
             src_ref=own,
             dst_ref=own,
-            send_sem=spread_send.at[u, k],
-            recv_sem=spread_recv.at[u, k],
+            send_sem=sent.at[4],
+            recv_sem=spread_recv.at[u],
             device_id=(far[k - 1],),
             device_id_type=MESH,
         )
 
     def own_block(u):
         size = sizes[u]
-        for k in range(1, 4):
-            line_copy(u, k).wait_recv()
+        three_landed(u, line_recv)
         here = pl.ds(starts[u], size)
         low_sum = functools.reduce(
             lambda a, b: a + b,
@@ -728,26 +751,26 @@
 
     def piece(rows, u, stage, partner):
         return send(
-            out_ref.at[rows], out_ref.at[rows], ag_send.at[u, stage], ag_recv.at[u, stage], partner
+            out_ref.at[rows], out_ref.at[rows], sent.at[5 + stage], ag_recv.at[u, stage], partner
         )
 
     def gather_one(u):
-        for k in range(1, 4):
-            spread_copy(u, k).wait_recv()
+        three_landed(u, spread_recv)
         first, second, _, flip_second = places(u)
         size = 4 * sizes[u]
         start = unit_start(u, core) + (2 * first + second) * size
         return piece(lines(start, size), u, 0, flip_second)
 
     def gather_two(u, copy):
-        copy.wait()
+        copy.wait_recv()
         first, _, flip_first, _ = places(u)
         size = 8 * sizes[u]
         return piece(lines(unit_start(u, core) + first * size, size), u, 1, flip_first)
 
     def gather_three(u, copy):
-        copy.wait()
-        pl.semaphore_wait(free_sem.at[u], 1)
+        copy.wait_recv()
+        if u == 0:
+            pl.semaphore_wait(free_sem, 1)
         return piece(lines(unit_start(u, core), 16 * sizes[u]), u, 2, flip_core)
 
     def renew(row, at_row):
@@ -979,39 +1002,43 @@
 
     def tail_step():
         sums = exchange_end(2, kept["tail"])
-        loss_ref[...] = sums[4 * TAIL : 4 * TAIL + 1, :1]
+        loss_ref[...] = sums[GROUP : GROUP + 1, :1]
+        sums = sums[:GROUP]
         old = jnp.concatenate([head_ref[...], norm_ref[...]], axis=0)
-        is_head = lax.broadcasted_iota(jnp.int32, (TAIL, width), 0) < classes
-        scale = jnp.where(is_head, scales[3], scales[4])
-        sums = jnp.concatenate([sums[TAIL * q : TAIL * (q + 1)] for q in range(4)], axis=1)
+        old = jnp.concatenate([old[:, 128 * q : 128 * (q + 1)] for q in range(4)], axis=0)
+        down = lax.broadcasted_iota(jnp.int32, (GROUP, 128), 0)
+        scale = jnp.where(lax.rem(down, TAIL) < classes, scales[3], scales[4])
         fresh = old - scale * jnp.tanh(sums * root)
         both = jnp.concatenate([sums, fresh], axis=0)
         high = both.astype(low)
         rest = both - high.astype(f32)
         middle = rest.astype(low)
         parts = jnp.concatenate([high, middle, (rest - middle.astype(f32)).astype(low)], axis=0)
-
-        flat_sums, flat_new = [], []
-        window = 256
-        for q in range(classes):
-            start = min(q * width // classes // 128 * 128, width - window)
-            down = lax.broadcasted_iota(jnp.int32, (window, width), 0)
-            across = lax.broadcasted_iota(jnp.int32, (window, width), 1)
-            gap = across - classes * down + (q * width - classes * start)
-            chosen = jnp.where(jnp.logical_and(gap >= 0, gap < classes), 1.0, 0.0).astype(low)
-            moved = jnp.dot(parts[:, start : start + window], chosen, preferred_element_type=f32)
-            moved = moved[: 2 * TAIL] + moved[2 * TAIL : 4 * TAIL] + moved[4 * TAIL :]
-            spot_of = lax.broadcasted_iota(jnp.int32, (TAIL, width), 1).astype(f32) + q * width
-            class_of = spot_of - classes * jnp.floor((spot_of + 0.5) / classes)
-            here = lax.broadcasted_iota(jnp.int32, (TAIL, width), 0).astype(f32) == class_of
-            flat_sums.append(jnp.sum(jnp.where(here, moved[:TAIL], 0.0), axis=0, keepdims=True))
-            flat_new.append(jnp.sum(jnp.where(here, moved[TAIL:], 0.0), axis=0, keepdims=True))
-        kept["sums"] = jnp.concatenate(flat_sums + [sums[classes:]], axis=0)
-        kept["new"] = jnp.concatenate(flat_new + [fresh[classes:]], axis=0)
-
-    def return_step():
+        length = 128 * classes
+        gap = lax.broadcasted_iota(jnp.int32, (128, length), 1) - classes * (
+            lax.broadcasted_iota(jnp.int32, (128, length), 0)
+        )
+        chosen = jnp.where(jnp.logical_and(gap >= 0, gap < classes), 1.0, 0.0).astype(low)
+        moved = jnp.dot(parts, chosen, preferred_element_type=f32)
+        moved = moved[: 2 * GROUP] + moved[2 * GROUP : 4 * GROUP] + moved[4 * GROUP :]
+        place_of = lax.broadcasted_iota(jnp.int32, (TAIL, length), 1).astype(f32)
+        class_of = place_of - classes * jnp.floor((place_of + 0.5) / classes)
+        here = lax.broadcasted_iota(jnp.int32, (TAIL, length), 0).astype(f32) == class_of
+        for which, ref in enumerate((tail_vote, tail_new)):
+            for q in range(4):
+                block = moved[GROUP * which + TAIL * q : GROUP * which + TAIL * (q + 1)]
+                line = jnp.sum(jnp.where(here, block, 0.0), axis=0, keepdims=True)
+                for k in range(classes):
+                    ref[classes * q + k : classes * q + k + 1, :] = line[:, 128 * k : 128 * (k + 1)]
+                for k in range(TAIL - classes):
+                    at = 4 * (classes + k) + q
+                    row = TAIL * q + classes + k
+                    ref[at : at + 1, :] = (sums, fresh)[which][row : row + 1]
+        out_ref[pl.ds(32 * SPAN, GROUP), :] = tail_new[...].astype(low)
+
+    def return_slots(slots_here):
         mine = [own_group(u) for u in range(len(units))]
-        for slot in range(spare + 1):
+        for slot in slots_here:
             group = me * spare + slot
             own = group < 0
             for u, unit in enumerate(units):
@@ -1022,40 +1049,42 @@
             def _():
                 land(0, group, me, slot, 0)[0].wait_recv()
 
-        pltpu.make_async_copy(
-            weight.at[pl.ds(0, OWN)], weight.at[pl.ds(0, OWN)], fetch_sem.at[7]
-        ).wait()
-        total[pl.ds(0, SPAN), :] = landed[pl.ds(0, SPAN), :].astype(f32)
-
-        @pl.loop(0, OWN // 16)
+        first, last = slots_here[0], min(slots_here[-1] + 1, spare)
+        here = pl.ds(first * GROUP, (last - first) * GROUP)
+        total[here, :] = landed[here, :].astype(f32)
+
+        @pl.loop(first, last)
         def _(k):
             row = pl.multiple_of(k * 16, 16)
             renew(row, first_row + row)
 
-        @pl.when(me < 31)
-        def _():
+    def return_step(part):
+        if part == 0:
             pltpu.make_async_copy(
-                weight.at[pl.ds(OWN, TAIL)], weight.at[pl.ds(OWN, TAIL)], fetch_sem.at[8]
+                weight.at[pl.ds(0, OWN)], weight.at[pl.ds(0, OWN)], fetch_sem.at[7]
             ).wait()
-            total[pl.ds(SPAN, GROUP), :] = landed[pl.ds(SPAN, GROUP), :].astype(f32)
-            renew(OWN, first_row + OWN)
-
-        def tail_rows(values, ref):
-            for u in (0, 8):
-                for q in range(4):
-                    flat_rows(OWN + u, q, values[u : u + 8, 128 * q : 128 * (q + 1)], ref)
-
-        @pl.when(me == 31)
-        def _():
-            tail_rows(kept["sums"], vote_flat)
-            tail_rows(kept["new"], new_flat)
-
-        shift = 2 * me
-        share = vote_ref.shape[0]
-        vote_ref[...] = vote_flat[pl.ds(shift, share), :]
-        new_ref[...] = new_flat[pl.ds(shift, share), :]
-        tail_rows(kept["new"], new_flat)
-        out_ref[pl.ds(32 * SPAN, GROUP), :] = new_flat[pl.ds(SPAN, GROUP), :].astype(low)
+            return_slots(range(0, 7))
+        elif part == 1:
+            return_slots(range(7, spare + 1))
+        else:
+
+            @pl.when(me < 31)
+            def _():
+                pltpu.make_async_copy(
+                    weight.at[pl.ds(OWN, TAIL)], weight.at[pl.ds(OWN, TAIL)], fetch_sem.at[8]
+                ).wait()
+                total[pl.ds(SPAN, GROUP), :] = landed[pl.ds(SPAN, GROUP), :].astype(f32)
+                renew(OWN, first_row + OWN)
+
+            @pl.when(me == 31)
+            def _():
+                vote_flat[pl.ds(SPAN, GROUP), :] = tail_vote[...]
+                new_flat[pl.ds(SPAN, GROUP), :] = tail_new[...]
+
+            shift = 2 * me
+            share = vote_ref.shape[0]
+            vote_ref[...] = vote_flat[pl.ds(shift, share), :]
+            new_ref[...] = new_flat[pl.ds(shift, share), :]
 
     in_flight = {}
     steps = (
@@ -1068,7 +1097,7 @@
         gather_two,
         gather_three,
         lambda u, copy: tail_step(),
-        lambda u, copy: return_step(),
+        lambda u, copy: return_step(u),
     )
 
     def go(number, u):
@@ -1174,16 +1203,18 @@
         lambda k: go(0, early + k) if k < 2 else None,
     )
     turn(10)
-    for u in range(len(units)):
-        in_flight[u].wait()
-        for k in range(1, 4):
-            line_copy(u, k).wait_send()
-            spread_copy(u, k).wait_send()
     for away, copy in passes:
 
         @pl.when(away)
         def _():
             copy.wait_send()
+
+    three = deep_in.at[pl.ds(0, 3 * SPAN)]
+    for kind, ref in enumerate((None, wide_in, deep_in, three, three, deep_in, wide_in, core_in)):
+        if kind:
+            sent_all(kind, ref)
+    for u in range(len(units)):
+        in_flight[u].wait_recv()
 
 
 def finish_kernel(count, chunks, *refs):
@@ -1288,20 +1319,19 @@
             pltpu.VMEM((OWN + TAIL, width), f32),
             pltpu.VMEM((SPAN + GROUP, 128), f32),
             pltpu.VMEM((SPAN + GROUP, 128), f32),
+            pltpu.VMEM((GROUP, 128), f32),
+            pltpu.VMEM((GROUP, 128), f32),
             dma((9 + len(units),)),
             dma((3, 10)),
             dma((3, 10)),
+            dma((8,)),
             dma((len(units), 3)),
-            dma((len(units), 3)),
-            dma((len(units), 4)),
-            dma((len(units), 4)),
+            dma((len(units),)),
             dma((2 * OWN // 16,)),
             dma((OWN // 16 + 1,)),
-            dma((len(units), 4)),
-            dma((len(units), 4)),
+            dma((len(units),)),
             dma((len(units), 3)),
-            dma((len(units), 3)),
-            pltpu.SemaphoreType.REGULAR((len(units),)),
+            pltpu.SemaphoreType.REGULAR,
             dma((2,)),
         ],
         compiler_params=pltpu.CompilerParams(

time: 138 us -> 135 us (0.978)
  Pallas kernels: 137 us -> 134 us
    pallas_call x1, Pallas kernels: 132 us -> 129 us  [run_step(): pl.pallas_call(functools.partial(step_kernel, tuple(edges), tuple(units),...]
where the time goes in v12:
time: 135 us
  Pallas kernels  134 us (99%)
    pallas_call x1, Pallas kernels, run_step(): pl.pallas_call(functools.partial(step_kernel, tuple(edges), tuple(units),...  129 us
    pallas_call x1, Pallas kernels, finish(): pl.pallas_call(functools.partial(finish_kernel, count, chunks), out_shape...  4.65 us

profile of v12, /device:TPU:0, one launch (start us, length us, event | category | flops | bytes accessed | tf_op | source)
XLA Modules:
  0.0 134.5 jit_solution(12891130623085689001)
XLA Ops:
  0.6 129.0 %step.1 = (f32[898,128]{1,0:T(8,128)S(1)}, f32[898,128]{1,0:T(8,128)S(1)}, bf16[28736,128]{1,0:T(8,128)(2,1)S(1)}, f32[1,7680]{1,0:T(1,128)S(1)}, f32[1,1546]{1,...) custom-call(bf16[4096,256]{1,0:T(8,128)(2,1)} %bitcast.9, f32[2304,512]{1,0:T(8,128)} %one_hbm.1, ...), custom_call_target="tpu_custom_call" | custom-call | tf_op jit(solution)/shard_map/step/pallas_call | solution.py:1268
  129.7 4.7 %finish.1 = (bf16[28736,128]{1,0:T(8,128)(2,1)}, f32[898,128]{1,0:T(8,128)}, f32[898,128]{1,0:T(8,128)}, f32[1,7680]{1,0:T(1,128)}, f32[1,1546]{1,0:T(1,128)}, /...) custom-call(bf16[28736,128]{1,0:T(8,128)(2,1)S(1)} %get-tuple-element.24.refs_0_, ...), custom_call_target="tpu_custom_call" | custom-call | tf_op jit(solution)/shard_map/finish/pallas_call | solution.py:1241

commit v13 on v12

--- a/solution.py
+++ b/solution.py
@@ -118,39 +118,41 @@
 
 SCHEDULE = (
     (),
+    (),
     (
-        (1, 0),
+        (1, 0), (0, 2),
     ),
     (
-        (0, 2), (1, 1),
+        (1, 1), (0, 3),
     ),
     (
-        (0, 3), (1, 2), (2, 0), (0, 4), (1, 3), (2, 1),
+        (1, 2), (0, 4),
     ),
     (
-        (0, 5), (1, 4), (2, 2), (3, 0),
-    ),
-    (
-        (0, 6), (1, 5), (2, 3), (3, 1),
-    ),
-    (
-        (0, 7), (1, 6), (2, 4), (3, 2), (4, 0),
+        (2, 0), (1, 3), (0, 5),
     ),
     (),
     (
-        (0, 8), (1, 7), (2, 5), (3, 3), (4, 1),
+        (2, 1), (1, 4), (0, 6),
+    ),
+    (
+        (3, 0), (2, 2), (1, 5), (0, 7),
     ),
     (),
     (
-        (1, 8), (2, 6), (3, 4), (4, 2), (1, 9), (2, 7), (3, 5), (4, 3), (5, 0), (0, 11), (1, 10),
-        (2, 8), (3, 6), (4, 4), (5, 1), (0, 12), (1, 11), (2, 9), (3, 7), (4, 5), (5, 2), (6, 0),
-        (0, 13), (1, 12), (2, 10), (3, 8), (4, 6), (5, 3), (6, 1), (1, 13), (2, 11), (3, 9),
-        (4, 7), (8, 0), (5, 4), (6, 2), (2, 12), (3, 10), (4, 8), (5, 5), (6, 3), (7, 0),
-        (2, 13), (3, 11), (4, 9), (5, 6), (6, 4), (7, 1), (3, 12), (4, 10), (5, 7), (6, 5),
-        (7, 2), (3, 13), (4, 11), (5, 8), (6, 6), (7, 3), (4, 12), (5, 9), (6, 7), (7, 4),
-        (4, 13), (5, 10), (6, 8), (7, 5), (5, 11), (6, 9), (7, 6), (5, 12), (6, 10), (7, 7),
-        (5, 13), (6, 11), (7, 8), (6, 12), (7, 9), (9, 0), (6, 13), (7, 10), (7, 11), (7, 12),
-        (9, 1), (7, 13), (9, 2),
+        (3, 1), (2, 3), (1, 6), (0, 8),
+    ),
+    (
+        (3, 2), (2, 4), (1, 7), (4, 0), (3, 3), (2, 5), (1, 8), (4, 1), (3, 4), (2, 6), (1, 9),
+        (0, 11), (4, 2), (3, 5), (2, 7), (1, 10), (0, 12), (5, 0), (4, 3), (3, 6), (2, 8),
+        (1, 11), (0, 13), (5, 1), (4, 4), (3, 7), (2, 9), (1, 12), (6, 0), (5, 2), (4, 5),
+        (3, 8), (2, 10), (1, 13), (6, 1), (5, 3), (4, 6), (3, 9), (2, 11), (6, 2), (5, 4),
+        (4, 7), (8, 0), (3, 10), (2, 12), (7, 0), (6, 3), (5, 5), (4, 8), (3, 11), (2, 13),
+        (7, 1), (6, 4), (5, 6), (4, 9), (3, 12), (7, 2), (6, 5), (5, 7), (4, 10), (3, 13),
+        (7, 3), (6, 6), (5, 8), (4, 11), (7, 4), (6, 7), (5, 9), (4, 12), (7, 5), (6, 8),
+        (5, 10), (4, 13), (7, 6), (6, 9), (5, 11), (7, 7), (6, 10), (5, 12), (7, 8), (6, 11),
+        (5, 13), (7, 9), (9, 0), (6, 12), (7, 10), (6, 13), (7, 11), (7, 12), (9, 1), (7, 13),
+        (9, 2),
     ),
 )
 
@@ -404,6 +406,7 @@
     side = 4
     band = side * slots
     pixel_count = side * side
+    side_pixels = 4 * pixel_count
     classes = head_ref.shape[0]
     keep = 1.0 - STEP ** (-0.8)
     low = jnp.bfloat16
@@ -469,10 +472,21 @@
     for half in range(2):
         lanes = slice(128 * half, 128 * (half + 1))
         loads[half].wait()
-        level[:count, :] = core_in[pl.ds(half * count, count), :].astype(f32)
+        apart = side_pixels + 8
+
+        @pl.loop(0, slots // 4)
+        def _(k):
+            for m in range(4):
+                slot = k * 4 + m
+                source = pl.multiple_of(half * count + slot * side_pixels, side_pixels)
+                target = pl.multiple_of(slot * apart, 8)
+                level[pl.ds(target, side_pixels), :] = core_in[
+                    pl.ds(source, side_pixels), :
+                ].astype(f32)
+
         for h in range(2 * side):
             for w in range(2 * side):
-                rows = level[pl.ds(2 * side * h + w, slots, stride=4 * pixel_count), :]
+                rows = level[pl.ds(2 * side * h + w, slots, stride=apart), :]
                 xs[w % 2, w // 2, h % 2, h // 2, :, lanes] = rows.astype(low)
 
     scales = {}
@@ -731,19 +745,21 @@
             [line_in[pl.ds(4 * starts[u] + t * size, size), :].astype(f32) for t in range(4)],
         ).astype(low)
         sum_low[here, :] = low_sum
-        total[here, :] = low_sum.astype(f32)
+        summed = low_sum.astype(f32)
         target = own_weight.at[pl.ds(starts[u] // 4, 16 * units[u][1])]
         pltpu.make_async_copy(target, target, fetch_sem.at[9 + u]).wait()
         matrices = units[u][4]
-        scale = jnp.where(core == 0, scales[matrices[0]], scales[matrices[1]])
+        scale = scales[matrices[0]]
+        if matrices[0] != matrices[1]:
+            scale = jnp.where(core == 0, scale, scales[matrices[1]])
+        turned = jnp.tanh(summed * root) * scale
         for m in range(units[u][1]):
             row = starts[u] // 4 + 16 * m
             for part in (0, 8):
                 for q in range(4):
-                    summed = total[pl.ds(row * 4 + 16 * q + part, 8), :]
+                    at = GROUP * m + 16 * q + part
                     old = own_weight[pl.ds(row + part, 8), 128 * q : 128 * (q + 1)]
-                    fresh = old - scale * jnp.tanh(summed * root)
-                    flat_rows(row + part, q, fresh, new_flat)
+                    flat_rows(row + part, q, old - turned[at : at + 8], new_flat)
         out_ref[lines(own_group(u) * GROUP, size), :] = new_flat[here, :].astype(low)
         for k in (3, 2, 1):
             spread_copy(u, k).start()
@@ -1112,8 +1128,6 @@
     early = edges[1] // 512 - edges[0] // 512
     matrix_votes(1, grad_two, (nothing, nothing), lambda k: go(0, k) if k < 2 else None)
     turn(0)
-    grad_short[...] = jnp.dot(xs_t[0, 0], back_side[...], preferred_element_type=f32)
-    matrix_votes(2, grad_short, (nothing, nothing), lambda k: None)
 
     gain_one, shift_one = none, none
     for j in range(side):
@@ -1140,6 +1154,10 @@
         )
         back_one[j, :side] = (grad * slope_one).astype(low).reshape(side, slots, width)
         turn(1 + j)
+
+    grad_short[...] = jnp.dot(xs_t[0, 0], back_side[...], preferred_element_type=f32)
+    matrix_votes(2, grad_short, (nothing, nothing), lambda k: None)
+    turn(5)
 
     square_head = grad_head * grad_head + EPS_ROW
     real = lax.broadcasted_iota(jnp.int32, square_head.shape, 0) < classes
@@ -1194,15 +1212,15 @@
             )
         if b == 1:
             kept["tail"] = exchange_middle(2, kept["tail"])
-        turn(5 + b)
+        turn(6 + b)
 
     matrix_votes(
         0,
         grad_one,
-        (lambda: turn(8), lambda: turn(9)),
+        (lambda: turn(9), lambda: turn(10)),
         lambda k: go(0, early + k) if k < 2 else None,
     )
-    turn(10)
+    turn(11)
     for away, copy in passes:
 
         @pl.when(away)

time: 135 us -> 131 us (0.970)
  Pallas kernels: 134 us -> 130 us
    pallas_call x1, Pallas kernels: 129 us -> 125 us  [run_step(): pl.pallas_call(functools.partial(step_kernel, tuple(edges), tuple(units),...]
where the time goes in v13:
time: 131 us
  Pallas kernels  130 us (99%)
    pallas_call x1, Pallas kernels, run_step(): pl.pallas_call(functools.partial(step_kernel, tuple(edges), tuple(units),...  125 us
    pallas_call x1, Pallas kernels, finish(): pl.pallas_call(functools.partial(finish_kernel, count, chunks), out_shape...  4.65 us

profile of v13, /device:TPU:0, one launch (start us, length us, event | category | flops | bytes accessed | tf_op | source)
XLA Modules:
  0.0 130.8 jit_solution(9084725292542869961)
XLA Ops:
  0.6 125.3 %step.1 = (f32[898,128]{1,0:T(8,128)S(1)}, f32[898,128]{1,0:T(8,128)S(1)}, bf16[28736,128]{1,0:T(8,128)(2,1)S(1)}, f32[1,7680]{1,0:T(1,128)S(1)}, f32[1,1546]{1,...) custom-call(bf16[4096,256]{1,0:T(8,128)(2,1)} %bitcast.9, f32[2304,512]{1,0:T(8,128)} %one_hbm.1, ...), custom_call_target="tpu_custom_call" | custom-call | tf_op jit(solution)/shard_map/step/pallas_call | solution.py:1286
  126.0 4.7 %finish.1 = (bf16[28736,128]{1,0:T(8,128)(2,1)}, f32[898,128]{1,0:T(8,128)}, f32[898,128]{1,0:T(8,128)}, f32[1,7680]{1,0:T(1,128)}, f32[1,1546]{1,0:T(1,128)}, /...) custom-call(bf16[28736,128]{1,0:T(8,128)(2,1)S(1)} %get-tuple-element.24.refs_0_, ...), custom_call_target="tpu_custom_call" | custom-call | tf_op jit(solution)/shard_map/finish/pallas_call | solution.py:1259

commit v14 on v13

--- a/solution.py
+++ b/solution.py
@@ -243,42 +243,58 @@
             square_ref[...] += fold(values * values)
 
 
-def factored_votes(grad, rows, row_at, rows_old, rows_new, col_old, level, votes, vote_at, between, after):
+def row_block(grad, row_at, rows_old, rows_new, level, k, carry):
     width = grad.shape[1]
     keep = 1.0 - STEP ** (-0.8)
     step = 128
     quarters = width // 128
-
-    def first(k, carry):
-        col_sum, row_sum = carry
-        start = pl.multiple_of(k * step, step)
+    col_sum, row_sum = carry
+    start = k * step
+    lanes = pl.ds(row_at + start, step)
+    if not isinstance(k, int):
+        start = pl.multiple_of(start, step)
         lanes = pl.ds(pl.multiple_of(row_at + start, step), step)
-        old = rows_old[:, lanes] * keep
-        line = jnp.zeros((8, 128), jnp.float32)
-        for m in range(step // 8):
-            block = grad[pl.ds(start + 8 * m, 8), :]
-            square = block * block
-            col_sum = col_sum + square
-            part = square[:, :128]
-            for q in range(1, quarters):
-                part = part + square[:, 128 * q : 128 * (q + 1)]
-            part = part * ((1.0 - keep) / width)
-            diagonal = eye_mask(8, 128, 8 * m)
-            part = part + jnp.where(diagonal, jnp.broadcast_to(old, (8, 128)), 0.0)
-            row = jnp.sum(part, axis=1, keepdims=True) + (1.0 - keep) * EPS_ROW
-            row = jnp.broadcast_to(row, (8, 128))
-            level[pl.ds(start + 8 * m, 8), :] = row
-            row_sum = row_sum + row
-            line = line + jnp.where(diagonal, row, 0.0)
-        rows_new[:, lanes] = jnp.sum(line, axis=0, keepdims=True)
-        return col_sum, row_sum
-
-    col_sum, row_sum = lax.fori_loop(
-        0,
-        rows // step,
-        first,
-        (jnp.zeros((8, width), jnp.float32), jnp.zeros((8, 128), jnp.float32)),
-    )
+    old = rows_old[:, lanes] * keep
+    line = jnp.zeros((8, 128), jnp.float32)
+    for m in range(step // 8):
+        block = grad[pl.ds(start + 8 * m, 8), :]
+        square = block * block
+        col_sum = col_sum + square
+        part = square[:, :128]
+        for q in range(1, quarters):
+            part = part + square[:, 128 * q : 128 * (q + 1)]
+        part = part * ((1.0 - keep) / width)
+        diagonal = eye_mask(8, 128, 8 * m)
+        part = part + jnp.where(diagonal, jnp.broadcast_to(old, (8, 128)), 0.0)
+        row = jnp.sum(part, axis=1, keepdims=True) + (1.0 - keep) * EPS_ROW
+        row = jnp.broadcast_to(row, (8, 128))
+        level[pl.ds(start + 8 * m, 8), :] = row
+        row_sum = row_sum + row
+        line = line + jnp.where(diagonal, row, 0.0)
+    rows_new[:, lanes] = jnp.sum(line, axis=0, keepdims=True)
+    return col_sum, row_sum
+
+
+def no_sums(width):
+    return jnp.zeros((8, width), jnp.float32), jnp.zeros((8, 128), jnp.float32)
+
+
+def factored_votes(
+    grad, rows, row_at, rows_old, rows_new, col_old, level, votes, vote_at, between, after, sums
+):
+    width = grad.shape[1]
+    keep = 1.0 - STEP ** (-0.8)
+    step = 128
+    quarters = width // 128
+    if sums is None:
+        sums = lax.fori_loop(
+            0,
+            rows // step,
+            functools.partial(row_block, grad, row_at, rows_old, rows_new, level),
+            no_sums(width),
+        )
+    col_sum, row_sum = sums
+
     col_new = keep * col_old + (1.0 - keep) * (
         jnp.sum(col_sum, axis=0, keepdims=True) / rows + EPS_ROW
     )
@@ -291,12 +307,12 @@
             here = pl.ds(start + 8 * m, 8)
             factor = lax.rsqrt(level[here, :]) * root_mean
             level[here, :] = factor
-            raw = grad[here, :] * scale
+            raw = grad[here, :] * jnp.concatenate([factor] * quarters, axis=1) * scale
             power = raw * raw
             part = power[:, :128]
             for q in range(1, quarters):
                 part = part + power[:, 128 * q : 128 * (q + 1)]
-            carry = carry + part * (factor * factor)
+            carry = carry + part
         return carry
 
     between[0]()
@@ -811,11 +827,6 @@
     scales[2] = scale_from(square[...], grad_short.size)
     for fetch in fetch_two:
         fetch.start()
-    for k in range(OWN // PIECE):
-        fetch_rows(first_row + k * PIECE, PIECE, k * PIECE, fetch_sem.at[7])
-    fetch_rows(first_row + OWN, TAIL, OWN, fetch_sem.at[8])
-    for u in range(len(units)):
-        own_fetch(u)
 
     def image_taps(j):
         pieces = []
@@ -912,6 +923,11 @@
         main_two[pl.ds(j * band, band), :] = value
         two_sums = add_up(two_sums, moments(value))
     copies = exchange_start(1, pack_rows(two_sums))
+    for k in range(OWN // PIECE):
+        fetch_rows(first_row + k * PIECE, PIECE, k * PIECE, fetch_sem.at[7])
+    fetch_rows(first_row + OWN, TAIL, OWN, fetch_sem.at[8])
+    for u in range(len(units)):
+        own_fetch(u)
     for j in range(side):
         block = active[j, 1 : side + 1].reshape(band, width)
         active_t[:, j * band : (j + 1) * band] = block.T
@@ -985,19 +1001,25 @@
         join_sums.append([jnp.sum(each, axis=0, keepdims=True) for each in three])
     gain_two, gain_side, shift_two = [jnp.concatenate(each, axis=1) for each in zip(*join_sums)]
 
+    two_passed = no_sums(width)
     for b in range(3):
         first, last = max(0, b - 1), min(side, side + b - 1)
         left = active_t[:, first * band : last * band]
         for a in range(3):
             right = back_two[first - b + 1 : last - b + 1, 2 - a : 2 - a + side]
-            grad_two[pl.ds((a * 3 + b) * width, width), :] = jnp.dot(
+            tap = a * 3 + b
+            grad_two[pl.ds(tap * width, width), :] = jnp.dot(
                 left, right.reshape(-1, width), preferred_element_type=f32
             )
+            for k in range(tap * width // 128, (tap + 1) * width // 128):
+                two_passed = row_block(
+                    grad_two, edges[0], row_ref, row_new, level, k, two_passed
+                )
 
     def nothing():
         pass
 
-    def matrix_votes(k, grad, between, after):
+    def matrix_votes(k, grad, between, after, sums=None):
         here = pl.ds(k * width, width)
         start = edges[k - 1] if k else 0
         col_new[:, here] = factored_votes(
@@ -1012,6 +1034,7 @@
             start,
             between,
             after,
+            sums,
         )
 
     kept = {}
@@ -1126,7 +1149,7 @@
             go(step_number, u)
 
     early = edges[1] // 512 - edges[0] // 512
-    matrix_votes(1, grad_two, (nothing, nothing), lambda k: go(0, k) if k < 2 else None)
+    matrix_votes(1, grad_two, (nothing, nothing), lambda k: go(0, k) if k < 2 else None, two_passed)
     turn(0)
 
     gain_one, shift_one = none, none

time: 131 us -> 127 us (0.969)
  Pallas kernels: 130 us -> 126 us
    pallas_call x1, Pallas kernels: 125 us -> 122 us  [run_step(): pl.pallas_call(functools.partial(step_kernel, tuple(edges), tuple(units),...]
where the time goes in v14:
time: 127 us
  Pallas kernels  126 us (99%)
    pallas_call x1, Pallas kernels, run_step(): pl.pallas_call(functools.partial(step_kernel, tuple(edges), tuple(units),...  122 us
    pallas_call x1, Pallas kernels, finish(): pl.pallas_call(functools.partial(finish_kernel, count, chunks), out_shape...  4.65 us

profile of v14, /device:TPU:0, one launch (start us, length us, event | category | flops | bytes accessed | tf_op | source)
XLA Modules:
  0.0 127.0 jit_solution(13571223552470915793)
XLA Ops:
  0.6 121.5 %step.1 = (f32[898,128]{1,0:T(8,128)S(1)}, f32[898,128]{1,0:T(8,128)S(1)}, bf16[28736,128]{1,0:T(8,128)(2,1)S(1)}, f32[1,7680]{1,0:T(1,128)S(1)}, f32[1,1546]{1,...) custom-call(bf16[4096,256]{1,0:T(8,128)(2,1)} %bitcast.9, f32[2304,512]{1,0:T(8,128)} %one_hbm.1, ...), custom_call_target="tpu_custom_call" | custom-call | tf_op jit(solution)/shard_map/step/pallas_call | solution.py:1309
  122.2 4.7 %finish.1 = (bf16[28736,128]{1,0:T(8,128)(2,1)}, f32[898,128]{1,0:T(8,128)}, f32[898,128]{1,0:T(8,128)}, f32[1,7680]{1,0:T(1,128)}, f32[1,1546]{1,0:T(1,128)}, /...) custom-call(bf16[28736,128]{1,0:T(8,128)(2,1)S(1)} %get-tuple-element.24.refs_0_, ...), custom_call_target="tpu_custom_call" | custom-call | tf_op jit(solution)/shard_map/finish/pallas_call | solution.py:1282

commit v15 on v14

--- a/solution.py
+++ b/solution.py
@@ -228,16 +228,14 @@
 
 
 def cast_weight(source, target, square_ref, taps, depth, fetches):
-    step = 128
+    step = 256
     for tap in taps:
         chunk = source.shape[0] // depth // len(fetches)
         if tap % chunk == 0:
             fetches[tap // chunk].wait()
         new_tap = (tap % 3) * 3 + tap // 3
 
-        @pl.loop(0, depth // step)
-        def _(k):
-            start = pl.multiple_of(k * step, step)
+        for start in range(0, depth, step):
             values = source[pl.ds(tap * depth + start, step), :]
             target[new_tap, pl.ds(start, step), :] = values.astype(jnp.bfloat16)
             square_ref[...] += fold(values * values)
@@ -301,9 +299,11 @@
     scale = lax.rsqrt(col_new)
     root_mean = jnp.sqrt(jnp.sum(row_sum, axis=0, keepdims=True) / rows)
 
+    run = 2 * step
+
     def second(k, carry):
-        start = pl.multiple_of(k * step, step)
-        for m in range(step // 8):
+        start = pl.multiple_of(k * run, run)
+        for m in range(run // 8):
             here = pl.ds(start + 8 * m, 8)
             factor = lax.rsqrt(level[here, :]) * root_mean
             level[here, :] = factor
@@ -316,27 +316,24 @@
         return carry
 
     between[0]()
-    power = lax.fori_loop(0, rows // step, second, jnp.zeros((8, 128), jnp.float32))
+    power = lax.fori_loop(0, rows // run, second, jnp.zeros((8, 128), jnp.float32))
     between[1]()
     clip = jnp.maximum(1.0, jnp.sqrt(total_of(power) / (rows * width)))
     scale = scale / clip
 
-    def third(k, _):
-        start = pl.multiple_of(k * step, step)
-        for m in range(step // 16):
+    def third(start, count):
+        for m in range(count // 16):
             here = pl.ds(start + 16 * m, 16)
             factor = level[here, :]
             factor = jnp.concatenate([factor] * quarters, axis=1)
             vote = jnp.tanh(grad[here, :] * factor * scale).astype(jnp.bfloat16)
-            at = pl.multiple_of((vote_at + start) * 4 + GROUP * m, GROUP)
+            at = (vote_at + start) * 4 + GROUP * m
             for q in range(quarters):
                 votes[pl.ds(at + 16 * q, 16), :] = vote[:, 128 * q : 128 * (q + 1)]
-        return 0
-
-    part = 512 // step
-    for k in range(0, rows // step, part):
-        lax.fori_loop(k, min(k + part, rows // step), third, 0)
-        after(k // part)
+
+    for k, start in enumerate(range(0, rows, 512)):
+        third(start, min(512, rows - start))
+        after(k)
     return col_new
 
 
@@ -1223,6 +1220,7 @@
     )
 
 
+    one_passed = no_sums(width)
     for b in range(3):
         first, last = (0, side - 1) if b == 0 else (0, side)
         shift = 1 if b == 0 else 0
@@ -1230,9 +1228,12 @@
             left = xs_t[0 if b == 1 else 1, 0 if a == 1 else 1, :, first * band : last * band]
             start = 1 if a == 0 else 0
             right = back_one[first + shift : last + shift, start : start + side]
-            grad_one[pl.ds((a * 3 + b) * in_width, in_width), :] = jnp.dot(
+            tap = a * 3 + b
+            grad_one[pl.ds(tap * in_width, in_width), :] = jnp.dot(
                 left, right.reshape(-1, width), preferred_element_type=f32
             )
+            for k in range(tap * in_width // 128, (tap + 1) * in_width // 128):
+                one_passed = row_block(grad_one, 0, row_ref, row_new, level, k, one_passed)
         if b == 1:
             kept["tail"] = exchange_middle(2, kept["tail"])
         turn(6 + b)
@@ -1242,6 +1243,7 @@
         grad_one,
         (lambda: turn(9), lambda: turn(10)),
         lambda k: go(0, early + k) if k < 2 else None,
+        one_passed,
     )
     turn(11)
     for away, copy in passes:

time: 127 us -> 126 us (level)
  no operation moved by 1% of the time
where the time goes in v15:
time: 126 us
  Pallas kernels  125 us (99%)
    pallas_call x1, Pallas kernels, run_step(): pl.pallas_call(functools.partial(step_kernel, tuple(edges), tuple(units),...  121 us
    pallas_call x1, Pallas kernels, finish(): pl.pallas_call(functools.partial(finish_kernel, count, chunks), out_shape...  4.65 us

profile of v15, /device:TPU:0, one launch (start us, length us, event | category | flops | bytes accessed | tf_op | source)
XLA Modules:
  0.0 126.0 jit_solution(18277557284598682823)
XLA Ops:
  0.6 120.5 %step.1 = (f32[898,128]{1,0:T(8,128)S(1)}, f32[898,128]{1,0:T(8,128)S(1)}, bf16[28736,128]{1,0:T(8,128)(2,1)S(1)}, f32[1,7680]{1,0:T(1,128)S(1)}, f32[1,1546]{1,...) custom-call(bf16[4096,256]{1,0:T(8,128)(2,1)} %bitcast.9, f32[2304,512]{1,0:T(8,128)} %one_hbm.1, ...), custom_call_target="tpu_custom_call" | custom-call | tf_op jit(solution)/shard_map/step/pallas_call | solution.py:1311
  121.2 4.7 %finish.1 = (bf16[28736,128]{1,0:T(8,128)(2,1)}, f32[898,128]{1,0:T(8,128)}, f32[898,128]{1,0:T(8,128)}, f32[1,7680]{1,0:T(1,128)}, f32[1,1546]{1,0:T(1,128)}, /...) custom-call(bf16[28736,128]{1,0:T(8,128)(2,1)S(1)} %get-tuple-element.24.refs_0_, ...), custom_call_target="tpu_custom_call" | custom-call | tf_op jit(solution)/shard_map/finish/pallas_call | solution.py:1284

commit v16 on v15

--- a/solution.py
+++ b/solution.py
@@ -1340,7 +1340,7 @@
             pltpu.VMEM((width, pixels), low),
             pltpu.VMEM((2, 2, in_width, pixels), low),
             pltpu.VMEM((128, width), f32),
-            pltpu.VMEM((conv_two.shape[0], 128), f32),
+            pltpu.VMEM((conv_two.shape[0] + 72, 128), f32),
             pltpu.VMEM((8, width), f32),
             pltpu.VMEM((24, 128), f32),
             pltpu.VMEM((8, 24, 128), f32),
@@ -1360,8 +1360,8 @@
             pltpu.VMEM((SPAN + GROUP, 128), f32),
             pltpu.VMEM((OWN, width), f32),
             pltpu.VMEM((OWN + TAIL, width), f32),
-            pltpu.VMEM((SPAN + GROUP, 128), f32),
-            pltpu.VMEM((SPAN + GROUP, 128), f32),
+            pltpu.VMEM((SPAN + GROUP + 32, 128), f32),
+            pltpu.VMEM((SPAN + GROUP + 32, 128), f32),
             pltpu.VMEM((GROUP, 128), f32),
             pltpu.VMEM((GROUP, 128), f32),
             dma((9 + len(units),)),

time: 126 us -> 126 us (level)
  no operation moved by 1% of the time
where the time goes in v16:
time: 126 us
  Pallas kernels  125 us (99%)
    pallas_call x1, Pallas kernels, run_step(): pl.pallas_call(functools.partial(step_kernel, tuple(edges), tuple(units),...  121 us
    pallas_call x1, Pallas kernels, finish(): pl.pallas_call(functools.partial(finish_kernel, count, chunks), out_shape...  4.65 us

profile of v16, /device:TPU:0, one launch (start us, length us, event | category | flops | bytes accessed | tf_op | source)
XLA Modules:
  0.0 126.1 jit_solution(17962310250476910279)
XLA Ops:
  0.6 120.6 %step.1 = (f32[898,128]{1,0:T(8,128)S(1)}, f32[898,128]{1,0:T(8,128)S(1)}, bf16[28736,128]{1,0:T(8,128)(2,1)S(1)}, f32[1,7680]{1,0:T(1,128)S(1)}, f32[1,1546]{1,...) custom-call(bf16[4096,256]{1,0:T(8,128)(2,1)} %bitcast.9, f32[2304,512]{1,0:T(8,128)} %one_hbm.1, ...), custom_call_target="tpu_custom_call" | custom-call | tf_op jit(solution)/shard_map/step/pallas_call | solution.py:1311
  121.2 4.7 %finish.1 = (bf16[28736,128]{1,0:T(8,128)(2,1)}, f32[898,128]{1,0:T(8,128)}, f32[898,128]{1,0:T(8,128)}, f32[1,7680]{1,0:T(1,128)}, f32[1,1546]{1,0:T(1,128)}, /...) custom-call(bf16[28736,128]{1,0:T(8,128)(2,1)S(1)} %get-tuple-element.24.refs_0_, ...), custom_call_target="tpu_custom_call" | custom-call | tf_op jit(solution)/shard_map/finish/pallas_call | solution.py:1284
